TPU v7x, 32 devices: a whole 2x2x4 slice. The times are simulated.
32 devices in a mesh: dp: 8 (over z, y), tensor: 4 (over x, core).
Axes of the slice: x: 2, y: 2, z: 4, core: 2. Of those that a mesh axis runs over, the one named last changes fastest.
Arguments:
- hidden_in: float32 [8192, 1536], P(('dp', 'tensor')), may hold values from -6 to 6
- norm_gain: float32 [1536], replicated, may hold values from 0.5 to 1.5
- gate_value_weight: bfloat16 [1536, 2, 3072], P('dp', None, 'tensor'), may hold values from -0.15625 to 0.15625
- state_proj_weight: bfloat16 [1536, 256], P('dp'), may hold values from -0.15625 to 0.15625
- step_weight: bfloat16 [1536, 48], P('dp', 'tensor'), may hold values from -0.15625 to 0.15625
- conv_value_kernel: float32 [3072, 4], P('tensor'), may hold values from -3 to 3
- conv_value_bias: float32 [3072], P('tensor'), may hold values from -3 to 3
- conv_state_kernel: float32 [256, 4], replicated, may hold values from -3 to 3
- conv_state_bias: float32 [256], replicated, may hold values from -3 to 3
- step_bias: float32 [48], P('tensor'), may hold values from -6 to -1
- decay_log: float32 [48], P('tensor'), may hold values from -3 to 2
- skip_scale: float32 [48], P('tensor'), may hold values from 0.5 to 1.5
- gate_norm_gain: float32 [3072], P('tensor'), may hold values from 0.5 to 1.5
- out_weight: bfloat16 [1536, 3072], P('dp', 'tensor'), may hold values from -0.109375 to 0.109375
- out_cotangent: float32 [8192, 1536], P(('dp', 'tensor')), may hold values from -6 to 6
- seq_lengths: int32 [32], replicated, may hold values from 0 to 1024, as said below
- seq_device: int32 [32], replicated, may hold values from 0 to 7, as said below
- seq_offset: int32 [32], replicated, may hold values from 0 to 3, as said below
Outputs:
- output: float32 [8192, 1536], P(('dp', 'tensor'))
- hidden_gradient: float32 [8192, 1536], P(('dp', 'tensor'))
- norm_gain_gradient: float32 [1536], P(('dp', 'tensor'))
- gate_value_weight_gradient: float32 [1536, 2, 3072], P('dp', None, 'tensor')
- state_proj_weight_gradient: float32 [1536, 256], P(('dp', 'tensor'))
- step_weight_gradient: float32 [1536, 48], P('dp', 'tensor')
- conv_value_kernel_gradient: float32 [3072, 4], P('tensor')
- conv_value_bias_gradient: float32 [3072], P('tensor')
- conv_state_kernel_gradient: float32 [256, 4], P(('dp', 'tensor'))
- conv_state_bias_gradient: float32 [256], P(('dp', 'tensor'))
- step_bias_gradient: float32 [48], P('tensor')
- decay_log_gradient: float32 [48], P('tensor')
- skip_scale_gradient: float32 [48], P('tensor')
- gate_norm_gain_gradient: float32 [3072], P('tensor')
- out_weight_gradient: float32 [1536, 3072], P('dp', 'tensor')
Inputs may be any that keep to these rules, and one draw needn't show every extreme that they name: A slot with seq_lengths > 0 is a sequence that occupies spans seq_offset to seq_offset + ceil(seq_lengths / 256) - 1 of the 4 spans of dp index seq_device; sequences of one dp index never share a span; a slot of length 0 occupies nothing. Some sequence has length 1024, and some slot is empty. `seq_device`: each dp index is named by 4 slots. `seq_offset`: some sequence begins at the last span of its dp index.
All inputs are finite; a program needn't handle non-finite values.
Results may differ from a plain program's by a relative error of at most 0.011.
Values may be sent and summed in bfloat16 or wider, within the bound.
No kernel may reach another device: no remote copies, remote signals or barrier semaphores. Data moves between devices by JAX's collectives and lax.ppermute only.
A program may use at most 192 MiB of HBM per device.

v0:
```python
from functools import partial

import jax
import jax.numpy as jnp
from jax import lax
from jax.sharding import PartitionSpec as P

D = 1536
KCONV = 4
SPAN = 256
E = 3072
TOK_DEV = 1024
SEQ_DEV = 4


EPSILON = 1e-05
HIGHEST = lax.Precision.HIGHEST


def contract(left, right, left_dim, right_dim):
    return lax.dot_general(
        left, right, (((left_dim,), (right_dim,)), ((), ())), preferred_element_type=jnp.float32
    )


def span_layout(seq_lengths, seq_device, seq_offset, device):
    span_index = jnp.arange(SEQ_DEV, dtype=jnp.int32)
    needed = (seq_lengths + SPAN - 1) // SPAN
    owned_seq = (seq_device == device) & (seq_lengths > 0)
    relative = span_index[None, :] - seq_offset[:, None]
    inside = owned_seq[:, None] & (relative >= 0) & (relative < needed[:, None])
    live_rows = jnp.sum(
        jnp.where(inside, jnp.clip(seq_lengths[:, None] - relative * SPAN, 0, SPAN), 0), axis=0
    )
    seq_first = jnp.any(inside & (relative == 0), axis=0)
    position = jnp.arange(TOK_DEV, dtype=jnp.int32) % SPAN
    row_mask = jnp.where(position < jnp.repeat(live_rows, SPAN), 1.0, 0.0).astype(jnp.float32)
    first_rows = jnp.repeat(seq_first, SPAN)
    keep_mask = jnp.stack(
        [jnp.logical_not(first_rows & (position < shift_by)) for shift_by in range(KCONV)]
    )
    return (row_mask, seq_first, keep_mask)


def causal_conv(values, kernel, offset_bias, keep_mask):
    row_count = values.shape[0]
    tap_count = kernel.shape[1]
    result = offset_bias[None, :] + kernel[:, tap_count - 1][None, :] * values
    for shift_by in range(1, tap_count):
        shifted = jnp.concatenate(
            [jnp.zeros((shift_by, values.shape[1]), values.dtype), values[: row_count - shift_by]],
            axis=0,
        )
        shifted = jnp.where(keep_mask[shift_by][:, None], shifted, 0.0)
        result = result + kernel[:, tap_count - 1 - shift_by][None, :] * shifted
    return result


def ssd_scan(values, b_state, c_state, step, decay_log, skip_scale, seq_first):
    row_count, head_count = step.shape
    head_width = values.shape[1] // head_count
    state_width = b_state.shape[1]
    span_count = row_count // SPAN
    log_decay = step * (-jnp.exp(decay_log))[None, :]
    lower_mask = jnp.arange(SPAN)[:, None] >= jnp.arange(SPAN)[None, :]
    scanned = (
        values.reshape(span_count, SPAN, head_count, head_width),
        b_state.reshape(span_count, SPAN, state_width),
        c_state.reshape(span_count, SPAN, state_width),
        step.reshape(span_count, SPAN, head_count),
        log_decay.reshape(span_count, SPAN, head_count),
        seq_first,
    )

    def span_step(carried, block_data):
        value_blk, b_blk, c_blk, step_blk, decay_blk, starts = block_data
        carried = jnp.where(starts, jnp.zeros_like(carried), carried)
        cum_decay = jnp.cumsum(decay_blk, axis=0)
        scores_bc = jnp.dot(c_blk, b_blk.T, precision=HIGHEST)
        gap_log = jnp.where(
            lower_mask[:, :, None], cum_decay[:, None, :] - cum_decay[None, :, :], 0.0
        )
        weights = (
            jnp.where(lower_mask[:, :, None], jnp.exp(gap_log), 0.0)
            * scores_bc[:, :, None]
            * step_blk[None, :, :]
        )
        diag_part = jnp.einsum("tsh,shp->thp", weights, value_blk, precision=HIGHEST)
        carry_part = (
            jnp.einsum("tn,hnp->thp", c_blk, carried, precision=HIGHEST)
            * jnp.exp(cum_decay)[:, :, None]
        )
        tail_weight = jnp.exp(cum_decay[-1][None, :] - cum_decay) * step_blk
        updated = jnp.exp(cum_decay[-1])[:, None, None] * carried + jnp.einsum(
            "sn,shp->hnp", b_blk, value_blk * tail_weight[:, :, None], precision=HIGHEST
        )
        result = diag_part + carry_part + skip_scale[None, :, None] * value_blk
        return (updated, result)

    zero_state = jnp.zeros((head_count, state_width, head_width), jnp.float32)
    _, outputs = lax.scan(jax.checkpoint(span_step), zero_state, scanned)
    return outputs.reshape(row_count, head_count * head_width)


def mixer_core(
    seq_first,
    keep_mask,
    gate_raw,
    value_raw,
    bc_raw,
    step_raw,
    conv_value_kernel,
    conv_value_bias,
    conv_state_kernel,
    conv_state_bias,
    step_bias,
    decay_log,
    skip_scale,
):
    values = jax.nn.silu(causal_conv(value_raw, conv_value_kernel, conv_value_bias, keep_mask))
    bc_conv = jax.nn.silu(causal_conv(bc_raw, conv_state_kernel, conv_state_bias, keep_mask))
    state_width = bc_raw.shape[1] // 2
    step = jax.nn.softplus(step_raw + step_bias[None, :])
    mixed = ssd_scan(
        values,
        bc_conv[:, :state_width],
        bc_conv[:, state_width:],
        step,
        decay_log,
        skip_scale,
        seq_first,
    )
    return mixed * jax.nn.silu(gate_raw)


def body(
    hidden_in,
    norm_gain,
    gate_value_weight,
    state_proj_weight,
    step_weight,
    conv_value_kernel,
    conv_value_bias,
    conv_state_kernel,
    conv_state_bias,
    step_bias,
    decay_log,
    skip_scale,
    gate_norm_gain,
    out_weight,
    out_cotangent,
    seq_lengths,
    seq_device,
    seq_offset,
):
    quarter = hidden_in.shape[0]
    group_width = gate_value_weight.shape[2]
    group_heads = step_weight.shape[1]
    full_gv, full_bc, full_step, full_out = (
        lax.all_gather(gate_value_weight, "dp", axis=0, tiled=True),
        lax.all_gather(state_proj_weight, "dp", axis=0, tiled=True),
        lax.all_gather(step_weight, "dp", axis=0, tiled=True),
        lax.all_gather(out_weight, "dp", axis=0, tiled=True),
    )
    joined = jnp.concatenate([full_gv.reshape(D, 2 * group_width), full_step, full_bc], axis=1)
    row_mask, seq_first, keep_mask = span_layout(
        seq_lengths, seq_device, seq_offset, lax.axis_index("dp")
    )
    local_mask = lax.dynamic_slice_in_dim(row_mask, lax.axis_index("tensor") * quarter, quarter)
    inv_rms = lax.rsqrt(jnp.mean(hidden_in * hidden_in, axis=-1) + EPSILON)
    scaled = hidden_in * inv_rms[:, None]
    normed_local = (scaled * norm_gain[None, :]).astype(jnp.bfloat16)
    normed = lax.all_gather(normed_local, "tensor", axis=0, tiled=True)
    projected = jnp.dot(normed, joined, preferred_element_type=jnp.float32)
    gate_raw = projected[:, :group_width]
    value_raw = projected[:, group_width : 2 * group_width]
    step_raw = projected[:, 2 * group_width : 2 * group_width + group_heads]
    bc_raw = projected[:, 2 * group_width + group_heads :]
    gated, pullback = jax.vjp(
        partial(mixer_core, seq_first, keep_mask),
        gate_raw,
        value_raw,
        bc_raw,
        step_raw,
        conv_value_kernel,
        conv_value_bias,
        conv_state_kernel,
        conv_state_bias,
        step_bias,
        decay_log,
        skip_scale,
    )
    square_total = lax.psum(jnp.sum(gated * gated, axis=-1), "tensor")
    gate_inv = lax.rsqrt(square_total / E + EPSILON)
    unit_norm = gated * gate_inv[:, None]
    normed_y = (unit_norm * gate_norm_gain[None, :]).astype(jnp.bfloat16)
    mixer_rows = lax.psum_scatter(
        contract(normed_y, full_out, 1, 1), "tensor", scatter_dimension=0, tiled=True
    )
    output = hidden_in + local_mask[:, None] * mixer_rows
    again_gv, again_bc, again_step, again_out = (
        lax.all_gather(gate_value_weight, "dp", axis=0, tiled=True),
        lax.all_gather(state_proj_weight, "dp", axis=0, tiled=True),
        lax.all_gather(step_weight, "dp", axis=0, tiled=True),
        lax.all_gather(out_weight, "dp", axis=0, tiled=True),
    )
    back_joined = jnp.concatenate(
        [again_gv.reshape(D, 2 * group_width), again_step, again_bc], axis=1
    )
    back_local = (local_mask[:, None] * out_cotangent).astype(jnp.bfloat16)
    back_mix = lax.all_gather(back_local, "tensor", axis=0, tiled=True)
    out_weight_grad = contract(back_mix, normed_y, 0, 0)
    back_y = jnp.dot(back_mix, again_out, preferred_element_type=jnp.float32)
    gate_gain_grad = jnp.sum(back_y * unit_norm, axis=0)
    weighted = back_y * gate_norm_gain[None, :]
    cross_sum = lax.psum(jnp.sum(weighted * unit_norm, axis=-1), "tensor")
    back_gated = gate_inv[:, None] * (weighted - unit_norm * (cross_sum / E)[:, None])
    pulled = pullback(back_gated)
    back_proj = jnp.concatenate([pulled[0], pulled[1], pulled[3], pulled[2]], axis=1).astype(
        jnp.bfloat16
    )
    weight_terms = contract(normed, back_proj, 0, 0)
    back_normed = lax.psum_scatter(
        contract(back_proj, back_joined, 1, 1), "tensor", scatter_dimension=0, tiled=True
    )
    norm_grad = jnp.sum(back_normed * scaled, axis=0)
    back_scaled = back_normed * norm_gain[None, :]
    hidden_gradient = out_cotangent + inv_rms[:, None] * (
        back_scaled - scaled * jnp.mean(back_scaled * scaled, axis=-1)[:, None]
    )
    gv_grad = weight_terms[:, : 2 * group_width].reshape(D, 2, group_width)
    step_grad = weight_terms[:, 2 * group_width : 2 * group_width + group_heads]
    bc_grad = weight_terms[:, 2 * group_width + group_heads :]
    gv_out, step_out, out_out = (
        lax.psum_scatter(gv_grad, "dp", scatter_dimension=0, tiled=True),
        lax.psum_scatter(step_grad, "dp", scatter_dimension=0, tiled=True),
        lax.psum_scatter(out_weight_grad, "dp", scatter_dimension=0, tiled=True),
    )
    bc_out, gain_out, state_kernel_out, state_bias_out = (
        lax.psum_scatter(bc_grad, ("dp", "tensor"), scatter_dimension=0, tiled=True),
        lax.psum_scatter(norm_grad, ("dp", "tensor"), scatter_dimension=0, tiled=True),
        lax.psum_scatter(pulled[6], ("dp", "tensor"), scatter_dimension=0, tiled=True),
        lax.psum_scatter(pulled[7], ("dp", "tensor"), scatter_dimension=0, tiled=True),
    )
    small_sums = lax.psum(
        (pulled[4], pulled[5], pulled[8], pulled[9], pulled[10], gate_gain_grad), "dp"
    )
    return (
        output,
        hidden_gradient,
        gain_out,
        gv_out,
        bc_out,
        step_out,
        small_sums[0],
        small_sums[1],
        state_kernel_out,
        state_bias_out,
        small_sums[2],
        small_sums[3],
        small_sums[4],
        small_sums[5],
        out_out,
    )


def solution(mesh):
    in_specs = (
        P(("dp", "tensor"), None),
        P(),
        P("dp", None, "tensor"),
        P("dp", None),
        P("dp", "tensor"),
        P("tensor", None),
        P("tensor"),
        P(),
        P(),
        P("tensor"),
        P("tensor"),
        P("tensor"),
        P("tensor"),
        P("dp", "tensor"),
        P(("dp", "tensor"), None),
        P(),
        P(),
        P(),
    )
    out_specs = (
        P(("dp", "tensor"), None),
        P(("dp", "tensor"), None),
        P(("dp", "tensor")),
        P("dp", None, "tensor"),
        P(("dp", "tensor"), None),
        P("dp", "tensor"),
        P("tensor", None),
        P("tensor"),
        P(("dp", "tensor"), None),
        P(("dp", "tensor")),
        P("tensor"),
        P("tensor"),
        P("tensor"),
        P("tensor"),
        P("dp", "tensor"),
    )
    return jax.shard_map(body, mesh=mesh, in_specs=in_specs, out_specs=out_specs, check_vma=False)
```

profile of v0, /device:TPU:0, one launch (start us, length us, event | category | flops | bytes accessed | tf_op | source)
XLA Modules:
  0.0 1306.2 jit_solution(16028280378713960918)
XLA Ops:
  16.3 35.8 %all_gather.25 = bf16[1536,256]{1,0:T(8,128)(2,1)S(1)} all-gather(bf16[192,256]{1,0:T(8,128)(2,1)S(1)} %copy-done.25), channel_id=1, replica_groups=mesh['dp'=8,'tensor'=4] {'dp'}, dimensions={0}, use_global_device_ids=true | all-gather | bytes 884736 | tf_op jit(solution)/shard_map/all_gather | solution.py:161
  52.2 30.9 %all-gather = bf16[8,192,12]{1,2,0:T(8,128)(2,1)S(1)} all-gather(bf16[1,192,12]{1,2,0:T(8,128)(2,1)S(1)} %bitcast.410), channel_id=1, replica_groups=mesh['dp'=8,'tensor'=4] {'dp'}, dimensions={0}, use_global_device_ids=true | all-gather | bytes 41472 | tf_op jit(solution)/shard_map/all_gather | solution.py:162
  87.7 12.6 all-gather.8.cloned.1.call-done
  100.2 5.4 copy.242
  105.7 9.5 concatenate.26
  115.2 14.0 %all-gather.6.cloned.1.call-done = bf16[1024,1536]{1,0:T(8,128)(2,1)} async-done(((bf16[256,1536]{1,0:T(8,128)(2,1)}), bf16[1024,1536]{1,0:T(8,128)(2,1)}) %all-gather.6.cloned.1.call-update) | async-done | bytes 3145744 | tf_op jit(solution)/shard_map/all_gather | solution.py:173
  129.2 9.6 fusion.153
  152.0 7.7 fusion.106
  159.7 3.8 reshape.358
  170.0 126.6 %while.46 = (s32[]{:T(128)}, f32[12,128,64]{1,2,0:T(8,128)S(1)}, f32[4,256,12,64]{1,0,3,2:T(4,128)}, f32[4,12,128,64]{2,3,1,0:T(8,128)}, f32[4,256,12]{1,2,0:T(8...) while((s32[]{:T(128)}, f32[12,128,64]{1,2,0:T(8,128)S(1)}, ...), condition=%wide.region_6.7_spmd.clone.clone, body=%wide.region_3.6_spmd.clone.clone.sunk | while | flops 1314428928 | bytes 12088955 | solution.py:101
  175.0 5.2 fusion.252
  181.0 17.9 %dynamic_update_slice.86 = f32[4,256,12,64]{1,0,3,2:T(4,128)} dynamic-update-slice(f32[4,256,12,64]{1,0,3,2:T(4,128)} %get-tuple-element.1301, f32[1,256,12,64]{1,0,3,2:T(1,128)S(1)} %copy.279, s32[]{:T(128)} %get-tuple-element.1299, s32[]{:T(128)} %constant.185.clone.1..sunk.1, s32[]{:T(128)} %constant.185.clone.1..sunk.1, s32[]{:T(128)} %constant.185.clone.1..sunk.1) | dynamic-update-slice | bytes 1572868 | tf_op jit(solution)/shard_map/jvp()/while/body/jit(dynamic_update_index_in_dim)/dynamic_update_slice | solution.py:101
  206.7 5.1 fusion.252
  212.7 17.9 %dynamic_update_slice.86 = f32[4,256,12,64]{1,0,3,2:T(4,128)} dynamic-update-slice(f32[4,256,12,64]{1,0,3,2:T(4,128)} %get-tuple-element.1301, f32[1,256,12,64]{1,0,3,2:T(1,128)S(1)} %copy.279, s32[]{:T(128)} %get-tuple-element.1299, s32[]{:T(128)} %constant.185.clone.1..sunk.1, s32[]{:T(128)} %constant.185.clone.1..sunk.1, s32[]{:T(128)} %constant.185.clone.1..sunk.1) | dynamic-update-slice | bytes 1572868 | tf_op jit(solution)/shard_map/jvp()/while/body/jit(dynamic_update_index_in_dim)/dynamic_update_slice | solution.py:101
  238.4 5.2 fusion.252
  244.4 17.9 %dynamic_update_slice.86 = f32[4,256,12,64]{1,0,3,2:T(4,128)} dynamic-update-slice(f32[4,256,12,64]{1,0,3,2:T(4,128)} %get-tuple-element.1301, f32[1,256,12,64]{1,0,3,2:T(1,128)S(1)} %copy.279, s32[]{:T(128)} %get-tuple-element.1299, s32[]{:T(128)} %constant.185.clone.1..sunk.1, s32[]{:T(128)} %constant.185.clone.1..sunk.1, s32[]{:T(128)} %constant.185.clone.1..sunk.1) | dynamic-update-slice | bytes 1572868 | tf_op jit(solution)/shard_map/jvp()/while/body/jit(dynamic_update_index_in_dim)/dynamic_update_slice | solution.py:101
  270.0 5.1 fusion.252
  276.0 17.9 %dynamic_update_slice.86 = f32[4,256,12,64]{1,0,3,2:T(4,128)} dynamic-update-slice(f32[4,256,12,64]{1,0,3,2:T(4,128)} %get-tuple-element.1301, f32[1,256,12,64]{1,0,3,2:T(1,128)S(1)} %copy.279, s32[]{:T(128)} %get-tuple-element.1299, s32[]{:T(128)} %constant.185.clone.1..sunk.1, s32[]{:T(128)} %constant.185.clone.1..sunk.1, s32[]{:T(128)} %constant.185.clone.1..sunk.1) | dynamic-update-slice | bytes 1572868 | tf_op jit(solution)/shard_map/jvp()/while/body/jit(dynamic_update_index_in_dim)/dynamic_update_slice | solution.py:101
  296.6 2.6 copy.243
  299.2 4.5 multiply_reduce_fusion.11
  303.7 6.0 psum.56
  309.8 9.0 multiply_reduce_fusion.5
  318.8 5.6 psum.57
  324.4 6.3 fusion.107
  330.7 5.1 reshape.363
  341.1 212.6 %while.45 = (s32[]{:T(128)}, f32[12]{0:T(128)S(1)}, f32[12,128,64]{1,2,0:T(8,128)S(1)}, f32[4,256,12,64]{1,0,3,2:T(4,128)}, f32[4,256,128]{2,1,0:T(8,128)}, /*in...) while((s32[]{:T(128)}, f32[12]{0:T(128)S(1)}, ...), condition=%wide.region_26.27_spmd.clone, body=%wide.region_12.26_spmd.clone.sunk | while | flops 3039754240 | bytes 31193800 | solution.py:101
  341.3 2.7 constant_dynamic-slice_fusion.4
  351.8 4.9 fusion.235
  369.1 3.6 fusion.238
  373.5 17.9 %dynamic_update_slice.82 = f32[4,256,12,64]{1,0,3,2:T(4,128)} dynamic-update-slice(f32[4,256,12,64]{1,0,3,2:T(4,128)} %get-tuple-element.1353, f32[1,256,12,64]{1,0,3,2:T(1,128)S(1)} %copy.270, s32[]{:T(128)S(6)} %sub.398, s32[]{:T(128)} %constant.185.clone.1..sunk, s32[]{:T(128)} %constant.185.clone.1..sunk, s32[]{:T(128)} %constant.185.clone.1..sunk) | dynamic-update-slice | bytes 1572868 | tf_op jit(solution)/shard_map/transpose(jvp())/while/body/jit(dynamic_update_index_in_dim)/dynamic_update_slice | solution.py:101
  394.3 2.7 constant_dynamic-slice_fusion.4
  404.8 4.9 fusion.235
  422.1 3.6 fusion.238
  426.5 17.9 %dynamic_update_slice.82 = f32[4,256,12,64]{1,0,3,2:T(4,128)} dynamic-update-slice(f32[4,256,12,64]{1,0,3,2:T(4,128)} %get-tuple-element.1353, f32[1,256,12,64]{1,0,3,2:T(1,128)S(1)} %copy.270, s32[]{:T(128)S(6)} %sub.398, s32[]{:T(128)} %constant.185.clone.1..sunk, s32[]{:T(128)} %constant.185.clone.1..sunk, s32[]{:T(128)} %constant.185.clone.1..sunk) | dynamic-update-slice | bytes 1572868 | tf_op jit(solution)/shard_map/transpose(jvp())/while/body/jit(dynamic_update_index_in_dim)/dynamic_update_slice | solution.py:101
  447.3 2.7 constant_dynamic-slice_fusion.4
  457.8 4.9 fusion.235
  475.1 3.6 fusion.238
  479.5 17.9 %dynamic_update_slice.82 = f32[4,256,12,64]{1,0,3,2:T(4,128)} dynamic-update-slice(f32[4,256,12,64]{1,0,3,2:T(4,128)} %get-tuple-element.1353, f32[1,256,12,64]{1,0,3,2:T(1,128)S(1)} %copy.270, s32[]{:T(128)S(6)} %sub.398, s32[]{:T(128)} %constant.185.clone.1..sunk, s32[]{:T(128)} %constant.185.clone.1..sunk, s32[]{:T(128)} %constant.185.clone.1..sunk) | dynamic-update-slice | bytes 1572868 | tf_op jit(solution)/shard_map/transpose(jvp())/while/body/jit(dynamic_update_index_in_dim)/dynamic_update_slice | solution.py:101
  500.3 2.7 constant_dynamic-slice_fusion.4
  510.8 4.9 fusion.235
  528.1 3.6 fusion.238
  532.5 17.9 %dynamic_update_slice.82 = f32[4,256,12,64]{1,0,3,2:T(4,128)} dynamic-update-slice(f32[4,256,12,64]{1,0,3,2:T(4,128)} %get-tuple-element.1353, f32[1,256,12,64]{1,0,3,2:T(1,128)S(1)} %copy.270, s32[]{:T(128)S(6)} %sub.398, s32[]{:T(128)} %constant.185.clone.1..sunk, s32[]{:T(128)} %constant.185.clone.1..sunk, s32[]{:T(128)} %constant.185.clone.1..sunk) | dynamic-update-slice | bytes 1572868 | tf_op jit(solution)/shard_map/transpose(jvp())/while/body/jit(dynamic_update_index_in_dim)/dynamic_update_slice | solution.py:101
  553.8 4.3 copy.244
  561.3 4.4 fusion.142
  567.7 6.4 fusion.141
  581.5 12.6 concatenate.33
  594.1 9.4 fusion.155
  603.5 4.2 copy-done.12
  608.9 8.1 slice.195
  617.0 14.9 %copy.175 = f32[1536,2,768]{2,1,0:T(2,128)} copy(f32[1536,2,768]{0,2,1:T(8,128)} %bitcast.364) | data formatting | bytes 18874368 | tf_op jit(solution)/shard_map/reshape | solution.py:231
  632.0 11.7 fusion.154
  645.5 6.9 fusion.140
  652.5 2.7 slice.196
  655.2 3.1 copy.180
  658.3 6.8 fusion.139
  667.2 39.1 %all-reduce.29 = (f32[768,4]{0,1:T(4,128)}, f32[768]{0:T(1024)}, f32[12]{0:T(128)}, f32[12]{0:T(128)}, f32[12]{0:T(128)}, /*index=5*/f32[768]{0:T(1024)}) all-reduce(f32[768,4]{0,1:T(4,128)S(1)} %pad_add_fusion, f32[768]{0:T(1024)S(1)} %get-tuple-element.901, ...), channel_id=1, replica_groups=mesh['dp'=8,'tensor'=4] {'dp'}, use_global_device_ids=true, to_apply=%region_38.39 | all-reduce | flops 4644 | bytes 37152 | tf_op jit(solution)/shard_map/psum | solution.py:245
  707.9 266.6 %all-reduce.32.cloned.1.call-done = f32[1536,2,768]{2,1,0:T(2,128)} async-done(((f32[1536,2,768]{2,1,0:T(2,128)}), f32[1536,2,768]{2,1,0:T(2,128)}) %all-reduce.32.cloned.1.call-update) | async-done | bytes 9437200
  974.5 2.7 constant_dynamic-slice_fusion.2
  977.2 57.4 %reduce-scatter.13.cloned.1.call-done = f32[256,1536]{1,0:T(8,128)} async-done(((f32[1024,1536]{1,0:T(8,128)}), f32[256,1536]{1,0:T(8,128)}) %reduce-scatter.13.cloned.1.call-update) | async-done | bytes 1572880 | tf_op jit(solution)/shard_map/reduce_scatter | solution.py:223
  1036.4 39.8 %all-reduce.28 = (f32[1536]{0:T(1024)S(1)}, f32[256,4]{0,1:T(4,128)S(1)}, f32[256]{0:T(256)S(1)}) all-reduce(f32[1536]{0:T(1024)S(1)} %get-tuple-element.899, f32[256,4]{0,1:T(4,128)S(1)} %pad_add_fusion.1, f32[256]{0:T(256)S(1)} %get-tuple-element.906), channel_id=4, replica_groups=mesh['dp'=8,'tensor'=4] {'dp','tensor'}, use_global_device_ids=true, to_apply=%region_30.31.clone | all-reduce | flops 2816 | bytes 22528
  1078.1 18.2 %reduce-scatter.11.cloned.1.call-done = f32[256,1536]{1,0:T(8,128)} async-done(((f32[1024,1536]{1,0:T(8,128)}), f32[256,1536]{1,0:T(8,128)}) %reduce-scatter.11.cloned.1.call-update) | async-done | bytes 1572880 | tf_op jit(solution)/shard_map/reduce_scatter | solution.py:197
  1096.2 4.0 multiply_add_fusion.1
  1100.2 99.7 %reduce-scatter.17.cloned.1.call-done = f32[48,256]{1,0:T(8,128)} async-done(((f32[1536,256]{1,0:T(8,128)}), f32[48,256]{1,0:T(8,128)}) %reduce-scatter.17.cloned.1.call-update) | async-done | bytes 49168
  1200.0 99.2 %reduce-scatter.15.cloned.1.call-done = f32[192,768]{1,0:T(8,128)} async-done(((f32[1536,768]{1,0:T(8,128)}), f32[192,768]{1,0:T(8,128)}) %reduce-scatter.15.cloned.1.call-update) | async-done | bytes 589840 | tf_op jit(solution)/shard_map/reduce_scatter | solution.py:237
  (522 shorter events, 189.3 us)
Async XLA Ops:
  7.2 3.2 copy-start.5
  7.2 5.8 copy-start.61
  7.2 5.8 copy-start.64
  7.2 5.8 copy-start.62
  7.2 6.7 copy-start.18
  7.2 93.0 %all-gather.8.cloned.1.call-start = ((), (), s32[]{:S(2)}) async-start(), calls=%async_computation.6 | async-start | bytes 5308416 | tf_op jit(solution)/shard_map/all_gather | solution.py:160
  8.0 121.3 %all-gather.6.cloned.1.call-start = ((), (), s32[]{:S(2)}) async-start(), calls=%async_computation.5 | async-start | bytes 3932160 | tf_op jit(solution)/shard_map/all_gather | solution.py:173
  10.4 6.0 copy-start.25
  12.2 40.0 %copy-start.52 = (bf16[192,12]{0,1:T(8,128)(2,1)S(1)}, bf16[192,12]{0,1:T(8,128)(2,1)}, u32[]{:S(2)}) copy-start(bf16[192,12]{0,1:T(8,128)(2,1)} %param.26) | copy-start | bytes 13828
  12.2 71.9 %copy-start.55 = (f32[256,4]{0,1:T(4,128)S(1)}, f32[256,4]{0,1:T(4,128)}, u32[]{:S(2)}) copy-start(f32[256,4]{0,1:T(4,128)} %param.29) | copy-start | bytes 12292
  12.2 72.5 %copy-start.38 = (f32[768,4]{0,1:T(4,128)S(1)}, f32[768,4]{0,1:T(4,128)}, u32[]{:S(2)}) copy-start(f32[768,4]{0,1:T(4,128)} %param.27) | copy-start | bytes 36868
  12.2 73.1 %copy-start.65 = (f32[12]{0:T(128)S(1)}, f32[12]{0:T(128)}, u32[]{:S(2)}) copy-start(f32[12]{0:T(128)} %param.32) | copy-start | bytes 148
  12.2 297.6 %all-gather.10.cloned.1.call-start = ((), (), s32[]{:S(2)}) async-start(), calls=%async_computation.7 | async-start | bytes 2654208 | tf_op jit(solution)/shard_map/all_gather | solution.py:163
  12.9 296.8 %all-gather.12.cloned.1.call-start = ((), (), s32[]{:S(2)}) async-start(), calls=%async_computation.9 | async-start | bytes 3932160 | tf_op jit(solution)/shard_map/all_gather | solution.py:211
  15.0 691.3 %reduce-scatter.19.cloned.1.call-start = ((), (), s32[]{:S(2)}) async-start(), calls=%async_computation.13 | async-start | bytes 884736
  84.0 21.6 %copy-start.28 = (pred[1024]{0:T(1024)(128)(4,1)}, pred[1024]{0:T(1024)(128)(4,1)S(1)}, u32[]{:S(2)}) copy-start(pred[1024]{0:T(1024)(128)(4,1)S(1)} %get-tuple-element.1026) | copy-start | bytes 3076
  84.1 21.6 %copy-start.31 = (pred[1024]{0:T(1024)(128)(4,1)}, pred[1024]{0:T(1024)(128)(4,1)S(1)}, u32[]{:S(2)}) copy-start(pred[1024]{0:T(1024)(128)(4,1)S(1)} %get-tuple-element.1027) | copy-start | bytes 3076
  138.8 5.8 copy-start
  139.0 5.6 copy-start.14
  139.1 5.5 copy-start.15
  139.3 5.4 copy-start.16
  139.7 12.3 copy-start.1
  142.0 2.7 copy-start.29
  142.0 2.7 copy-start.32
  142.0 2.7 copy-start.42
  142.0 2.7 copy-start.44
  142.0 2.7 copy-start.46
  142.1 2.7 copy-start.50
  142.1 2.7 copy-start.63
  163.5 2.2 copy-start.57
  165.8 4.1 copy-start.10
  165.8 4.1 copy-start.11
  165.8 4.1 copy-start.27
  166.9 3.1 copy-start.21
  299.2 10.6 copy-start.53
  335.8 5.3 copy-start.13
  335.8 5.3 copy-start.35
  364.0 5.1 copy-start.7
  417.0 5.1 copy-start.7
  470.0 5.1 copy-start.7
  523.0 5.1 copy-start.7
  553.7 4.4 copy-start.20
  553.7 7.6 copy-start.30
  553.8 7.6 copy-start.33
  553.8 12.0 copy-start.41
  553.8 12.0 copy-start.47
  559.1 7.5 copy-start.8
  561.3 4.9 copy-start.40
  561.3 4.9 copy-start.45
  561.3 5.3 copy-start.3
  561.3 5.3 copy-start.4
  576.7 2.2 copy-start.51
  577.8 2.3 copy-start.34
  603.5 4.2 copy-start.12
  608.9 365.6 %all-reduce.32.cloned.1.call-start = ((), (), s32[]{:S(2)}) async-start(), calls=%async_computation.14 | async-start | bytes 18874368
  631.9 402.6 %reduce-scatter.13.cloned.1.call-start = ((), (), s32[]{:S(2)}) async-start(), calls=%async_computation.10 | async-start | bytes 7864320 | tf_op jit(solution)/shard_map/reduce_scatter | solution.py:223
  643.7 452.5 %reduce-scatter.11.cloned.1.call-start = ((), (), s32[]{:S(2)}) async-start(), calls=%async_computation.8 | async-start | bytes 7864320 | tf_op jit(solution)/shard_map/reduce_scatter | solution.py:197
  652.4 547.5 %reduce-scatter.17.cloned.1.call-start = ((), (), s32[]{:S(2)}) async-start(), calls=%async_computation.12 | async-start | bytes 1622016
  658.3 640.9 %reduce-scatter.15.cloned.1.call-start = ((), (), s32[]{:S(2)}) async-start(), calls=%async_computation.11 | async-start | bytes 5308416 | tf_op jit(solution)/shard_map/reduce_scatter | solution.py:237
  665.2 369.4 %copy-start.6 = (f32[256,1536]{1,0:T(8,128)S(1)}, f32[256,1536]{1,0:T(8,128)}, u32[]{:S(2)}) copy-start(f32[256,1536]{1,0:T(8,128)} %param.22) | copy-start | bytes 4718596
  665.2 369.4 %copy-start.26 = (f32[1536]{0:T(1024)S(1)}, f32[1536]{0:T(1024)}, u32[]{:S(2)}) copy-start(f32[1536]{0:T(1024)} %param.23) | copy-start | bytes 18436
  665.2 369.4 %copy-start.37 = (f32[256]{0:T(256)S(1)}, f32[256]{0:T(256)}, u32[]{:S(2)}) copy-start(f32[256]{0:T(256)} %copy-done.36) | copy-start | bytes 3076
  665.2 431.0 %copy-start.19 = (f32[256,1536]{1,0:T(8,128)S(1)}, f32[256,1536]{1,0:T(8,128)}, u32[]{:S(2)}) copy-start(f32[256,1536]{1,0:T(8,128)} %param.36) | copy-start | bytes 4718596
  665.2 431.0 %copy-start.49 = (f32[256]{0:T(256)S(1)}, f32[256]{0:T(256)}, u32[]{:S(2)}) copy-start(f32[256]{0:T(256)} %copy-done.48) | copy-start | bytes 3076
  (17 other events, 23.1 us)
Sparse Core Ops, SparseCore 0:
  10.2 89.9 all-gather.7
  102.4 26.8 all-gather.5
  131.4 52.0 all-gather.9
  185.5 27.0 all-gather.11
  609.0 63.8 reduce-scatter.18
  677.1 297.3 all-reduce.31
  977.2 57.3 reduce-scatter.12
  1037.1 59.0 reduce-scatter.10
  1102.9 97.0 reduce-scatter.16
  1204.5 94.6 reduce-scatter.14
where the time goes:
time: 1320 us; the launch traced here: 1310 us
  waiting for transfers between devices  569 us (43%)
  local copies, waits for them, and re-layouts  321 us (24%)
  matrix products  158 us (12%)
  blocking collectives  157 us (12%)
  other arithmetic  82.4 us (6%)
  between operations  16 us (1%)
    unnamed x13, waiting for transfers between devices  368 us
    dynamic_update_slice x32, local copies, waits for them, and re-layouts, ssd_scan(): _, outputs = lax.scan(jax.checkpoint(span_step), zero_state, scanned)  161 us
    reduce_scatter x1, waiting for transfers between devices, body(): lax.psum_scatter(out_weight_grad, 'dp', scatter_dimension=0, tiled=True)  99.2 us
    reduce_scatter x1, waiting for transfers between devices, body(): lax.psum_scatter(contract(back_proj, back_joined, 1, 1), 'tensor', scatte...  57.4 us
    dot_general x12, matrix products, span_step(): jnp.einsum('tsh,shp->thp', weights, value_blk, precision=HIGHEST)  54.7 us
    unnamed x157, local copies, waits for them, and re-layouts  40.7 us
    unnamed x1, blocking collectives  39.8 us
    psum x1, blocking collectives, body(): lax.psum((pulled[4], pulled[5], pulled[8], pulled[9], pulled[10], gate_ga...  39.1 us
  transfers between devices with their start and end apart: 10, of which 7 were waited for; matrix products, arithmetic and copies ran while one was open for 20% of the time, Pallas kernels for 0%

commit v1 on v0

v1 whole, which is shorter than its diff:
```python
from functools import partial

import jax, jax.numpy as jnp
from jax import lax
from jax.experimental import pallas as pl
from jax.experimental.pallas import tpu as pltpu
from jax.sharding import PartitionSpec as P
f32=jnp.float32; bf16=jnp.bfloat16
Q=128
NS=128
VW=768
HW=64
CW=1024
RW=1152
SPAN=256
NEG=-1e30

def mm(a,b,ca=1,cb=0):
    return lax.dot_general(a,b,(((ca,),(cb,)),((),())),preferred_element_type=f32)

def split2(x):
    hi=x.astype(bf16); return hi,(x-hi.astype(f32)).astype(bf16)

def split3(x):
    hi=x.astype(bf16); r=x-hi.astype(f32); mid=r.astype(bf16); return hi,mid,(r-mid.astype(f32)).astype(bf16)

def tri_sum(tri,x):
    a,b,c=split3(x); w=x.shape[1]
    p=mm(tri,jnp.concatenate([a,b,c],axis=1))
    return p[:,:w]+p[:,w:2*w]+p[:,2*w:]

def spread(x,ee):
    a,b=split2(x)
    return mm(jnp.concatenate([a,b],axis=1),ee)

def head_sum(x,hh):
    a,b=split2(x)
    return mm(jnp.concatenate([a,b],axis=1),hh)

def iotas():
    return lax.broadcasted_iota(jnp.int32,(Q,Q),0),lax.broadcasted_iota(jnp.int32,(Q,Q),1)

def softplus(z):
    return jnp.maximum(z,0.0)+jnp.log(1.0+jnp.exp(-jnp.abs(z)))

def sig(z):
    return 1.0/(1.0+jnp.exp(-z))

def halves(x):
    lane=lax.broadcasted_iota(jnp.int32,x.shape,1)
    lo=jnp.where(lane<HW,x,0.0); hi=jnp.where(lane<HW,0.0,x)
    return jnp.concatenate([lo.astype(bf16),hi.astype(bf16)],axis=0)

def fwd_kernel(c0,nc,first_ref,raw_ref,ck_ref,cb_ref,sb_ref,dl_ref,ee_ref,s_in,t_in,y_ref,pre_ref,sp_ref,s_ref,t_ref,ext):
    i=pl.program_id(0)
    @pl.when(i==0)
    def _():
        s_ref[...]=s_in[...]; t_ref[...]=t_in[...]
    c=c0+i
    start=(first_ref[c//(SPAN//Q)]==1)&(c%(SPAN//Q)==0)
    @pl.when(start)
    def _():
        s_ref[...]=jnp.zeros_like(s_ref); t_ref[...]=jnp.zeros_like(t_ref)
    ext[0:8,:]=t_ref[...]
    x=raw_ref[:,:CW]
    ext[8:8+Q,:]=x
    t_ref[...]=raw_ref[Q-8:Q,:CW]
    pre=cb_ref[...]+ck_ref[3:4,:]*x
    for j in (1,2,3):
        pre=pre+ck_ref[3-j:4-j,:]*ext[8-j:8-j+Q,:]
    pre_ref[...]=pre
    act=pre*sig(pre)
    v=act[:,:VW]; b=act[:,VW:VW+NS].astype(bf16); cc=act[:,VW+NS:].astype(bf16)
    dt=softplus(raw_ref[:,CW:]+sb_ref[...])
    a=-dt*jnp.exp(dl_ref[...])
    row,col=iotas()
    low=row>=col
    tri=jnp.where(low,1.0,0.0).astype(bf16)
    cum=tri_sum(tri,a)
    cum_t=cum.T
    last=cum[Q-1:Q,:]
    ee=ee_ref[...]
    sprd=spread(jnp.concatenate([dt,jnp.exp(cum),jnp.exp(last-cum)],axis=0),ee)
    dte,ecum,etail=sprd[:Q],sprd[Q:2*Q],sprd[2*Q:]
    x=v*dte
    g=mm(cc,b,1,1)
    parts=[]
    for p in range(VW//128):
        ws=[]
        for h in (2*p,2*p+1):
            d=jnp.where(low,cum[:,h:h+1]-cum_t[h:h+1,:],NEG)
            ws.append((jnp.exp(d)*g).astype(bf16))
        parts.append(mm(jnp.concatenate(ws,axis=1),halves(x[:,128*p:128*p+128])))
    s=s_ref[...]
    sp_ref[0]=s
    y_ref[...]=jnp.concatenate(parts,axis=1)+ecum*mm(cc,s.astype(bf16))
    s_ref[...]=ecum[Q-1:Q,:]*s+mm(b,(x*etail).astype(bf16),0,0)

def bwd_kernel(c0,nc,nall,first_ref,raw_ref,pre_ref,y_ref,dy_ref,sp_ref,ck_ref,sb_ref,dl_ref,sk_ref,ee_ref,hh_ref,ds_in,sn_in,h_in,acc_in,acs_in,
               out_ref,ds_ref,sn_ref,h_ref,acc_ref,acs_ref,ext):
    i=pl.program_id(0)
    @pl.when(i==0)
    def _():
        ds_ref[...]=ds_in[...]; sn_ref[...]=sn_in[...]; h_ref[...]=h_in[...]; acc_ref[...]=acc_in[...]; acs_ref[...]=acs_in[...]
    c=c0+nc-1-i
    nxt=jnp.minimum(c+1,nall-1)
    start=(first_ref[nxt//(SPAN//Q)]==1)&(nxt%(SPAN//Q)==0)
    @pl.when(start)
    def _():
        ds_ref[...]=jnp.zeros_like(ds_ref); h_ref[...]=jnp.zeros_like(h_ref)
    pre=pre_ref[...]
    sg=sig(pre)
    act=pre*sg
    v=act[:,:VW]; b=act[:,VW:VW+NS].astype(bf16); cc=act[:,VW+NS:].astype(bf16)
    z=raw_ref[:,CW:]+sb_ref[...]
    dt=softplus(z)
    edl=jnp.exp(dl_ref[...])
    a=-dt*edl
    row,col=iotas()
    low=row>=col; up=row<=col
    cum=tri_sum(jnp.where(low,1.0,0.0).astype(bf16),a)
    cum_t=cum.T
    last=cum[Q-1:Q,:]
    ee=ee_ref[...]
    sprd=spread(jnp.concatenate([dt,jnp.exp(cum),jnp.exp(last-cum)],axis=0),ee)
    dte,ecum,etail=sprd[:Q],sprd[Q:2*Q],sprd[2*Q:]
    x=v*dte
    xb=x.astype(bf16)
    dy=dy_ref[...].astype(f32)
    dyb=dy.astype(bf16)
    gt=mm(b,cc,1,1)
    dgt=jnp.zeros((Q,Q),f32)
    parts=[]
    for p in range(VW//128):
        cols=slice(128*p,128*p+128)
        dw=mm(halves(x[:,cols]),dyb[:,cols],1,1)
        ws=[]
        for k in (0,1):
            h=2*p+k
            lt=jnp.exp(jnp.where(up,cum_t[h:h+1,:]-cum[:,h:h+1],NEG))
            ws.append((lt*gt).astype(bf16))
            dgt=dgt+lt*dw[k*Q:(k+1)*Q]
        parts.append(mm(jnp.concatenate(ws,axis=1),halves(dy[:,cols])))
    ds=ds_ref[...]
    dsb=ds.astype(bf16)
    s=sp_ref[0]
    dx=jnp.concatenate(parts,axis=1)+etail*mm(b,dsb)
    dgtb=dgt.astype(bf16)
    dye=(dy*ecum).astype(bf16)
    db=mm(dgtb,cc)+mm((x*etail).astype(bf16),dsb,1,1)
    dc=mm(dgtb,b,0,0)+mm(dye,s.astype(bf16),1,1)
    kk=jnp.sum(ds*sn_ref[...],axis=0,keepdims=True)
    kk=jnp.concatenate([kk,jnp.zeros((7,VW),f32)],axis=0)
    hs=head_sum(jnp.concatenate([dyb.astype(f32)*y_ref[...]-xb.astype(f32)*dx,v*dx,kk],axis=0),hh_ref[...])
    dcum,q,k0=hs[:Q],hs[Q:2*Q],hs[2*Q:2*Q+1]
    da=k0+tri_sum(jnp.where(up,1.0,0.0).astype(bf16),dcum)
    dst=(q-da*edl)*sig(z)
    ds_ref[...]=ecum[Q-1:Q,:]*ds+mm(cc,dye,0,0)
    sn_ref[...]=s
    acs_ref[0:1,:]+=jnp.sum(da*a,axis=0,keepdims=True)
    acs_ref[1:2,:]+=jnp.sum(dst,axis=0,keepdims=True)
    dv=dte*dx+sk_ref[...]*dy
    acc_ref[5:6,:VW]+=jnp.sum(dy*v,axis=0,keepdims=True)
    dpre=jnp.concatenate([dv,db,dc],axis=1)*(sg*(1.0+pre-act))
    ext[0:Q,:]=dpre
    ext[Q:Q+8,:]=h_ref[...]
    h_ref[...]=dpre[0:8,:]
    xr=raw_ref[:,:CW]
    draw=ck_ref[3:4,:]*dpre
    acc_ref[3:4,:]+=jnp.sum(dpre*xr,axis=0,keepdims=True)
    acc_ref[4:5,:]+=jnp.sum(dpre,axis=0,keepdims=True)
    for j in (1,2,3):
        sh=ext[j:j+Q,:]
        draw=draw+ck_ref[3-j:4-j,:]*sh
        acc_ref[3-j:4-j,:]+=jnp.sum(sh*xr,axis=0,keepdims=True)
    out_ref[:,:CW]=draw.astype(bf16)
    out_ref[:,CW:]=dst.astype(bf16)

def sd(shape,dt=f32): return jax.ShapeDtypeStruct(shape,dt)

def whole(shape): return pl.BlockSpec(shape,lambda i,*_: (0,)*len(shape))

def ssd_fwd(c0,nc,first,raw,ck,cb,sb,dl,ee,s_in,t_in):
    rb=lambda w: pl.BlockSpec((Q,w),lambda i,*_: (i,0))
    rin=pl.BlockSpec((Q,RW),lambda i,*_: (c0+i,0))
    return pl.pallas_call(partial(fwd_kernel,c0,nc),
        out_shape=(sd((nc*Q,VW)),sd((nc*Q,CW)),sd((nc,NS,VW)),sd((NS,VW)),sd((8,CW))),
        grid_spec=pltpu.PrefetchScalarGridSpec(num_scalar_prefetch=1,grid=(nc,),
            in_specs=[rin,whole((4,CW)),whole((1,CW)),whole((1,128)),whole((1,128)),whole((256,VW)),whole((NS,VW)),whole((8,CW))],
            out_specs=(rb(VW),rb(CW),pl.BlockSpec((1,NS,VW),lambda i,*_: (i,0,0)),whole((NS,VW)),whole((8,CW))),
            scratch_shapes=[pltpu.VMEM((Q+8,CW),f32)]),
        compiler_params=pltpu.CompilerParams(vmem_limit_bytes=40<<20),
        cost_estimate=pl.CostEstimate(flops=int(1.5e9*nc/8),bytes_accessed=16_000_000*nc//8,transcendentals=3_000_000*nc//8),
        name=f"ssd_forward_{c0}")(first,raw,ck,cb,sb,dl,ee,s_in,t_in)

def ssd_bwd(c0,nc,nall,first,raw,pre,y,dy,sp,ck,sb,dl,sk,ee,hh,ds,sn,hd,acc,acs,off=0):
    rv=lambda w,o=c0: pl.BlockSpec((Q,w),lambda i,*_: (o+nc-1-i,0))
    return pl.pallas_call(partial(bwd_kernel,c0,nc,nall),
        out_shape=(sd((nc*Q,RW),bf16),sd((NS,VW)),sd((NS,VW)),sd((8,CW)),sd((8,CW)),sd((8,128))),
        grid_spec=pltpu.PrefetchScalarGridSpec(num_scalar_prefetch=1,grid=(nc,),
            in_specs=[rv(RW),rv(CW,0),rv(VW,0),rv(VW),pl.BlockSpec((1,NS,VW),lambda i,*_: (nc-1-i,0,0)),
                      whole((4,CW)),whole((1,128)),whole((1,128)),whole((1,VW)),whole((256,VW)),whole((2*VW,128)),
                      whole((NS,VW)),whole((NS,VW)),whole((8,CW)),whole((8,CW)),whole((8,128))],
            out_specs=(rv(RW,0),whole((NS,VW)),whole((NS,VW)),whole((8,CW)),whole((8,CW)),whole((8,128))),
            scratch_shapes=[pltpu.VMEM((Q+8,CW),f32)]),
        compiler_params=pltpu.CompilerParams(vmem_limit_bytes=40<<20),
        cost_estimate=pl.CostEstimate(flops=int(3e9*nc/8),bytes_accessed=24_000_000*nc//8,transcendentals=4_000_000*nc//8),
        name=f"ssd_backward_{c0}")(first,raw,pre,y,dy,sp,ck,sb,dl,sk,ee,hh,ds,sn,hd,acc,acs)


D = 1536
H = 48
E = 3072
TOK_DEV = 1024
SEQ_DEV = 4
EPSILON = 1e-05
PARTS = 2


def contract(left, right, left_dim, right_dim, out=f32):
    return lax.dot_general(
        left, right, (((left_dim,), (right_dim,)), ((), ())), preferred_element_type=f32
    ).astype(out)


def span_layout(seq_lengths, seq_device, seq_offset, device):
    span_index = jnp.arange(SEQ_DEV, dtype=jnp.int32)
    needed = (seq_lengths + SPAN - 1) // SPAN
    owned_seq = (seq_device == device) & (seq_lengths > 0)
    relative = span_index[None, :] - seq_offset[:, None]
    inside = owned_seq[:, None] & (relative >= 0) & (relative < needed[:, None])
    live_rows = jnp.sum(
        jnp.where(inside, jnp.clip(seq_lengths[:, None] - relative * SPAN, 0, SPAN), 0), axis=0
    )
    seq_first = jnp.any(inside & (relative == 0), axis=0)
    return live_rows, seq_first.astype(jnp.int32)


def ring_order(count):
    if count == 8:
        return [0, 2, 4, 6, 7, 5, 3, 1]
    return list(range(count))


def place_kernel(cols, rows, off_ref, *refs):
    count = len(cols)
    out, sem = refs[count], refs[count + 1]
    copies = []
    for k, (c0, w) in enumerate(cols):
        at = pl.multiple_of(off_ref[k] * rows, 16)
        copies.append(
            pltpu.make_async_copy(refs[k], out.at[pl.ds(at, rows), pl.ds(c0, w)], sem.at[k])
        )
    for copy in copies:
        copy.start()
    for copy in copies:
        copy.wait()


def place(pieces, offsets, total):
    rows = pieces[0][0].shape[0]
    cols = [(c0, x.shape[1]) for x, c0 in pieces]
    width = max(c0 + w for c0, w in cols)
    any_spec = pl.BlockSpec(memory_space=pl.ANY)
    return pl.pallas_call(
        partial(place_kernel, cols, rows),
        out_shape=jax.ShapeDtypeStruct((total, width), pieces[0][0].dtype),
        grid_spec=pltpu.PrefetchScalarGridSpec(
            num_scalar_prefetch=1,
            grid=(1,),
            in_specs=[any_spec] * len(cols),
            out_specs=any_spec,
            scratch_shapes=[pltpu.SemaphoreType.DMA((len(cols),))],
        ),
        cost_estimate=pl.CostEstimate(flops=0, bytes_accessed=2 * total * width * 2, transcendentals=0),
        name="place_rows",
    )(offsets, *[x for x, _ in pieces])


class Ring:
    def __init__(self, count):
        self.count = count
        self.order = ring_order(count)
        at = {d: i for i, d in enumerate(self.order)}
        self.table = [[self.order[(at[d] + k) % count] for k in range(count)] for d in range(count)]
        self.ahead = [(self.order[i], self.order[(i + 1) % count]) for i in range(count)]
        self.back = [(b, a) for a, b in self.ahead]

    def places(self):
        return jnp.asarray(self.table, jnp.int32)[lax.axis_index("dp")]

    def gather(self, x):
        half = self.count // 2
        mid = x.shape[1] // 2 // 128 * 128
        pieces = [(x, 0, 0)]
        f = b = x
        for s in range(1, half + 1):
            if s == half:
                f, b = f[:, :mid], b[:, mid:]
            f = lax.ppermute(f, "dp", self.ahead)
            b = lax.ppermute(b, "dp", self.back)
            pieces += [(f, 0, self.count - s), (b, mid if s == half else 0, s)]
        return pieces

    def assemble(self, pieces, places):
        offsets = jnp.stack([places[k] for _, _, k in pieces])
        return place([(x, c0) for x, c0, _ in pieces], offsets, self.count * pieces[0][0].shape[0])

    def scatter_sum(self, x, places):
        half = self.count // 2
        mid = x.shape[2] // 2 // 128 * 128

        def block(k):
            return lax.dynamic_index_in_dim(x, places[k % self.count], 0, keepdims=False)

        far = block(half)
        f, b = far[:, :mid], far[:, mid:]
        for s in range(half - 1, -1, -1):
            f = lax.ppermute(f, "dp", self.ahead).astype(f32)
            b = lax.ppermute(b, "dp", self.back).astype(f32)
            own_f, own_b = block(s).astype(f32), block(self.count - s).astype(f32)
            if s == half - 1:
                f = jnp.pad(f, ((0, 0), (0, x.shape[2] - mid)))
                b = jnp.pad(b, ((0, 0), (mid, 0)))
            if s:
                f = (own_f + f).astype(bf16)
                b = (own_b + b).astype(bf16)
        return block(0).astype(f32) + f + b


def xor_swap(x, axis, count, bit):
    return lax.ppermute(x, axis, [(i, i ^ bit) for i in range(count)])


def bits_of(count):
    return [1 << k for k in range(count.bit_length() - 1)]


def sum_all(x, axis, count):
    for bit in bits_of(count):
        x = x + xor_swap(x, axis, count, bit)
    return x


def gather_tensor(x, count, me):
    pieces = {0: x}
    for bit in reversed(bits_of(count)):
        for k in list(pieces):
            pieces[k ^ bit] = xor_swap(pieces[k], "tensor", count, bit)
    keys = list(pieces)
    offsets = me ^ jnp.asarray(keys, jnp.int32)
    return place([(pieces[k], 0) for k in keys], offsets, count * x.shape[0])


def scatter_tensor(x, count, me, out=f32):
    left = count
    for bit in bits_of(count):
        mine = (me // bit) % 2
        x = x.reshape((left // 2, 2) + x.shape[-2:])
        send = lax.dynamic_index_in_dim(x, 1 - mine, 1, keepdims=False)
        keep = lax.dynamic_index_in_dim(x, mine, 1, keepdims=False)
        got = xor_swap(send, "tensor", count, bit)
        left //= 2
        x = keep.astype(f32) + got.astype(f32)
        if left > 1:
            x = x.astype(bf16)
    return x[0].astype(out)


def after(x, *others):
    return lax.optimization_barrier((x,) + others)[0]


def body(
    n_dp,
    n_tensor,
    hidden_in,
    norm_gain,
    gate_value_weight,
    state_proj_weight,
    step_weight,
    conv_value_kernel,
    conv_value_bias,
    conv_state_kernel,
    conv_state_bias,
    step_bias,
    decay_log,
    skip_scale,
    gate_norm_gain,
    out_weight,
    out_cotangent,
    seq_lengths,
    seq_device,
    seq_offset,
):
    quarter = hidden_in.shape[0]
    heads = step_weight.shape[1]
    rows = gate_value_weight.shape[0]
    pad_heads = lambda x: jnp.pad(x, (0, 128 - heads))[None]
    me = lax.axis_index("tensor")
    ring = Ring(n_dp)
    places = ring.places()

    live_rows, seq_first = span_layout(seq_lengths, seq_device, seq_offset, lax.axis_index("dp"))
    row = me * quarter + jnp.arange(quarter, dtype=jnp.int32)
    local_live = jnp.sum(
        jnp.where((row // SPAN)[:, None] == jnp.arange(SEQ_DEV)[None, :], live_rows[None, :], 0), axis=1
    )
    local_mask = (row % SPAN < local_live).astype(f32)

    first_own = jnp.concatenate(
        [gate_value_weight[:, 1, :], state_proj_weight, jnp.pad(step_weight, ((0, 0), (0, 128 - heads)))],
        axis=1,
    )
    first_pieces = ring.gather(first_own)
    inv_rms = lax.rsqrt(jnp.mean(hidden_in * hidden_in, axis=-1) + EPSILON)
    scaled = hidden_in * inv_rms[:, None]
    normed_local = (scaled * norm_gain[None, :]).astype(bf16)
    normed = gather_tensor(normed_local, n_tensor, me)
    gate_own = after(gate_value_weight[:, 0, :], first_pieces[-3][0], first_pieces[-4][0])
    gate_pieces = ring.gather(gate_own)
    out_own = after(out_weight, gate_pieces[-3][0], gate_pieces[-4][0])
    out_pieces = ring.gather(out_own)
    back_local = (local_mask[:, None] * out_cotangent).astype(bf16)
    back_mix = gather_tensor(after(back_local, normed), n_tensor, me)

    conv_kernel = jnp.concatenate([conv_value_kernel, conv_state_kernel], axis=0).T
    conv_bias = jnp.concatenate([conv_value_bias, conv_state_bias])[None]
    e1 = (jnp.arange(128)[:, None] == jnp.arange(VW)[None, :] // HW).astype(bf16)
    ee = jnp.concatenate([e1, e1], axis=0)
    hh = jnp.concatenate([e1.T, e1.T], axis=0)
    sb, dl = pad_heads(step_bias), pad_heads(decay_log)
    skip = jnp.repeat(skip_scale, HW)[None]
    zeros = lambda *s: jnp.zeros(s, f32)

    first_w = ring.assemble(first_pieces, places)
    raw = contract(normed, first_w, 1, 0)
    chunks = TOK_DEV // Q
    n = chunks // PARTS
    state, tail = zeros(NS, VW), zeros(8, CW)
    y_parts, pre_parts, state_parts = [], [], []
    for i in range(PARTS):
        y0, pre, sp, state, tail = ssd_fwd(
            i * n, n, seq_first, raw, conv_kernel, conv_bias, sb, dl, ee, state, tail
        )
        y_parts.append(y0)
        pre_parts.append(pre)
        state_parts.append(sp)
    y0 = jnp.concatenate(y_parts, axis=0)
    values = jax.nn.silu(jnp.concatenate([p[:, :VW] for p in pre_parts], axis=0))
    ssd = y0 + skip * values

    gate_w = ring.assemble(gate_pieces, places)
    gate_raw = contract(normed, gate_w, 1, 0)
    gate_sig = jax.nn.sigmoid(gate_raw)
    gate = gate_raw * gate_sig
    gated = ssd * gate
    square = jnp.sum(gated * gated, axis=-1)
    square = sum_all(square.reshape(8, 128), "tensor", n_tensor).reshape(TOK_DEV)
    gate_inv = lax.rsqrt(square / E + EPSILON)
    unit = gated * gate_inv[:, None]
    normed_y = (unit * gate_norm_gain[None, :]).astype(bf16)
    out_grad = contract(back_mix, normed_y, 0, 0, bf16)
    out_w = ring.assemble(out_pieces, places)
    out_out = ring.scatter_sum(out_grad.reshape(n_dp, rows, VW), places)

    back_y = contract(back_mix, out_w, 1, 0)
    gain_grad = jnp.sum(back_y * unit, axis=0)
    weighted = back_y * gate_norm_gain[None, :]
    cross = jnp.sum(weighted * unit, axis=-1)
    cross = sum_all(cross.reshape(8, 128), "tensor", n_tensor).reshape(TOK_DEV)
    back_gated = gate_inv[:, None] * (weighted - unit * (cross / E)[:, None])
    back_gate = (back_gated * ssd * (gate_sig * (1.0 + gate_raw - gate))).astype(bf16)
    back_ssd = back_gated * gate

    gate_grad = contract(normed, back_gate, 0, 0, bf16)
    gate_out = ring.scatter_sum(gate_grad.reshape(n_dp, rows, VW), places)
    mixer = contract(normed_y, out_w, 1, 1, bf16)
    mixer_rows = scatter_tensor(mixer.reshape(n_tensor, quarter, D), n_tensor, me)
    output = hidden_in + local_mask[:, None] * mixer_rows

    ds, sn, hd, acc, acs = zeros(NS, VW), zeros(NS, VW), zeros(8, CW), zeros(8, CW), zeros(8, 128)
    back_parts = []
    for i in reversed(range(PARTS)):
        out, ds, sn, hd, acc, acs = ssd_bwd(
            i * n, n, chunks, seq_first, raw, pre_parts[i], y_parts[i], back_ssd, state_parts[i],
            conv_kernel, sb, dl, skip, ee, hh, ds, sn, hd, acc, acs,
        )
        back_parts.insert(0, out)
    back_first = jnp.concatenate(back_parts, axis=0)

    value_grad = contract(normed, back_first[:, :VW], 0, 0, bf16)
    value_out = ring.scatter_sum(value_grad.reshape(n_dp, rows, VW), places)
    state_grad = contract(normed, back_first[:, VW:CW], 0, 0, bf16)
    step_grad = contract(back_first[:, CW:], normed, 0, 0, bf16)[:16]
    share = rows // n_tensor
    state_grad = state_grad.reshape(n_dp, n_tensor, share, 2 * NS).transpose(1, 0, 2, 3)
    state_grad = scatter_tensor(
        state_grad.reshape(n_tensor, n_dp * share, 2 * NS), n_tensor, me, bf16
    ).reshape(n_dp, share, 2 * NS)
    step_grad = step_grad.reshape(16, n_dp, rows).transpose(1, 0, 2)
    step_grad = jnp.pad(step_grad, ((0, 0), (0, 0), (0, 2 * NS - rows)))
    small_out = ring.scatter_sum(jnp.concatenate([state_grad, step_grad], axis=1), places)

    back_normed = contract(back_first, first_w, 1, 1) + contract(back_gate, gate_w, 1, 1)
    norm_grad = jnp.sum(back_normed * normed.astype(f32), axis=0) / norm_gain
    back_rows = scatter_tensor(
        back_normed.astype(bf16).reshape(n_tensor, quarter, D), n_tensor, me
    )
    back_scaled = back_rows * norm_gain[None, :]
    hidden_gradient = out_cotangent + inv_rms[:, None] * (
        back_scaled - scaled * jnp.mean(back_scaled * scaled, axis=-1)[:, None]
    )

    shared = jnp.concatenate([acc[:5, VW:], norm_grad.reshape(6, 256), zeros(5, 256)], axis=0)
    shared = sum_all(shared, "tensor", n_tensor)
    own = jnp.concatenate(
        [acc[:6], jnp.pad(jnp.concatenate([gain_grad, acs[0], acs[1]]), (0, 0))[None], zeros(1, CW)], axis=0
    )
    small = jnp.concatenate([own, shared.reshape(4, CW)], axis=0)
    small = sum_all(small, "dp", n_dp)
    shared = small[8:].reshape(16, 256)
    index = lax.axis_index("dp") * n_tensor + me
    all_count = n_dp * n_tensor
    kern_share = 2 * NS // all_count
    state_kernel_out = lax.dynamic_slice(shared, (0, index * kern_share), (5, kern_share))
    norm_out = lax.dynamic_slice(shared[5:11].reshape(D), (index * (D // all_count),), (D // all_count,))
    return (
        output,
        hidden_gradient,
        norm_out,
        jnp.stack([gate_out, value_out], axis=1),
        small_out[:share],
        small_out[share:, :rows].T[:, :heads],
        small[:4, :VW].T,
        small[4, :VW],
        state_kernel_out[:4].T,
        state_kernel_out[4],
        small[6, VW + 128 : VW + 128 + heads],
        small[6, VW : VW + heads],
        jnp.sum(small[5, :VW].reshape(heads, HW), axis=1),
        small[6, :VW],
        out_out,
    )


def solution(mesh):
    in_specs = (
        P(("dp", "tensor"), None),
        P(),
        P("dp", None, "tensor"),
        P("dp", None),
        P("dp", "tensor"),
        P("tensor", None),
        P("tensor"),
        P(),
        P(),
        P("tensor"),
        P("tensor"),
        P("tensor"),
        P("tensor"),
        P("dp", "tensor"),
        P(("dp", "tensor"), None),
        P(),
        P(),
        P(),
    )
    out_specs = (
        P(("dp", "tensor"), None),
        P(("dp", "tensor"), None),
        P(("dp", "tensor")),
        P("dp", None, "tensor"),
        P(("dp", "tensor"), None),
        P("dp", "tensor"),
        P("tensor", None),
        P("tensor"),
        P(("dp", "tensor"), None),
        P(("dp", "tensor")),
        P("tensor"),
        P("tensor"),
        P("tensor"),
        P("tensor"),
        P("dp", "tensor"),
    )
    return jax.shard_map(
        partial(body, mesh.shape["dp"], mesh.shape["tensor"]),
        mesh=mesh,
        in_specs=in_specs,
        out_specs=out_specs,
        check_vma=False,
    )
```

time: 1320 us -> 848 us (0.64)
  Pallas kernels: 0 us -> 486 us
  waiting for transfers between devices: 569 us -> 124 us
  local copies, waits for them, and re-layouts: 321 us -> 49.8 us
  blocking collectives: 157 us -> 0 us
  matrix products: 158 us -> 53.3 us
  starting transfers between devices: 0.41 us -> 78.8 us
  other arithmetic: 82.4 us -> 29.3 us
    pallas_call x0 -> x9, Pallas kernels: none -> 486 us  [the longest x5 450 us: place(): pl.pallas_call(partial(place_kernel, cols, rows), out_shape=jax.ShapeDtyp...]
    unnamed x13 -> x0, waiting for transfers between devices: 368 us -> none
    reduce_scatter x3 -> x0, waiting for transfers between devices: 175 us -> none  [the longest x1 99.2 us: body(): lax.psum_scatter(out_weight_grad, 'dp', scatter_dimension=0, tiled=True)]
    dynamic_update_slice x32 -> x0, local copies, waits for them, and re-layouts: 161 us -> none  [ssd_scan(): _, outputs = lax.scan(jax.checkpoint(span_step), zero_state, scanned)]
    ppermute x0 -> x77, waiting for transfers between devices: none -> 124 us  [the longest x16 47.2 us: scatter_sum(): b = lax.ppermute(b, 'dp', self.back).astype(f32)]
    dot_general x50 -> x0, matrix products: 117 us -> none  [the longest x12 54.7 us: span_step(): jnp.einsum('tsh,shp->thp', weights, value_blk, precision=HIGHEST)]
    ppermute x0 -> x77, starting transfers between devices: none -> 78.8 us  [the longest x16 26.7 us: scatter_sum(): f = lax.ppermute(f, 'dp', self.ahead).astype(f32)]
    all_gather x2 -> x0, blocking collectives: 66.7 us -> none  [the longest x1 35.8 us: body(): lax.all_gather(state_proj_weight, 'dp', axis=0, tiled=True)]
  transfers between devices with their start and end apart: 10 -> 77, of which waited for: 7 -> 32; matrix products, arithmetic and copies ran while one was open for 20% -> 14% of each run, Pallas kernels for 0% -> 58%
where the time goes in v1:
time: 848 us; the launch traced here: 839 us
  Pallas kernels  486 us (57%)
  waiting for transfers between devices  124 us (15%)
  starting transfers between devices  78.8 us (9%)
  matrix products  53.3 us (6%)
  local copies, waits for them, and re-layouts  49.8 us (6%)
  other arithmetic  29.3 us (3%)
  between operations  18.1 us (2%)
    pallas_call x5, Pallas kernels, place(): pl.pallas_call(partial(place_kernel, cols, rows), out_shape=jax.ShapeDtyp...  450 us
    dot_general x11, matrix products, contract(): lax.dot_general(left, right, (((left_dim,), (right_dim,)), ((), ())), pre...  53.3 us
    ppermute x16, waiting for transfers between devices, scatter_sum(): b = lax.ppermute(b, 'dp', self.back).astype(f32)  47.2 us
    ppermute x21, waiting for transfers between devices, xor_swap(): return lax.ppermute(x, axis, [(i, i ^ bit) for i in range(count)])  36.6 us
    ppermute x16, starting transfers between devices, scatter_sum(): f = lax.ppermute(f, 'dp', self.ahead).astype(f32)  26.7 us
    pallas_call x2, Pallas kernels, ssd_bwd(): pl.pallas_call(partial(bwd_kernel, c0, nc, nall), out_shape=(sd((nc * Q,...  25.2 us
    ppermute x12, waiting for transfers between devices, gather(): b = lax.ppermute(b, 'dp', self.back)  24.3 us
  transfers between devices with their start and end apart: 77, of which 32 were waited for; matrix products, arithmetic and copies ran while one was open for 14% of the time, Pallas kernels for 58%

profile of v1, /device:TPU:0, one launch (start us, length us, event | category | flops | bytes accessed | tf_op | source)
XLA Modules:
  0.0 838.8 jit_solution(18065772808625429793)
XLA Ops:
  0.7 3.2 fusion.58
  4.9 3.0 collective-permute-start.4
  9.3 2.0 collective-permute-start
  11.6 6.8 collective-permute-done.4.refs_2_
  22.3 7.7 collective-permute-done.6.refs_4_
  33.1 7.5 collective-permute-done.8.refs_6_
  44.6 4.5 collective-permute-done.11.refs_1_
  54.5 2.8 collective-permute-done.13.refs_3_
  57.9 2.1 collective-permute-done.14.refs_4_
  62.2 6.5 stack.14.off_ref
  72.1 97.1 %place_rows.5 = bf16[1024,1536]{1,0:T(8,128)(2,1)} custom-call(s32[4]{0:T(128)} %broadcast_xor_fusion.off_ref, bf16[256,1536]{1,0:T(8,128)(2,1)} %multiply_convert_fusion.3.refs_0_, bf16[256,1536]{1,0:T(8,128)(2,1)} %collective-permute-done.refs_1_, bf16[256,1536]{1,0:T(8,128)(2,1)} %collective-permute-done.1.refs_2_, bf16[256,1536]{1,0:T(8,128)(2,1)} %copy-done.36), custom_call_target="tpu_custom_call" | custom-call | bytes 6291456 | tf_op jit(solution)/shard_map/place_rows/pallas_call | solution.py:265
  170.5 109.1 %place_rows.6 = bf16[1536,1152]{1,0:T(8,128)(2,1)} custom-call(s32[9]{0:T(128)} %stack.14.off_ref, bf16[192,1152]{1,0:T(8,128)(2,1)} %fusion.33.refs_0_, bf16[192,1152]{1,0:T(8,128)(2,1)} %collective-permute-done.3.refs_1_, bf16[192,1152]{1,0:T(8,128)(2,1)} %collective-permute-done.4.refs_2_, bf16[192,1152]{1,0:T(8,128)(2,1)} %copy-done.40, ...), custom_call_target="tpu_custom_call" | custom-call | bytes 7077888 | tf_op jit(solution)/shard_map/place_rows/pallas_call | solution.py:265
  283.8 7.2 fusion.64.raw_ref
  291.1 5.0 ssd_forward_0.1
  298.3 5.7 ssd_forward_4.1
  305.4 1.9 slice.235
  308.7 73.3 %place_rows.7 = bf16[1536,768]{1,0:T(8,128)(2,1)} custom-call(s32[9]{0:T(128)} %stack.14.off_ref, bf16[192,768]{1,0:T(8,128)(2,1)} %bitcast.249, bf16[192,768]{1,0:T(8,128)(2,1)} %copy-done.42, bf16[192,768]{1,0:T(8,128)(2,1)} %copy-done.43, bf16[192,768]{1,0:T(8,128)(2,1)} %collective-permute-done.13.refs_3_, ...), custom_call_target="tpu_custom_call" | custom-call | bytes 4718592 | tf_op jit(solution)/shard_map/place_rows/pallas_call | solution.py:265
  384.3 10.3 %multiply_reduce_fusion.3 = (f32[1024]{0:T(1024)S(1)}, f32[1024,768]{1,0:T(8,128)}, f32[1024,768]{1,0:T(8,128)}) fusion(f32[512,768]{1,0:T(8,128)} %slice.236, f32[512,768]{1,0:T(8,128)} %slice.235, f32[768]{0:T(1024)S(1)} %copy-done.55, f32[512,768]{1,0:T(8,128)} %copy-done.5, f32[512,768]{1,0:T(8,128)} %copy-done.3, bf16[1024,1536]{1,0:T(8,128)(2,1)} %place_rows.5, ...), kind=kOutput, calls=%fused_computation.17 | convolution fusion | flops 2427714560 | bytes 18095104 | tf_op jit(solution)/shard_map/dot_general | solution.py:221
  418.7 97.1 %place_rows.9 = bf16[1024,1536]{1,0:T(8,128)(2,1)} custom-call(s32[4]{0:T(128)} %broadcast_xor_fusion.off_ref, bf16[256,1536]{1,0:T(8,128)(2,1)} %multiply_convert_fusion.2.refs_0_, bf16[256,1536]{1,0:T(8,128)(2,1)} %collective-permute-done.31.refs_1_, bf16[256,1536]{1,0:T(8,128)(2,1)} %collective-permute-done.32.refs_2_, ...), custom_call_target="tpu_custom_call" | custom-call | bytes 6291456 | tf_op jit(solution)/shard_map/place_rows/pallas_call | solution.py:265
  515.9 5.7 convolution_convert_fusion.1
  526.4 73.3 %place_rows.8 = bf16[1536,768]{1,0:T(8,128)(2,1)} custom-call(s32[9]{0:T(128)} %stack.14.off_ref, bf16[192,768]{1,0:T(8,128)(2,1)} %refs_0_, bf16[192,768]{1,0:T(8,128)(2,1)} %collective-permute-done.21.refs_1_, bf16[192,768]{1,0:T(8,128)(2,1)} %collective-permute-done.22.refs_2_, bf16[192,768]{1,0:T(8,128)(2,1)} %collective-permute-done.23.refs_3_, ...), custom_call_target="tpu_custom_call" | custom-call | bytes 4718592 | tf_op jit(solution)/shard_map/place_rows/pallas_call | solution.py:265
  599.7 6.6 multiply_reduce_fusion.1
  606.5 3.2 convolution_convert_fusion
  613.5 4.3 fusion.5
  617.8 12.3 %ssd_backward_4.1 = (bf16[512,1152]{1,0:T(8,128)(2,1)S(1)}, f32[128,768]{1,0:T(8,128)S(1)}, f32[128,768]{1,0:T(8,128)S(1)}, f32[8,1024]{1,0:T(8,128)S(1)}, f32[8,1024]{1,0:T(8,128)S(1)}, /*index=5*/f32[8,128]{1,0:T(8,128)S(1)}) custom-call(s32[4]{0:T(128)S(1)} %convert_element_type.455.first_ref, f32[1024,1152]{1,0:T(8,128)} %copy-done, ...), custom_call_target="tpu_custom_call" | custom-call | flops 1500000000 | bytes 12000000 | tf_op jit(solution)/shard_map/ssd_backward_4/pallas_call | solution.py:198
  630.1 13.0 %ssd_backward_0.1 = (bf16[512,1152]{1,0:T(8,128)(2,1)S(1)}, f32[128,768]{1,0:T(8,128)}, f32[128,768]{1,0:T(8,128)}, f32[8,1024]{1,0:T(8,128)}, f32[8,1024]{1,0:T(8,128)S(1)}, /*index=5*/f32[8,128]{1,0:T(8,128)S(1)}) custom-call(s32[4]{0:T(128)S(1)} %convert_element_type.455.first_ref, f32[1024,1152]{1,0:T(8,128)} %copy-done, ...), custom_call_target="tpu_custom_call" | custom-call | flops 1500000000 | bytes 12000000 | tf_op jit(solution)/shard_map/ssd_backward_0/pallas_call | solution.py:198
  646.6 3.0 convolution_convert_fusion.2
  649.6 3.2 convolution_convert_fusion.3
  652.9 4.6 fusion.65
  660.1 7.9 multiply_reduce_fusion
  668.1 2.7 dynamic-slice_bitcast_fusion
  672.4 2.2 collective-permute-done.39
  676.4 2.6 collective-permute-done.40
  683.0 1.8 fusion.11
  687.4 1.8 fusion.26
  689.2 2.0 collective-permute-start.42
  691.2 1.7 fusion.18
  692.9 3.0 collective-permute-done.42
  695.9 3.0 collective-permute-start.44
  712.1 4.3 collective-permute-done.60
  718.2 3.1 collective-permute-start.61
  722.4 2.0 collective-permute-done.61
  725.8 2.5 collective-permute-start.62
  729.5 2.4 collective-permute-done.62
  731.9 2.1 collective-permute-start.63
  734.1 1.8 collective-permute-done.65
  740.4 2.5 collective-permute-done.66
  742.9 2.0 collective-permute-start.53
  746.2 2.7 collective-permute-done.67
  751.0 1.8 collective-permute-done.53
  755.1 3.1 collective-permute-done.68
  761.1 7.0 collective-permute-done.48
  768.5 5.9 collective-permute-done.56
  774.8 5.9 collective-permute-done.75
  781.1 6.0 collective-permute-done.49
  787.4 5.9 collective-permute-done.57
  793.4 1.7 collective-permute-start.46
  800.1 1.8 fusion.1
  804.6 2.6 collective-permute-done.50
  807.4 3.0 collective-permute-done.58
  810.7 1.9 copy.64
  812.6 10.3 %collective-permute-done.37 = bf16[1,256,1536]{2,1,0:T(8,128)(2,1)S(1)} collective-permute-done((bf16[1,256,1536]{2,1,0:T(8,128)(2,1)S(1)}, bf16[1,256,1536]{2,1,0:T(8,128)(2,1)S(1)}, u32[]{:S(2)}, u32[]{:S(2)}) %collective-permute-start.37) | collective-permute-done | bytes 786464 | tf_op jit(solution)/shard_map/ppermute | solution.py:332
  823.5 12.5 %collective-permute-done.30 = bf16[1,256,1536]{2,1,0:T(8,128)(2,1)S(1)} collective-permute-done((bf16[1,256,1536]{2,1,0:T(8,128)(2,1)S(1)}, bf16[1,256,1536]{2,1,0:T(8,128)(2,1)S(1)}, u32[]{:S(2)}, u32[]{:S(2)}) %collective-permute-start.30) | collective-permute-done | bytes 786464 | tf_op jit(solution)/shard_map/ppermute | solution.py:332
  836.0 2.3 multiply_add_fusion
  (385 shorter events, 113.3 us)
Async XLA Ops:
  4.9 13.5 %collective-permute-start.4 = (bf16[192,1152]{1,0:T(8,128)(2,1)}, bf16[192,1152]{1,0:T(8,128)(2,1)}, u32[]{:S(2)}, u32[]{:S(2)}) collective-permute-start(bf16[192,1152]{1,0:T(8,128)(2,1)} %fusion.33.refs_0_), channel_id=1, source_target_pairs={{8,0},{16,8},{24,16},{28,24},{20,28},{12,20},{4,12},{0,4},{9,1},{1... | collective-permute-start | bytes 1327112 | tf_op jit(solution)/shard_map/ppermute | solution.py:301
  7.9 12.2 %collective-permute-start.3 = (bf16[192,1152]{1,0:T(8,128)(2,1)}, bf16[192,1152]{1,0:T(8,128)(2,1)}, u32[]{:S(2)}, u32[]{:S(2)}) collective-permute-start(bf16[192,1152]{1,0:T(8,128)(2,1)} %fusion.33.refs_0_), channel_id=1, source_target_pairs={{0,8},{8,16},{16,24},{24,28},{28,20},{20,12},{12,4},{4,0},{1,9},{9... | collective-permute-start | bytes 1327112 | tf_op jit(solution)/shard_map/ppermute | solution.py:300
  9.3 35.1 %collective-permute-start = (bf16[256,1536]{1,0:T(8,128)(2,1)}, bf16[256,1536]{1,0:T(8,128)(2,1)}, u32[]{:S(2)}, u32[]{:S(2)}) collective-permute-start(bf16[256,1536]{1,0:T(8,128)(2,1)} %multiply_convert_fusion.3.refs_0_), channel_id=1, source_target_pairs={{0,2},{1,3},{2,0},{3,1},{4,6},{5,7},{6,4},{7,5},{8,10},{9,11},{10,... | collective-permute-start | bytes 2359304 | tf_op jit(solution)/shard_map/ppermute | solution.py:332
  11.3 58.1 %collective-permute-start.1 = (bf16[256,1536]{1,0:T(8,128)(2,1)}, bf16[256,1536]{1,0:T(8,128)(2,1)}, u32[]{:S(2)}, u32[]{:S(2)}) collective-permute-start(bf16[256,1536]{1,0:T(8,128)(2,1)} %multiply_convert_fusion.3.refs_0_), channel_id=1, source_target_pairs={{0,1},{1,0},{2,3},{3,2},{4,5},{5,4},{6,7},{7,6},{8,9},{9,8},{10,11... | collective-permute-start | bytes 2359304 | tf_op jit(solution)/shard_map/ppermute | solution.py:332
  18.4 11.6 %collective-permute-start.6 = (bf16[192,1152]{1,0:T(8,128)(2,1)}, bf16[192,1152]{1,0:T(8,128)(2,1)S(1)}, u32[]{:S(2)}, u32[]{:S(2)}) collective-permute-start(bf16[192,1152]{1,0:T(8,128)(2,1)} %collective-permute-done.4.refs_2_), channel_id=1, source_target_pairs={{8,0},{16,8},{24,16},{28,24},{20,28},{12,20},{4,12},{0,4},{9,1},{1... | collective-permute-start | bytes 1327112 | tf_op jit(solution)/shard_map/ppermute | solution.py:301
  20.1 11.2 %collective-permute-start.5 = (bf16[192,1152]{1,0:T(8,128)(2,1)}, bf16[192,1152]{1,0:T(8,128)(2,1)S(1)}, u32[]{:S(2)}, u32[]{:S(2)}) collective-permute-start(bf16[192,1152]{1,0:T(8,128)(2,1)} %collective-permute-done.3.refs_1_), channel_id=1, source_target_pairs={{0,8},{8,16},{16,24},{24,28},{28,20},{20,12},{12,4},{4,0},{1,9},{9... | collective-permute-start | bytes 1327112 | tf_op jit(solution)/shard_map/ppermute | solution.py:300
  30.0 10.5 %collective-permute-start.8 = (bf16[192,1152]{1,0:T(8,128)(2,1)S(1)}, bf16[192,1152]{1,0:T(8,128)(2,1)S(1)}, u32[]{:S(2)}, u32[]{:S(2)}) collective-permute-start(bf16[192,1152]{1,0:T(8,128)(2,1)S(1)} %collective-permute-done.6.refs_4_), channel_id=1, source_target_pairs={{8,0},{16,8},{24,16},{28,24},{20,28},{12,20},{4,12},{0,4},{9,1},{1... | collective-permute-start | bytes 1327112 | tf_op jit(solution)/shard_map/ppermute | solution.py:301
  31.4 10.3 %collective-permute-start.7 = (bf16[192,1152]{1,0:T(8,128)(2,1)S(1)}, bf16[192,1152]{1,0:T(8,128)(2,1)S(1)}, u32[]{:S(2)}, u32[]{:S(2)}) collective-permute-start(bf16[192,1152]{1,0:T(8,128)(2,1)S(1)} %collective-permute-done.5.refs_3_), channel_id=1, source_target_pairs={{0,8},{8,16},{16,24},{24,28},{28,20},{20,12},{12,4},{4,0},{1,9},{9... | collective-permute-start | bytes 1327112 | tf_op jit(solution)/shard_map/ppermute | solution.py:300
  41.7 7.3 collective-permute-start.11
  42.4 7.6 collective-permute-start.12
  44.4 26.8 %collective-permute-start.2 = (bf16[256,1536]{1,0:T(8,128)(2,1)}, bf16[256,1536]{1,0:T(8,128)(2,1)S(1)}, u32[]{:S(2)}, u32[]{:S(2)}) collective-permute-start(bf16[256,1536]{1,0:T(8,128)(2,1)} %collective-permute-done.refs_1_), channel_id=1, source_target_pairs={{0,1},{1,0},{2,3},{3,2},{4,5},{5,4},{6,7},{7,6},{8,9},{9,8},{10,11... | collective-permute-start | bytes 2359304 | tf_op jit(solution)/shard_map/ppermute | solution.py:332
  49.0 8.2 collective-permute-start.13
  50.0 10.0 %collective-permute-start.14 = (bf16[192,768]{1,0:T(8,128)(2,1)S(1)}, bf16[192,768]{1,0:T(8,128)(2,1)}, u32[]{:S(2)}, u32[]{:S(2)}) collective-permute-start(bf16[192,768]{1,0:T(8,128)(2,1)S(1)} %collective-permute-done.12.refs_2_), channel_id=1, source_target_pairs={{8,0},{16,8},{24,16},{28,24},{20,28},{12,20},{4,12},{0,4},{9,1},{1... | collective-permute-start | bytes 884744 | tf_op jit(solution)/shard_map/ppermute | solution.py:301
  52.9 117.6 %collective-permute-start.10 = (bf16[192,640]{1,0:T(8,128)(2,1)}, bf16[192,640]{1,0:T(8,128)(2,1)}, u32[]{:S(2)}, u32[]{:S(2)}) collective-permute-start(bf16[192,640]{1,0:T(8,128)(2,1)} %slice.272), channel_id=1, source_target_pairs={{8,0},{16,8},{24,16},{28,24},{20,28},{12,20},{4,12},{0,4},{9,1},{1... | collective-permute-start | bytes 737288 | tf_op jit(solution)/shard_map/ppermute | solution.py:301
  57.3 222.3 %collective-permute-start.15 = (bf16[192,768]{1,0:T(8,128)(2,1)}, bf16[192,768]{1,0:T(8,128)(2,1)S(1)}, u32[]{:S(2)}, u32[]{:S(2)}) collective-permute-start(bf16[192,768]{1,0:T(8,128)(2,1)} %collective-permute-done.13.refs_3_), channel_id=1, source_target_pairs={{0,8},{8,16},{16,24},{24,28},{28,20},{20,12},{12,4},{4,0},{1,9},{9... | collective-permute-start | bytes 884744 | tf_op jit(solution)/shard_map/ppermute | solution.py:300
  60.0 219.5 %collective-permute-start.16 = (bf16[192,768]{1,0:T(8,128)(2,1)}, bf16[192,768]{1,0:T(8,128)(2,1)S(1)}, u32[]{:S(2)}, u32[]{:S(2)}) collective-permute-start(bf16[192,768]{1,0:T(8,128)(2,1)} %collective-permute-done.14.refs_4_), channel_id=1, source_target_pairs={{8,0},{16,8},{24,16},{28,24},{20,28},{12,20},{4,12},{0,4},{9,1},{1... | collective-permute-start | bytes 884744 | tf_op jit(solution)/shard_map/ppermute | solution.py:301
  69.4 101.1 %collective-permute-start.9 = (bf16[192,512]{1,0:T(8,128)(2,1)}, bf16[192,512]{1,0:T(8,128)(2,1)}, u32[]{:S(2)}, u32[]{:S(2)}) collective-permute-start(bf16[192,512]{1,0:T(8,128)(2,1)} %slice.271), channel_id=1, source_target_pairs={{0,8},{8,16},{16,24},{24,28},{28,20},{20,12},{12,4},{4,0},{1,9},{9... | collective-permute-start | bytes 589832 | tf_op jit(solution)/shard_map/ppermute | solution.py:300
  169.2 212.8 %collective-permute-start.31 = (bf16[256,1536]{1,0:T(8,128)(2,1)}, bf16[256,1536]{1,0:T(8,128)(2,1)}, u32[]{:S(2)}, u32[]{:S(2)}) collective-permute-start(bf16[256,1536]{1,0:T(8,128)(2,1)} %multiply_convert_fusion.2.refs_0_), channel_id=1, source_target_pairs={{0,2},{1,3},{2,0},{3,1},{4,6},{5,7},{6,4},{7,5},{8,10},{9,11},{10,... | collective-permute-start | bytes 2359304 | tf_op jit(solution)/shard_map/ppermute | solution.py:332
  279.6 102.5 %collective-permute-start.21 = (bf16[192,768]{1,0:T(8,128)(2,1)}, bf16[192,768]{1,0:T(8,128)(2,1)}, u32[]{:S(2)}, u32[]{:S(2)}) collective-permute-start(bf16[192,768]{1,0:T(8,128)(2,1)} %refs_0_), channel_id=1, source_target_pairs={{0,8},{8,16},{16,24},{24,28},{28,20},{20,12},{12,4},{4,0},{1,9},{9... | collective-permute-start | bytes 884744 | tf_op jit(solution)/shard_map/ppermute | solution.py:300
  281.2 102.5 %collective-permute-start.22 = (bf16[192,768]{1,0:T(8,128)(2,1)}, bf16[192,768]{1,0:T(8,128)(2,1)}, u32[]{:S(2)}, u32[]{:S(2)}) collective-permute-start(bf16[192,768]{1,0:T(8,128)(2,1)} %refs_0_), channel_id=1, source_target_pairs={{8,0},{16,8},{24,16},{28,24},{20,28},{12,20},{4,12},{0,4},{9,1},{1... | collective-permute-start | bytes 884744 | tf_op jit(solution)/shard_map/ppermute | solution.py:301
  281.7 25.7 %collective-permute-start.17 = (bf16[192,384]{1,0:T(8,128)(2,1)S(1)}, bf16[192,384]{1,0:T(8,128)(2,1)S(1)}, u32[]{:S(2)}, u32[]{:S(2)}) collective-permute-start(bf16[192,384]{1,0:T(8,128)(2,1)S(1)} %slice.273), channel_id=1, source_target_pairs={{0,8},{8,16},{16,24},{24,28},{28,20},{20,12},{12,4},{4,0},{1,9},{9... | collective-permute-start | bytes 442376 | tf_op jit(solution)/shard_map/ppermute | solution.py:300
  283.3 24.1 %collective-permute-start.18 = (bf16[192,384]{1,0:T(8,128)(2,1)S(1)}, bf16[192,384]{1,0:T(8,128)(2,1)S(1)}, u32[]{:S(2)}, u32[]{:S(2)}) collective-permute-start(bf16[192,384]{1,0:T(8,128)(2,1)S(1)} %slice.274), channel_id=1, source_target_pairs={{8,0},{16,8},{24,16},{28,24},{20,28},{12,20},{4,12},{0,4},{9,1},{1... | collective-permute-start | bytes 442376 | tf_op jit(solution)/shard_map/ppermute | solution.py:301
  307.4 111.4 %collective-permute-start.32 = (bf16[256,1536]{1,0:T(8,128)(2,1)}, bf16[256,1536]{1,0:T(8,128)(2,1)}, u32[]{:S(2)}, u32[]{:S(2)}) collective-permute-start(bf16[256,1536]{1,0:T(8,128)(2,1)} %multiply_convert_fusion.2.refs_0_), channel_id=1, source_target_pairs={{0,1},{1,0},{2,3},{3,2},{4,5},{5,4},{6,7},{7,6},{8,9},{9,8},{10,11... | collective-permute-start | bytes 2359304 | tf_op jit(solution)/shard_map/ppermute | solution.py:332
  382.0 36.7 %collective-permute-start.33 = (bf16[256,1536]{1,0:T(8,128)(2,1)}, bf16[256,1536]{1,0:T(8,128)(2,1)}, u32[]{:S(2)}, u32[]{:S(2)}) collective-permute-start(bf16[256,1536]{1,0:T(8,128)(2,1)} %collective-permute-done.31.refs_1_), channel_id=1, source_target_pairs={{0,1},{1,0},{2,3},{3,2},{4,5},{5,4},{6,7},{7,6},{8,9},{9,8},{10,11... | collective-permute-start | bytes 2359304 | tf_op jit(solution)/shard_map/ppermute | solution.py:332
  382.1 19.1 %collective-permute-start.23 = (bf16[192,768]{1,0:T(8,128)(2,1)}, bf16[192,768]{1,0:T(8,128)(2,1)}, u32[]{:S(2)}, u32[]{:S(2)}) collective-permute-start(bf16[192,768]{1,0:T(8,128)(2,1)} %collective-permute-done.21.refs_1_), channel_id=1, source_target_pairs={{0,8},{8,16},{16,24},{24,28},{28,20},{20,12},{12,4},{4,0},{1,9},{9... | collective-permute-start | bytes 884744 | tf_op jit(solution)/shard_map/ppermute | solution.py:300
  383.7 19.1 %collective-permute-start.24 = (bf16[192,768]{1,0:T(8,128)(2,1)}, bf16[192,768]{1,0:T(8,128)(2,1)}, u32[]{:S(2)}, u32[]{:S(2)}) collective-permute-start(bf16[192,768]{1,0:T(8,128)(2,1)} %collective-permute-done.22.refs_2_), channel_id=1, source_target_pairs={{8,0},{16,8},{24,16},{28,24},{20,28},{12,20},{4,12},{0,4},{9,1},{1... | collective-permute-start | bytes 884744 | tf_op jit(solution)/shard_map/ppermute | solution.py:301
  394.7 8.6 %collective-permute-start.19 = (f32[8,128]{1,0:T(8,128)S(1)}, f32[8,128]{1,0:T(8,128)S(1)}, u32[]{:S(2)}, u32[]{:S(2)}) collective-permute-start(f32[8,128]{1,0:T(8,128)S(1)} %bitcast.257), channel_id=1, source_target_pairs={{0,1},{1,0},{2,3},{3,2},{4,5},{5,4},{6,7},{7,6},{8,9},{9,8},{10,11... | collective-permute-start | bytes 12296 | tf_op jit(solution)/shard_map/ppermute | solution.py:332
  401.2 12.3 %collective-permute-start.25 = (bf16[192,768]{1,0:T(8,128)(2,1)}, bf16[192,768]{1,0:T(8,128)(2,1)}, u32[]{:S(2)}, u32[]{:S(2)}) collective-permute-start(bf16[192,768]{1,0:T(8,128)(2,1)} %collective-permute-done.23.refs_3_), channel_id=1, source_target_pairs={{0,8},{8,16},{16,24},{24,28},{28,20},{20,12},{12,4},{4,0},{1,9},{9... | collective-permute-start | bytes 884744 | tf_op jit(solution)/shard_map/ppermute | solution.py:300
  402.8 13.5 %collective-permute-start.26 = (bf16[192,768]{1,0:T(8,128)(2,1)}, bf16[192,768]{1,0:T(8,128)(2,1)}, u32[]{:S(2)}, u32[]{:S(2)}) collective-permute-start(bf16[192,768]{1,0:T(8,128)(2,1)} %collective-permute-done.24.refs_4_), channel_id=1, source_target_pairs={{8,0},{16,8},{24,16},{28,24},{20,28},{12,20},{4,12},{0,4},{9,1},{1... | collective-permute-start | bytes 884744 | tf_op jit(solution)/shard_map/ppermute | solution.py:301
  403.3 10.2 %collective-permute-start.20 = (f32[8,128]{1,0:T(8,128)S(1)}, f32[8,128]{1,0:T(8,128)S(1)}, u32[]{:S(2)}, u32[]{:S(2)}) collective-permute-start(f32[8,128]{1,0:T(8,128)S(1)} %bitcast_add_fusion.1), channel_id=1, source_target_pairs={{0,2},{1,3},{2,0},{3,1},{4,6},{5,7},{6,4},{7,5},{8,10},{9,11},{10,... | collective-permute-start | bytes 12296 | tf_op jit(solution)/shard_map/ppermute | solution.py:332
  415.1 110.6 %collective-permute-start.27 = (bf16[192,384]{1,0:T(8,128)(2,1)}, bf16[192,384]{1,0:T(8,128)(2,1)S(1)}, u32[]{:S(2)}, u32[]{:S(2)}) collective-permute-start(bf16[192,384]{1,0:T(8,128)(2,1)} %slice.275), channel_id=1, source_target_pairs={{0,8},{8,16},{16,24},{24,28},{28,20},{20,12},{12,4},{4,0},{1,9},{9... | collective-permute-start | bytes 442376 | tf_op jit(solution)/shard_map/ppermute | solution.py:300
  417.9 107.8 %collective-permute-start.28 = (bf16[192,384]{1,0:T(8,128)(2,1)}, bf16[192,384]{1,0:T(8,128)(2,1)}, u32[]{:S(2)}, u32[]{:S(2)}) collective-permute-start(bf16[192,384]{1,0:T(8,128)(2,1)} %slice.276), channel_id=1, source_target_pairs={{8,0},{16,8},{24,16},{28,24},{20,28},{12,20},{4,12},{0,4},{9,1},{1... | collective-permute-start | bytes 442376 | tf_op jit(solution)/shard_map/ppermute | solution.py:301
  523.7 157.6 %collective-permute-start.69 = (bf16[192,384]{1,0:T(8,128)(2,1)}, bf16[192,384]{1,0:T(8,128)(2,1)}, u32[]{:S(2)}, u32[]{:S(2)}) collective-permute-start(bf16[192,384]{1,0:T(8,128)(2,1)} %get-tuple-element.106), channel_id=1, source_target_pairs={{0,8},{8,16},{16,24},{24,28},{28,20},{20,12},{12,4},{4,0},{1,9},{9... | collective-permute-start | bytes 442376 | tf_op jit(solution)/shard_map/ppermute | solution.py:319
  524.9 212.3 %collective-permute-start.73 = (bf16[192,384]{1,0:T(8,128)(2,1)}, bf16[192,384]{1,0:T(8,128)(2,1)}, u32[]{:S(2)}, u32[]{:S(2)}) collective-permute-start(bf16[192,384]{1,0:T(8,128)(2,1)} %get-tuple-element.107), channel_id=1, source_target_pairs={{8,0},{16,8},{24,16},{28,24},{20,28},{12,20},{4,12},{0,4},{9,1},{1... | collective-permute-start | bytes 442376 | tf_op jit(solution)/shard_map/ppermute | solution.py:320
  612.3 186.3 %collective-permute-start.29 = (bf16[2,256,1536]{2,1,0:T(8,128)(2,1)}, bf16[2,256,1536]{2,1,0:T(8,128)(2,1)}, u32[]{:S(2)}, u32[]{:S(2)}) collective-permute-start(bf16[2,256,1536]{2,1,0:T(8,128)(2,1)} %dynamic-slice_bitcast_fusion.1), channel_id=1, source_target_pairs={{0,1},{1,0},{2,3},{3,2},{4,5},{5,4},{6,7},{7,6},{8,9},{9,8},{10,11... | collective-permute-start | bytes 4718600 | tf_op jit(solution)/shard_map/ppermute | solution.py:332
  658.3 27.4 %collective-permute-start.43 = (bf16[192,384]{1,0:T(8,128)(2,1)}, bf16[192,384]{1,0:T(8,128)(2,1)}, u32[]{:S(2)}, u32[]{:S(2)}) collective-permute-start(bf16[192,384]{1,0:T(8,128)(2,1)} %get-tuple-element.108), channel_id=1, source_target_pairs={{0,8},{8,16},{16,24},{24,28},{28,20},{20,12},{12,4},{4,0},{1,9},{9... | collective-permute-start | bytes 442376 | tf_op jit(solution)/shard_map/ppermute | solution.py:319
  679.0 10.2 %collective-permute-start.51 = (bf16[192,384]{1,0:T(8,128)(2,1)}, bf16[192,384]{1,0:T(8,128)(2,1)S(1)}, u32[]{:S(2)}, u32[]{:S(2)}) collective-permute-start(bf16[192,384]{1,0:T(8,128)(2,1)} %get-tuple-element.110), channel_id=1, source_target_pairs={{0,8},{8,16},{16,24},{24,28},{28,20},{20,12},{12,4},{4,0},{1,9},{9... | collective-permute-start | bytes 442376 | tf_op jit(solution)/shard_map/ppermute | solution.py:319
  685.6 23.0 %collective-permute-start.59 = (bf16[2,384,256]{2,1,0:T(8,128)(2,1)S(1)}, bf16[2,384,256]{2,1,0:T(8,128)(2,1)}, u32[]{:S(2)}, u32[]{:S(2)}) collective-permute-start(bf16[2,384,256]{2,1,0:T(8,128)(2,1)S(1)} %dynamic-slice_bitcast_fusion.2), channel_id=1, source_target_pairs={{0,1},{1,0},{2,3},{3,2},{4,5},{5,4},{6,7},{7,6},{8,9},{9,8},{10,11... | collective-permute-start | bytes 1179656 | tf_op jit(solution)/shard_map/ppermute | solution.py:332
  685.7 32.5 %collective-permute-start.70 = (bf16[192,768]{1,0:T(8,128)(2,1)}, bf16[192,768]{1,0:T(8,128)(2,1)}, u32[]{:S(2)}, u32[]{:S(2)}) collective-permute-start(bf16[192,768]{1,0:T(8,128)(2,1)} %fusion.11), channel_id=1, source_target_pairs={{0,8},{8,16},{16,24},{24,28},{28,20},{20,12},{12,4},{4,0},{1,9},{9... | collective-permute-start | bytes 884744 | tf_op jit(solution)/shard_map/ppermute | solution.py:319
  689.2 6.8 collective-permute-start.42
  695.9 29.9 %collective-permute-start.44 = (bf16[192,768]{1,0:T(8,128)(2,1)}, bf16[192,768]{1,0:T(8,128)(2,1)}, u32[]{:S(2)}, u32[]{:S(2)}) collective-permute-start(bf16[192,768]{1,0:T(8,128)(2,1)} %fusion.26), channel_id=1, source_target_pairs={{0,8},{8,16},{16,24},{24,28},{28,20},{20,12},{12,4},{4,0},{1,9},{9... | collective-permute-start | bytes 884744 | tf_op jit(solution)/shard_map/ppermute | solution.py:319
  710.0 6.3 collective-permute-start.60
  716.3 15.6 %collective-permute-start.52 = (bf16[192,768]{1,0:T(8,128)(2,1)}, bf16[192,768]{1,0:T(8,128)(2,1)S(1)}, u32[]{:S(2)}, u32[]{:S(2)}) collective-permute-start(bf16[192,768]{1,0:T(8,128)(2,1)} %fusion.18), channel_id=1, source_target_pairs={{0,8},{8,16},{16,24},{24,28},{28,20},{20,12},{12,4},{4,0},{1,9},{9... | collective-permute-start | bytes 884744 | tf_op jit(solution)/shard_map/ppermute | solution.py:319
  724.3 14.1 %collective-permute-start.71 = (bf16[192,768]{1,0:T(8,128)(2,1)S(1)}, bf16[192,768]{1,0:T(8,128)(2,1)S(1)}, u32[]{:S(2)}, u32[]{:S(2)}) collective-permute-start(bf16[192,768]{1,0:T(8,128)(2,1)S(1)} %fusion.12), channel_id=1, source_target_pairs={{0,8},{8,16},{16,24},{24,28},{28,20},{20,12},{12,4},{4,0},{1,9},{9... | collective-permute-start | bytes 884744 | tf_op jit(solution)/shard_map/ppermute | solution.py:319
  725.8 6.1 collective-permute-start.62
  735.8 7.1 collective-permute-start.47
  735.9 14.1 %collective-permute-start.55 = (bf16[192,384]{1,0:T(8,128)(2,1)S(1)}, bf16[192,384]{1,0:T(8,128)(2,1)S(1)}, u32[]{:S(2)}, u32[]{:S(2)}) collective-permute-start(bf16[192,384]{1,0:T(8,128)(2,1)S(1)} %copy-done.48), channel_id=1, source_target_pairs={{8,0},{16,8},{24,16},{28,24},{20,28},{12,20},{4,12},{0,4},{9,1},{1... | collective-permute-start | bytes 442376 | tf_op jit(solution)/shard_map/ppermute | solution.py:320
  737.2 7.7 collective-permute-start.45
  742.9 59.0 %collective-permute-start.36 = (bf16[2,256,1536]{2,1,0:T(8,128)(2,1)S(1)}, bf16[2,256,1536]{2,1,0:T(8,128)(2,1)S(1)}, u32[]{:S(2)}, u32[]{:S(2)}) collective-permute-start(bf16[2,256,1536]{2,1,0:T(8,128)(2,1)S(1)} %copy-done.32), channel_id=1, source_target_pairs={{0,1},{1,0},{2,3},{3,2},{4,5},{5,4},{6,7},{7,6},{8,9},{9,8},{10,11... | collective-permute-start | bytes 4718600 | tf_op jit(solution)/shard_map/ppermute | solution.py:332
  742.9 9.8 %collective-permute-start.53 = (bf16[192,768]{1,0:T(8,128)(2,1)S(1)}, bf16[192,768]{1,0:T(8,128)(2,1)S(1)}, u32[]{:S(2)}, u32[]{:S(2)}) collective-permute-start(bf16[192,768]{1,0:T(8,128)(2,1)S(1)} %fusion.19), channel_id=1, source_target_pairs={{0,8},{8,16},{16,24},{24,28},{28,20},{20,12},{12,4},{4,0},{1,9},{9... | collective-permute-start | bytes 884744 | tf_op jit(solution)/shard_map/ppermute | solution.py:319
  748.9 10.8 %collective-permute-start.74 = (bf16[192,768]{1,0:T(8,128)(2,1)S(1)}, bf16[192,768]{1,0:T(8,128)(2,1)S(1)}, u32[]{:S(2)}, u32[]{:S(2)}) collective-permute-start(bf16[192,768]{1,0:T(8,128)(2,1)S(1)} %get-tuple-element.97), channel_id=1, source_target_pairs={{8,0},{16,8},{24,16},{28,24},{20,28},{12,20},{4,12},{0,4},{9,1},{1... | collective-permute-start | bytes 884744 | tf_op jit(solution)/shard_map/ppermute | solution.py:320
  754.3 40.9 %collective-permute-start.72 = (bf16[192,768]{1,0:T(8,128)(2,1)S(1)}, bf16[192,768]{1,0:T(8,128)(2,1)S(1)}, u32[]{:S(2)}, u32[]{:S(2)}) collective-permute-start(bf16[192,768]{1,0:T(8,128)(2,1)S(1)} %get-tuple-element.96), channel_id=1, source_target_pairs={{0,8},{8,16},{16,24},{24,28},{28,20},{20,12},{12,4},{4,0},{1,9},{9... | collective-permute-start | bytes 884744 | tf_op jit(solution)/shard_map/ppermute | solution.py:319
  758.1 9.9 %collective-permute-start.48 = (bf16[192,768]{1,0:T(8,128)(2,1)S(1)}, bf16[192,768]{1,0:T(8,128)(2,1)S(1)}, u32[]{:S(2)}, u32[]{:S(2)}) collective-permute-start(bf16[192,768]{1,0:T(8,128)(2,1)S(1)} %get-tuple-element.99), channel_id=1, source_target_pairs={{8,0},{16,8},{24,16},{28,24},{20,28},{12,20},{4,12},{0,4},{9,1},{1... | collective-permute-start | bytes 884744 | tf_op jit(solution)/shard_map/ppermute | solution.py:320
  759.7 14.7 %collective-permute-start.56 = (bf16[192,768]{1,0:T(8,128)(2,1)S(1)}, bf16[192,768]{1,0:T(8,128)(2,1)S(1)}, u32[]{:S(2)}, u32[]{:S(2)}) collective-permute-start(bf16[192,768]{1,0:T(8,128)(2,1)S(1)} %get-tuple-element.101), channel_id=1, source_target_pairs={{8,0},{16,8},{24,16},{28,24},{20,28},{12,20},{4,12},{0,4},{9,1},{1... | collective-permute-start | bytes 884744 | tf_op jit(solution)/shard_map/ppermute | solution.py:320
  768.1 12.6 %collective-permute-start.75 = (bf16[192,768]{1,0:T(8,128)(2,1)S(1)}, bf16[192,768]{1,0:T(8,128)(2,1)S(1)}, u32[]{:S(2)}, u32[]{:S(2)}) collective-permute-start(bf16[192,768]{1,0:T(8,128)(2,1)S(1)} %fusion.9), channel_id=1, source_target_pairs={{8,0},{16,8},{24,16},{28,24},{20,28},{12,20},{4,12},{0,4},{9,1},{1... | collective-permute-start | bytes 884744 | tf_op jit(solution)/shard_map/ppermute | solution.py:320
  774.4 12.6 %collective-permute-start.49 = (bf16[192,768]{1,0:T(8,128)(2,1)S(1)}, bf16[192,768]{1,0:T(8,128)(2,1)S(1)}, u32[]{:S(2)}, u32[]{:S(2)}) collective-permute-start(bf16[192,768]{1,0:T(8,128)(2,1)S(1)} %fusion.24), channel_id=1, source_target_pairs={{8,0},{16,8},{24,16},{28,24},{20,28},{12,20},{4,12},{0,4},{9,1},{1... | collective-permute-start | bytes 884744 | tf_op jit(solution)/shard_map/ppermute | solution.py:320
  780.7 12.6 %collective-permute-start.57 = (bf16[192,768]{1,0:T(8,128)(2,1)S(1)}, bf16[192,768]{1,0:T(8,128)(2,1)S(1)}, u32[]{:S(2)}, u32[]{:S(2)}) collective-permute-start(bf16[192,768]{1,0:T(8,128)(2,1)S(1)} %fusion.16), channel_id=1, source_target_pairs={{8,0},{16,8},{24,16},{28,24},{20,28},{12,20},{4,12},{0,4},{9,1},{1... | collective-permute-start | bytes 884744 | tf_op jit(solution)/shard_map/ppermute | solution.py:320
  787.0 10.4 %collective-permute-start.76 = (bf16[192,768]{1,0:T(8,128)(2,1)S(1)}, bf16[192,768]{1,0:T(8,128)(2,1)S(1)}, u32[]{:S(2)}, u32[]{:S(2)}) collective-permute-start(bf16[192,768]{1,0:T(8,128)(2,1)S(1)} %fusion.10), channel_id=1, source_target_pairs={{8,0},{16,8},{24,16},{28,24},{20,28},{12,20},{4,12},{0,4},{9,1},{1... | collective-permute-start | bytes 884744 | tf_op jit(solution)/shard_map/ppermute | solution.py:320
  793.4 10.7 %collective-permute-start.46 = (bf16[192,768]{1,0:T(8,128)(2,1)S(1)}, bf16[192,768]{1,0:T(8,128)(2,1)S(1)}, u32[]{:S(2)}, u32[]{:S(2)}) collective-permute-start(bf16[192,768]{1,0:T(8,128)(2,1)S(1)} %get-tuple-element.98), channel_id=1, source_target_pairs={{0,8},{8,16},{16,24},{24,28},{28,20},{20,12},{12,4},{4,0},{1,9},{9... | collective-permute-start | bytes 884744 | tf_op jit(solution)/shard_map/ppermute | solution.py:319
  795.2 12.2 %collective-permute-start.54 = (bf16[192,768]{1,0:T(8,128)(2,1)S(1)}, bf16[192,768]{1,0:T(8,128)(2,1)S(1)}, u32[]{:S(2)}, u32[]{:S(2)}) collective-permute-start(bf16[192,768]{1,0:T(8,128)(2,1)S(1)} %get-tuple-element.100), channel_id=1, source_target_pairs={{0,8},{8,16},{16,24},{24,28},{28,20},{20,12},{12,4},{4,0},{1,9},{9... | collective-permute-start | bytes 884744 | tf_op jit(solution)/shard_map/ppermute | solution.py:319
  797.4 9.9 %collective-permute-start.50 = (bf16[192,768]{1,0:T(8,128)(2,1)S(1)}, bf16[192,768]{1,0:T(8,128)(2,1)S(1)}, u32[]{:S(2)}, u32[]{:S(2)}) collective-permute-start(bf16[192,768]{1,0:T(8,128)(2,1)S(1)} %fusion.25), channel_id=1, source_target_pairs={{8,0},{16,8},{24,16},{28,24},{20,28},{12,20},{4,12},{0,4},{9,1},{1... | collective-permute-start | bytes 884744 | tf_op jit(solution)/shard_map/ppermute | solution.py:320
  798.6 11.8 %collective-permute-start.58 = (bf16[192,768]{1,0:T(8,128)(2,1)S(1)}, bf16[192,768]{1,0:T(8,128)(2,1)S(1)}, u32[]{:S(2)}, u32[]{:S(2)}) collective-permute-start(bf16[192,768]{1,0:T(8,128)(2,1)S(1)} %fusion.17), channel_id=1, source_target_pairs={{8,0},{16,8},{24,16},{28,24},{20,28},{12,20},{4,12},{0,4},{9,1},{1... | collective-permute-start | bytes 884744 | tf_op jit(solution)/shard_map/ppermute | solution.py:320
  802.4 20.5 %collective-permute-start.37 = (bf16[1,256,1536]{2,1,0:T(8,128)(2,1)S(1)}, bf16[1,256,1536]{2,1,0:T(8,128)(2,1)S(1)}, u32[]{:S(2)}, u32[]{:S(2)}) collective-permute-start(bf16[1,256,1536]{2,1,0:T(8,128)(2,1)S(1)} %constant_dynamic-slice_fusion.2), channel_id=1, source_target_pairs={{0,2},{1,3},{2,0},{3,1},{4,6},{5,7},{6,4},{7,5},{8,10},{9,11},{10,... | collective-permute-start | bytes 2359304 | tf_op jit(solution)/shard_map/ppermute | solution.py:332
  804.0 31.9 %collective-permute-start.30 = (bf16[1,256,1536]{2,1,0:T(8,128)(2,1)S(1)}, bf16[1,256,1536]{2,1,0:T(8,128)(2,1)S(1)}, u32[]{:S(2)}, u32[]{:S(2)}) collective-permute-start(bf16[1,256,1536]{2,1,0:T(8,128)(2,1)S(1)} %constant_dynamic-slice_fusion.3), channel_id=1, source_target_pairs={{0,2},{1,3},{2,0},{3,1},{4,6},{5,7},{6,4},{7,5},{8,10},{9,11},{10,... | collective-permute-start | bytes 2359304 | tf_op jit(solution)/shard_map/ppermute | solution.py:332
  (84 other events, 1913.5 us)

commit v2 on v1

v2 whole, which is shorter than its diff:
```python
from functools import partial

import jax, jax.numpy as jnp
from jax import lax
from jax.experimental import pallas as pl
from jax.experimental.pallas import tpu as pltpu
from jax.sharding import PartitionSpec as P
f32=jnp.float32; bf16=jnp.bfloat16
Q=128
NS=128
VW=768
HW=64
CW=1024
RW=1152
SPAN=256
LIMIT=14<<20
NEG=-1e30

def mm(a,b,ca=1,cb=0):
    return lax.dot_general(a,b,(((ca,),(cb,)),((),())),preferred_element_type=f32)

def split2(x):
    hi=x.astype(bf16); return hi,(x-hi.astype(f32)).astype(bf16)

def split3(x):
    hi=x.astype(bf16); r=x-hi.astype(f32); mid=r.astype(bf16); return hi,mid,(r-mid.astype(f32)).astype(bf16)

def mm3(a,b,ca=1,cb=0):
    ah,al=split2(a); bh,bl=split2(b)
    return mm(jnp.concatenate([ah,ah,al],axis=ca),jnp.concatenate([bh,bl,bh],axis=cb),ca,cb)

def tri_sum(tri,x):
    a,b,c=split3(x); w=x.shape[1]
    p=mm(tri,jnp.concatenate([a,b,c],axis=1))
    return p[:,:w]+p[:,w:2*w]+p[:,2*w:]

def spread(x,ee):
    a,b=split2(x)
    return mm(jnp.concatenate([a,b],axis=1),ee)

def head_sum(x,hh):
    a,b=split2(x)
    return mm(jnp.concatenate([a,b],axis=1),hh)

def iotas():
    return lax.broadcasted_iota(jnp.int32,(Q,Q),0),lax.broadcasted_iota(jnp.int32,(Q,Q),1)

def softplus(z):
    return jnp.maximum(z,0.0)+jnp.log(1.0+jnp.exp(-jnp.abs(z)))

def sig(z):
    return 1.0/(1.0+jnp.exp(-z))

def halves(x):
    lane=lax.broadcasted_iota(jnp.int32,x.shape,1)
    lo=jnp.where(lane<HW,x,0.0); hi=jnp.where(lane<HW,0.0,x)
    return jnp.concatenate([lo.astype(bf16),hi.astype(bf16)],axis=0)

def spread_matrix(shape):
    r=lax.broadcasted_iota(jnp.int32,shape,0)%128; c=lax.broadcasted_iota(jnp.int32,shape,1)//HW
    return jnp.where(r==c,1.0,0.0).astype(bf16)

def sum_matrix(shape):
    r=lax.broadcasted_iota(jnp.int32,shape,0)%VW//HW; c=lax.broadcasted_iota(jnp.int32,shape,1)
    return jnp.where(r==c,1.0,0.0).astype(bf16)

def halves2(x):
    lane=lax.broadcasted_iota(jnp.int32,x.shape,1)
    h,l=split2(jnp.concatenate([jnp.where(lane<HW,x,0.0),jnp.where(lane<HW,0.0,x)],axis=0))
    return h,l

def fwd_kernel(c0,nc,first_ref,raw_ref,par_ref,*rest):
    y_ref,pre_ref,sp_ref,s_ref,t_ref,ext,ee_ref=rest[-7:]
    ck_ref=par_ref
    i=pl.program_id(0)
    @pl.when(i==0)
    def _():
        ee_ref[...]=spread_matrix(ee_ref.shape)
        if c0:
            s_ref[...]=rest[0][...]; t_ref[...]=rest[1][...]
        else:
            s_ref[...]=jnp.zeros_like(s_ref); t_ref[...]=jnp.zeros_like(t_ref)
    c=c0+i
    start=(first_ref[c//(SPAN//Q)]==1)&(c%(SPAN//Q)==0)
    @pl.when(start)
    def _():
        s_ref[...]=jnp.zeros_like(s_ref); t_ref[...]=jnp.zeros_like(t_ref)
    ext[0:8,:]=t_ref[...]
    x=raw_ref[:,:CW]
    ext[8:8+Q,:]=x
    t_ref[...]=raw_ref[Q-8:Q,:CW]
    pre=par_ref[4:5,:]+ck_ref[3:4,:]*x
    for j in (1,2,3):
        pre=pre+ck_ref[3-j:4-j,:]*ext[8-j:8-j+Q,:]
    pre_ref[...]=pre
    act=pre*sig(pre)
    v=act[:,:VW]; b=act[:,VW:VW+NS].astype(bf16); cc=act[:,VW+NS:].astype(bf16)
    dt=softplus(raw_ref[:,CW:]+par_ref[5:6,:128])
    a=-dt*jnp.exp(par_ref[6:7,:128])
    row,col=iotas()
    low=row>=col
    tri=jnp.where(low,1.0,0.0).astype(bf16)
    cum=tri_sum(tri,a)
    cum_t=cum.T
    last=cum[Q-1:Q,:]
    ee=ee_ref[...]
    sprd=spread(jnp.concatenate([dt,jnp.exp(cum),jnp.exp(last-cum)],axis=0),ee)
    dte,ecum,etail=sprd[:Q],sprd[Q:2*Q],sprd[2*Q:]
    x=v*dte
    g=mm(cc,b,1,1)
    parts=[]
    for p in range(VW//128):
        ws=[]
        for h in (2*p,2*p+1):
            d=jnp.where(low,cum[:,h:h+1]-cum_t[h:h+1,:],NEG)
            ws.append((jnp.exp(d)*g).astype(bf16))
        parts.append(mm(jnp.concatenate(ws,axis=1),halves(x[:,128*p:128*p+128])))
    s=s_ref[...]
    sp_ref[0]=s
    y_ref[...]=jnp.concatenate(parts,axis=1)+ecum*mm(cc,s.astype(bf16))+par_ref[7:8,:VW]*v
    s_ref[...]=ecum[Q-1:Q,:]*s+mm(b,(x*etail).astype(bf16),0,0)

def bwd_kernel(c0,nc,nall,first_ref,raw_ref,pre_ref,y_ref,dy_ref,sp_ref,par_ref,*rest):
    out_ref,vs_ref,ds_ref,sn_ref,h_ref,acc_ref,acs_ref,ext,ee_ref,hh_ref=rest[-10:]
    ck_ref=par_ref
    i=pl.program_id(0)
    @pl.when(i==0)
    def _():
        ee_ref[...]=spread_matrix(ee_ref.shape)
        hh_ref[...]=sum_matrix(hh_ref.shape)
        for k,ref in enumerate((ds_ref,sn_ref,h_ref,acc_ref,acs_ref)):
            ref[...]=jnp.zeros_like(ref) if c0+nc==nall else rest[k][...]
    c=c0+nc-1-i
    nxt=jnp.minimum(c+1,nall-1)
    start=(first_ref[nxt//(SPAN//Q)]==1)&(nxt%(SPAN//Q)==0)
    @pl.when(start)
    def _():
        ds_ref[...]=jnp.zeros_like(ds_ref); h_ref[...]=jnp.zeros_like(h_ref)
    pre=pre_ref[...]
    sg=sig(pre)
    act=pre*sg
    v=act[:,:VW]; bf=act[:,VW:VW+NS]; cf=act[:,VW+NS:]
    b=bf.astype(bf16); cc=cf.astype(bf16)
    z=raw_ref[:,CW:]+par_ref[5:6,:128]
    dt=softplus(z)
    edl=jnp.exp(par_ref[6:7,:128])
    a=-dt*edl
    row,col=iotas()
    low=row>=col; up=row<=col
    cum=tri_sum(jnp.where(low,1.0,0.0).astype(bf16),a)
    cum_t=cum.T
    last=cum[Q-1:Q,:]
    ee=ee_ref[...]
    sprd=spread(jnp.concatenate([dt,jnp.exp(cum),jnp.exp(last-cum)],axis=0),ee)
    dte,ecum,etail=sprd[:Q],sprd[Q:2*Q],sprd[2*Q:]
    x=v*dte
    xb=x.astype(bf16)
    dy=dy_ref[...].astype(f32)
    dyb=dy.astype(bf16)
    gt=mm(b,cc,1,1)
    dgt=jnp.zeros((Q,Q),f32)
    parts=[]
    for p in range(VW//128):
        cols=slice(128*p,128*p+128)
        dyh,dyl=split2(dy[:,cols])
        xh,xl=halves2(x[:,cols])
        dw=mm(jnp.concatenate([xh,xl,xh],axis=1),jnp.concatenate([dyh,dyh,dyl],axis=1),1,1)
        ws=[]
        for k in (0,1):
            h=2*p+k
            lt=jnp.exp(jnp.where(up,cum_t[h:h+1,:]-cum[:,h:h+1],NEG))
            ws.append((lt*gt).astype(bf16))
            dgt=dgt+lt*dw[k*Q:(k+1)*Q]
        parts.append(mm(jnp.concatenate(ws,axis=1),halves(dy[:,cols])))
    ds=ds_ref[...]
    dsb=ds.astype(bf16)
    s=sp_ref[0]
    dxd=jnp.concatenate(parts,axis=1)
    bds=mm(b,dsb)
    dx=dxd+etail*bds
    xe=(x*etail).astype(bf16)
    dye=dy*ecum
    db=mm3(dgt,cf)+mm3(x*etail,ds,1,1)
    dc=mm3(dgt,bf,0,0)+mm3(dye,s,1,1)
    kk=jnp.sum(dsb.astype(f32)*sn_ref[...],axis=0,keepdims=True)
    kk=jnp.concatenate([kk,jnp.zeros((7,VW),f32)],axis=0)
    hs=head_sum(jnp.concatenate([dyb.astype(f32)*(y_ref[...]-par_ref[7:8,:VW]*v)-xb.astype(f32)*dxd-xe.astype(f32)*bds,v*dx,kk],axis=0),hh_ref[...])
    dcum,q,k0=hs[:Q],hs[Q:2*Q],hs[2*Q:2*Q+1]
    da=k0+tri_sum(jnp.where(up,1.0,0.0).astype(bf16),dcum)
    dst=(q-da*edl)*sig(z)
    ds_ref[...]=ecum[Q-1:Q,:]*ds+mm3(cf,dye,0,0)
    sn_ref[...]=s
    acs_ref[0:1,:]+=jnp.sum(da*a,axis=0,keepdims=True)
    acs_ref[1:2,:]+=jnp.sum(dst,axis=0,keepdims=True)
    dv=dte*dx+par_ref[7:8,:VW]*dy
    acc_ref[5:6,:VW]+=jnp.sum(dy*v,axis=0,keepdims=True)
    dpre=jnp.concatenate([dv,db,dc],axis=1)*(sg*(1.0+pre-act))
    ext[0:Q,:]=dpre
    ext[Q:Q+8,:]=h_ref[...]
    h_ref[...]=dpre[0:8,:]
    xr=raw_ref[:,:CW]
    draw=ck_ref[3:4,:]*dpre
    acc_ref[3:4,:]+=jnp.sum(dpre*xr,axis=0,keepdims=True)
    acc_ref[4:5,:]+=jnp.sum(dpre,axis=0,keepdims=True)
    for j in (1,2,3):
        sh=ext[j:j+Q,:]
        draw=draw+ck_ref[3-j:4-j,:]*sh
        acc_ref[3-j:4-j,:]+=jnp.sum(sh*xr,axis=0,keepdims=True)
    drawb,dstb=draw.astype(bf16),dst.astype(bf16)
    out_ref[:,:CW]=drawb
    out_ref[:,CW:]=dstb
    vs_ref[:,:VW]=drawb[:,:VW]
    vs_ref[:,VW:]=dstb

def sd(shape,dt=f32): return jax.ShapeDtypeStruct(shape,dt)

def whole(shape): return pl.BlockSpec(shape,lambda i,*_: (0,)*len(shape))

def once(shape): return pl.BlockSpec(shape,lambda i,*_: (0,)*len(shape),pipeline_mode=pl.Buffered(1))

def ssd_fwd(c0,nc,nall,first,raw,par,carry):
    rb=lambda w: pl.BlockSpec((Q,w),lambda i,*_: (c0+i,0))
    any_spec=pl.BlockSpec(memory_space=pl.ANY)
    held=[whole((NS,VW)),whole((8,CW))]
    return pl.pallas_call(partial(fwd_kernel,c0,nc),
        out_shape=(sd((nall*Q,VW)),sd((nall*Q,CW)),sd((nall,NS,VW)),sd((NS,VW)),sd((8,CW))),
        grid_spec=pltpu.PrefetchScalarGridSpec(num_scalar_prefetch=1,grid=(nc,),
            in_specs=[rb(RW),once((8,CW))]+(held+[any_spec]*3 if carry else []),
            out_specs=(rb(VW),rb(CW),pl.BlockSpec((1,NS,VW),lambda i,*_: (c0+i,0,0)),*held),
            scratch_shapes=[pltpu.VMEM((Q+8,CW),f32),pltpu.VMEM((256,VW),bf16)]),
        input_output_aliases={5+k:k for k in range(3)} if carry else {},
        compiler_params=pltpu.CompilerParams(vmem_limit_bytes=LIMIT),
        cost_estimate=pl.CostEstimate(flops=int(1.5e9*nc/8),bytes_accessed=30_000_000*nc//8,transcendentals=3_000_000*nc//8),
        name=f"ssd_forward_{c0}")(first,raw,par,*(carry[3:]+carry[:3] if carry else ()))

def ssd_bwd(c0,nc,nall,first,raw,pre,y,dy,sp,par,carry):
    rv=lambda w: pl.BlockSpec((Q,w),lambda i,*_: (c0+nc-1-i,0))
    any_spec=pl.BlockSpec(memory_space=pl.ANY)
    held=[whole((NS,VW)),whole((NS,VW)),whole((8,CW)),whole((8,CW)),whole((8,128))]
    return pl.pallas_call(partial(bwd_kernel,c0,nc,nall),
        out_shape=(sd((nall*Q,RW),bf16),sd((nall*Q,VW+128),bf16),sd((NS,VW)),sd((NS,VW)),sd((8,CW)),sd((8,CW)),sd((8,128))),
        grid_spec=pltpu.PrefetchScalarGridSpec(num_scalar_prefetch=1,grid=(nc,),
            in_specs=[rv(RW),rv(CW),rv(VW),rv(VW),pl.BlockSpec((1,NS,VW),lambda i,*_: (c0+nc-1-i,0,0)),once((8,CW))]
                     +(held+[any_spec]*2 if carry else []),
            out_specs=(rv(RW),rv(VW+128),*held),
            scratch_shapes=[pltpu.VMEM((Q+8,CW),f32),pltpu.VMEM((256,VW),bf16),pltpu.VMEM((2*VW,128),bf16)]),
        input_output_aliases={12+k:k for k in range(2)} if carry else {},
        compiler_params=pltpu.CompilerParams(vmem_limit_bytes=LIMIT),
        cost_estimate=pl.CostEstimate(flops=int(3e9*nc/8),bytes_accessed=60_000_000*nc//8,transcendentals=4_000_000*nc//8),
        name=f"ssd_backward_{c0}")(first,raw,pre,y,dy,sp,par,*(carry[2:]+carry[:2] if carry else ()))


D = 1536
H = 48
E = 3072
TOK_DEV = 1024
SEQ_DEV = 4
EPSILON = 1e-05
FWD_PARTS = 2
BACK_PARTS = 2


def contract(left, right, left_dim, right_dim, out=f32):
    return lax.dot_general(
        left, right, (((left_dim,), (right_dim,)), ((), ())), preferred_element_type=f32
    ).astype(out)


def span_layout(seq_lengths, seq_device, seq_offset, device):
    span_index = jnp.arange(SEQ_DEV, dtype=jnp.int32)
    needed = (seq_lengths + SPAN - 1) // SPAN
    owned_seq = (seq_device == device) & (seq_lengths > 0)
    relative = span_index[None, :] - seq_offset[:, None]
    inside = owned_seq[:, None] & (relative >= 0) & (relative < needed[:, None])
    live_rows = jnp.sum(
        jnp.where(inside, jnp.clip(seq_lengths[:, None] - relative * SPAN, 0, SPAN), 0), axis=0
    )
    seq_first = jnp.any(inside & (relative == 0), axis=0)
    return live_rows, seq_first.astype(jnp.int32)


def ring_order(count):
    if count == 8:
        return [0, 2, 4, 6, 7, 5, 3, 1]
    return list(range(count))


def lay(cols, rows, off_ref, refs, out):
    for k, (c0, w) in enumerate(cols):
        out[pl.ds(pl.multiple_of(off_ref[k] * rows, 16), rows), c0 : c0 + w] = refs[k][...]


def row_sums(x):
    a, b = split2(x)
    ones = jnp.ones((8, x.shape[1]), bf16)
    return mm(ones, a, 1, 1) + mm(ones, b, 1, 1)


def project_kernel(cols, rows, nx, off_ref, *refs):
    n = len(cols)
    xs = refs[n : n + nx]
    w_ref, x_ref, xt_ref, raw_ref, gate_ref = refs[n + nx :]
    i = pl.program_id(0)

    @pl.when(i == 0)
    def _():
        lay(cols, rows, off_ref, refs, w_ref)

    for k in range(nx):

        @pl.when(i == k)
        def _(k=k):
            x_ref[...] = xs[k][...]

    xt_ref[...] = x_ref[...].T
    r = mm(x_ref[...], w_ref[...])
    raw_ref[...] = r[:, :RW]
    gate_ref[...] = r[:, RW:]


def project(pieces, offsets, xs, total):
    rows, n = pieces[0][0].shape[0], len(pieces)
    cols = [(c0, x.shape[1]) for x, c0 in pieces]
    width = max(c0 + w for c0, w in cols)
    q, depth = xs[0].shape
    nx = len(xs)
    at = lambda w: pl.BlockSpec((q, w), lambda i, off: (off[n + i], 0))
    return pl.pallas_call(
        partial(project_kernel, cols, rows, nx),
        out_shape=(sd((total, width), bf16), sd((q * nx, depth), bf16), sd((depth, q * nx), bf16), sd((q * nx, RW)), sd((q * nx, width - RW))),
        grid_spec=pltpu.PrefetchScalarGridSpec(
            num_scalar_prefetch=1,
            grid=(nx,),
            in_specs=[once(x.shape) for x, _ in pieces] + [once(x.shape) for x in xs],
            out_specs=(whole((total, width)), at(depth), pl.BlockSpec((depth, q), lambda i, off: (0, off[n + i])), at(RW), at(width - RW)),
        ),
        compiler_params=pltpu.CompilerParams(vmem_limit_bytes=30 << 20),
        cost_estimate=pl.CostEstimate(flops=2 * q * nx * total * width, bytes_accessed=30_000_000, transcendentals=0),
        name="project",
    )(offsets, *[x for x, _ in pieces], *xs)


def cotangent_kernel(cols, rows, nx, off_ref, *refs):
    n = len(cols)
    xs = refs[n : n + nx]
    ssd_ref, gr_ref, gain_ref, w_ref, x_ref, by_ref, sum_ref, yr_ref = refs[n + nx :]
    i = pl.program_id(0)

    @pl.when(i == 0)
    def _():
        lay(cols, rows, off_ref, refs, w_ref)

    for k in range(nx):

        @pl.when(i == k)
        def _(k=k):
            x_ref[...] = xs[k][...]

    by = mm(x_ref[...], w_ref[...])
    by_ref[...] = by
    gr = gr_ref[...]
    gated = ssd_ref[...] * (gr * sig(gr))
    yr_ref[...] = (gated * gain_ref[...]).astype(bf16)
    square = row_sums(gated * gated)
    cross = row_sums(by * gain_ref[...] * gated)
    top = lax.broadcasted_iota(jnp.int32, square.shape, 0) == 0
    sum_ref[0] = jnp.where(top, square, cross)


def cotangent(pieces, offsets, xs, ssd, gate_raw, gain, total):
    rows, n = pieces[0][0].shape[0], len(pieces)
    cols = [(c0, x.shape[1]) for x, c0 in pieces]
    width = max(c0 + w for c0, w in cols)
    q, depth = xs[0].shape
    nx = len(xs)
    at = lambda w: pl.BlockSpec((q, w), lambda i, off: (off[n + i], 0))
    return pl.pallas_call(
        partial(cotangent_kernel, cols, rows, nx),
        out_shape=(sd((total, width), bf16), sd((q * nx, depth), bf16), sd((q * nx, width)), sd((nx, 8, q)), sd((q * nx, width), bf16)),
        grid_spec=pltpu.PrefetchScalarGridSpec(
            num_scalar_prefetch=1,
            grid=(nx,),
            in_specs=[once(x.shape) for x, _ in pieces]
            + [once(x.shape) for x in xs]
            + [at(width), at(width), once((1, width))],
            out_specs=(
                whole((total, width)),
                at(depth),
                at(width),
                pl.BlockSpec((1, 8, q), lambda i, off: (off[n + i], 0, 0)),
                at(width),
            ),
        ),
        compiler_params=pltpu.CompilerParams(vmem_limit_bytes=22 << 20),
        cost_estimate=pl.CostEstimate(flops=2 * q * nx * total * width, bytes_accessed=24_000_000, transcendentals=800_000),
        name="cotangent",
    )(offsets, *[x for x, _ in pieces], *xs, ssd, gate_raw, gain)


def gate_kernel(sum_ref, by_ref, gr_ref, ssd_ref, gain_ref, ny_ref, bg_ref, dy_ref, gg_ref):
    @pl.when(pl.program_id(0) == 0)
    def _():
        gg_ref[...] = jnp.zeros_like(gg_ref)

    sums = sum_ref[0].T
    inv = lax.rsqrt(sums[:, 0:1] / E + EPSILON)
    gr, ssd, by, gain = gr_ref[...], ssd_ref[...], by_ref[...], gain_ref[...]
    sg = sig(gr)
    gate = gr * sg
    unit = ssd * gate * inv
    ny_ref[...] = (unit * gain).astype(bf16)
    gg_ref[0:1, :] += jnp.sum(by * unit, axis=0, keepdims=True)
    back = inv * (by * gain - unit * (inv * sums[:, 1:2] / E))
    bg_ref[...] = (back * ssd * (sg * (1.0 + gr - gate))).astype(bf16)
    dy_ref[...] = back * gate


def gate_back(sums, by, gate_raw, ssd, gain):
    t, width = by.shape
    n, _, q = sums.shape
    rb = pl.BlockSpec((q, width), lambda i: (i, 0))
    return pl.pallas_call(
        gate_kernel,
        out_shape=(sd((t, width), bf16), sd((t, width), bf16), sd((t, width)), sd((8, width))),
        grid=(n,),
        in_specs=[pl.BlockSpec((1, 8, q), lambda i: (i, 0, 0)), rb, rb, rb, once((1, width))],
        out_specs=(rb, rb, rb, whole((8, width))),
        compiler_params=pltpu.CompilerParams(vmem_limit_bytes=12 << 20),
        cost_estimate=pl.CostEstimate(flops=20_000_000, bytes_accessed=15_000_000, transcendentals=800_000),
        name="gate_back",
    )(sums, by, gate_raw, ssd, gain)


def normed_kernel(at_ref, first_ref, gate_ref, w_ref, x_ref, ng_in, out_ref, ng_ref):
    @pl.when(pl.program_id(0) == 0)
    def _():
        ng_ref[...] = ng_in[...]

    back = mm(first_ref[...], w_ref[:, :RW], 1, 1) + mm(gate_ref[...], w_ref[:, RW:], 1, 1)
    out_ref[0] = back.astype(bf16)
    ng_ref[0:1, :] += jnp.sum(back * x_ref[...].astype(f32), axis=0, keepdims=True)


def back_normed_rows(at, q, first, gate, w, normed, ng):
    depth = normed.shape[1]
    n = at.shape[0]
    rb = lambda c: pl.BlockSpec((q, c), lambda i, at: (at[i], 0))
    return pl.pallas_call(
        normed_kernel,
        out_shape=(sd((n, q, depth), bf16), sd((8, depth))),
        grid_spec=pltpu.PrefetchScalarGridSpec(
            num_scalar_prefetch=1,
            grid=(n,),
            in_specs=[rb(RW), rb(VW), once(w.shape), rb(depth), once((8, depth))],
            out_specs=(pl.BlockSpec((1, q, depth), lambda i, at: (i, 0, 0)), whole((8, depth))),
        ),
        compiler_params=pltpu.CompilerParams(vmem_limit_bytes=16 << 20),
        cost_estimate=pl.CostEstimate(flops=2 * n * q * depth * (RW + VW), bytes_accessed=16_000_000, transcendentals=0),
        name="back_normed",
    )(at, first, gate, w, normed, ng)


def mixer_kernel(at_ref, x_ref, w_ref, out_ref):
    out_ref[0] = mm(x_ref[...], w_ref[...], 1, 1).astype(bf16)


def mixer_blocks(at, q, x, w):
    n, (depth, width) = at.shape[0], w.shape
    return pl.pallas_call(
        mixer_kernel,
        out_shape=sd((n, q, depth), bf16),
        grid_spec=pltpu.PrefetchScalarGridSpec(
            num_scalar_prefetch=1,
            grid=(n,),
            in_specs=[pl.BlockSpec((q, width), lambda i, at: (at[i], 0)), once(w.shape)],
            out_specs=pl.BlockSpec((1, q, depth), lambda i, at: (i, 0, 0)),
        ),
        compiler_params=pltpu.CompilerParams(vmem_limit_bytes=10 << 20),
        cost_estimate=pl.CostEstimate(flops=2 * n * q * depth * width, bytes_accessed=7_000_000, transcendentals=0),
        name="mixer_rows",
    )(at, x, w)


def grad_kernel(per, rows, at_ref, xt_ref, back_ref, out_ref):
    i = pl.program_id(0)
    r = mm(xt_ref[...], back_ref[...]).astype(bf16)
    for d in range(per):
        out_ref[pl.ds(at_ref[i * per + d], 1)] = r[d * rows : (d + 1) * rows][None]


def weight_grad(at, xt, back, n_dp):
    depth, t = xt.shape
    rows, width = depth // n_dp, back.shape[1]
    steps = 2
    return pl.pallas_call(
        partial(grad_kernel, n_dp // steps, rows),
        out_shape=sd((n_dp, rows, width), bf16),
        grid_spec=pltpu.PrefetchScalarGridSpec(
            num_scalar_prefetch=1,
            grid=(steps,),
            in_specs=[pl.BlockSpec((depth // steps, t), lambda i, at: (i, 0)), once(back.shape)],
            out_specs=whole((n_dp, rows, width)),
        ),
        compiler_params=pltpu.CompilerParams(vmem_limit_bytes=16 << 20),
        cost_estimate=pl.CostEstimate(flops=2 * depth * t * width, bytes_accessed=8_000_000, transcendentals=0),
        name="weight_grad",
    )(at, xt, back)


def state_grad_kernel(n_tensor, per, rows, at_ref, xt_ref, back_ref, out_ref):
    i = pl.program_id(0)
    share = rows // n_tensor
    r = mm(xt_ref[...], back_ref[...]).astype(bf16)
    for d in range(per):
        for t in range(n_tensor):
            k = d * n_tensor + t
            out_ref[pl.ds(at_ref[i * per * n_tensor + k], 1)] = r[k * share : (k + 1) * share][None]


def state_weight_grad(at, xt, back, n_dp, n_tensor):
    depth, t = xt.shape
    rows = depth // n_dp
    share, width, steps = rows // n_tensor, 2 * NS, 2
    return pl.pallas_call(
        partial(state_grad_kernel, n_tensor, n_dp // steps, rows),
        out_shape=sd((n_tensor * n_dp, share, width), bf16),
        grid_spec=pltpu.PrefetchScalarGridSpec(
            num_scalar_prefetch=1,
            grid=(steps,),
            in_specs=[pl.BlockSpec((depth // steps, t), lambda i, at: (i, 0)), pl.BlockSpec((t, width), lambda i, at: (0, VW // width))],
            out_specs=whole((n_tensor * n_dp, share, width)),
        ),
        compiler_params=pltpu.CompilerParams(vmem_limit_bytes=10 << 20),
        cost_estimate=pl.CostEstimate(flops=2 * depth * t * width, bytes_accessed=5_000_000, transcendentals=0),
        name="state_weight_grad",
    )(at, xt, back)


class Ring:
    def __init__(self, count):
        self.count = count
        self.half = count // 2
        self.order = ring_order(count)
        at = {d: i for i, d in enumerate(self.order)}
        self.table = [[self.order[(at[d] + k) % count] for k in range(count)] for d in range(count)]
        self.ahead = [(self.order[i], self.order[(i + 1) % count]) for i in range(count)]
        self.back = [(b, a) for a, b in self.ahead]

    def rows_of(self, table):
        return jnp.asarray(table, jnp.int32)[lax.axis_index("dp")]

    def hop(self, f, b):
        return lax.ppermute(f, "dp", self.ahead), lax.ppermute(b, "dp", self.back)


class Gather:
    def __init__(self, ring, x):
        self.ring, self.mid = ring, x.shape[1] // 2 // 128 * 128
        self.pieces, self.f, self.b, self.s = [(x, 0)], x, x, 0

    def ready(self):
        if self.s == self.ring.half - 1:
            return [self.f[:, : self.mid], self.b[:, self.mid :]]
        return [self.f, self.b]

    def step(self, f, b):
        self.s += 1
        self.f, self.b = self.ring.hop(f, b)
        self.pieces += [(self.f, 0), (self.b, self.mid if self.s == self.ring.half else 0)]

    @staticmethod
    def offsets(ring):
        ahead = [0]
        for s in range(1, ring.half + 1):
            ahead += [ring.count - s, s]
        return [[ring.table[d][k] for k in ahead] for d in range(ring.count)]


class Scatter:
    def __init__(self, ring, x):
        self.ring, self.x, self.mid, self.s = ring, x, x.shape[2] // 2 // 128 * 128, ring.half

    def ready(self):
        x, s, mid = self.x, self.s, self.mid
        if s == self.ring.half:
            return [x[s, :, :mid], x[s, :, mid:]]
        f, b = self.f, self.b
        if s == self.ring.half - 1:
            f = jnp.pad(f, ((0, 0), (0, x.shape[2] - mid)))
            b = jnp.pad(b, ((0, 0), (mid, 0)))
        f = x[s].astype(f32) + f.astype(f32)
        b = x[self.ring.count - s].astype(f32) + b.astype(f32)
        return [f.astype(bf16), b.astype(bf16)]

    def step(self, f, b):
        self.f, self.b = self.ring.hop(f, b)
        self.s -= 1

    def total(self):
        return self.x[0].astype(f32) + self.f.astype(f32) + self.b.astype(f32)


def swap(x, axis, count, bits):
    return lax.ppermute(x, axis, [(i, i ^ bits) for i in range(count)])


def tensor_order(count):
    keys = [0]
    bit = count // 2
    while bit:
        keys += [k ^ bit for k in keys]
        bit //= 2
    return keys


def pick(x, index, axis=0):
    return lax.dynamic_index_in_dim(x, index, axis, keepdims=False)


def groups_of(count):
    bits = [1 << k for k in range(count.bit_length() - 1)]
    first = len(bits) % 2
    return ([bits[:first]] if first else []) + [bits[k : k + 2] for k in range(first, len(bits), 2)]


def others(bits):
    return [bits[0]] if len(bits) == 1 else [bits[0], bits[1], bits[0] | bits[1]]


class Spread:
    def __init__(self, x, axis, count):
        self.x, self.axis, self.count, self.groups = x, axis, count, groups_of(count)

    def step(self, x):
        bits = self.groups.pop(0)
        self.x = sum((swap(x, self.axis, self.count, k) for k in others(bits)), x)


class Share:
    def __init__(self, x, axis, count):
        self.x, self.axis, self.count, self.groups = x, axis, count, groups_of(count)

    def ready(self):
        bits = self.groups[0]
        n = 2 ** len(bits)
        self.parts = self.x.reshape((self.x.shape[0] // n, n) + self.x.shape[1:])
        return [self.parts[:, k // bits[0]].astype(bf16) for k in others(bits)]

    def step(self, sends):
        bits = self.groups.pop(0)
        got = [swap(x, self.axis, self.count, k) for x, k in zip(sends, others(bits))]
        self.x = sum((g.astype(f32) for g in got), self.parts[:, 0].astype(f32))


def together(*lists):
    flat = lax.optimization_barrier(tuple(x for xs in lists for x in xs))
    out, at = [], 0
    for xs in lists:
        out.append(list(flat[at : at + len(xs)]))
        at += len(xs)
    return out


def body(
    n_dp,
    n_tensor,
    hidden_in,
    norm_gain,
    gate_value_weight,
    state_proj_weight,
    step_weight,
    conv_value_kernel,
    conv_value_bias,
    conv_state_kernel,
    conv_state_bias,
    step_bias,
    decay_log,
    skip_scale,
    gate_norm_gain,
    out_weight,
    out_cotangent,
    seq_lengths,
    seq_device,
    seq_offset,
):
    quarter = hidden_in.shape[0]
    heads = step_weight.shape[1]
    rows = gate_value_weight.shape[0]
    me, dp = lax.axis_index("tensor"), lax.axis_index("dp")
    ring = Ring(n_dp)
    ring_at = ring.rows_of([[ring.table[d].index(k) for k in range(n_dp)] for d in range(n_dp)])
    order = me ^ jnp.asarray([3, 1, 2, 0], jnp.int32)
    ids = jnp.arange(n_dp * n_tensor, dtype=jnp.int32)
    state_at = (ids % n_tensor ^ me) * n_dp + (ids // n_tensor ^ dp)
    offsets = jnp.concatenate([ring.rows_of(Gather.offsets(ring)), me ^ jnp.asarray(tensor_order(n_tensor), jnp.int32)])
    to_core = lambda x: swap(x, "tensor", n_tensor, 1)
    to_far = lambda x: swap(x, "tensor", n_tensor, 2)

    live_rows, seq_first = span_layout(seq_lengths, seq_device, seq_offset, dp)
    row = me * quarter + jnp.arange(quarter, dtype=jnp.int32)
    local_live = jnp.sum(
        jnp.where((row // SPAN)[:, None] == jnp.arange(SEQ_DEV)[None, :], live_rows[None, :], 0), axis=1
    )
    local_mask = (row % SPAN < local_live).astype(f32)

    pad_to = lambda x, w: jnp.pad(x, (0, w - x.shape[0]))[None]
    params = jnp.concatenate(
        [
            jnp.concatenate([conv_value_kernel, conv_state_kernel], axis=0).T,
            jnp.concatenate([conv_value_bias, conv_state_bias])[None],
            pad_to(step_bias, CW),
            pad_to(decay_log, CW),
            pad_to(jnp.repeat(skip_scale, HW), CW),
        ],
        axis=0,
    )
    gain = gate_norm_gain[None]
    zeros = lambda *s: jnp.zeros(s, f32)

    first_own = jnp.concatenate(
        [
            gate_value_weight[:, 1, :],
            state_proj_weight,
            jnp.pad(step_weight, ((0, 0), (0, 128 - heads))),
            gate_value_weight[:, 0, :],
        ],
        axis=1,
    )
    inv_rms = lax.rsqrt(jnp.mean(hidden_in * hidden_in, axis=-1) + EPSILON)
    scaled = hidden_in * inv_rms[:, None]
    normed_local = (scaled * norm_gain[None, :]).astype(bf16)
    back_local = (local_mask[:, None] * out_cotangent).astype(bf16)
    (first_own, offsets, ring_at, order, state_at, seq_first, params) = lax.optimization_barrier(
        (first_own, offsets, ring_at, order, state_at, seq_first, params)
    )
    first = Gather(ring, first_own)
    out = Gather(ring, out_weight)
    normed_local, = lax.optimization_barrier((normed_local,))
    first.step(*first.ready())
    normed_parts = [normed_local, to_far(normed_local)]
    for s in range(1, ring.half):
        sends = [first.ready()]
        if s == 1:
            sends.append(normed_parts)
        if s == min(2, ring.half - 1):
            sends.append([back_local] + normed_parts[2:])
        if s == ring.half - 1:
            sends += [out.ready(), back_parts]
        sends = together(*sends)
        first.step(*sends.pop(0))
        if s == 1:
            [a, b] = sends.pop(0)
            normed_parts = [a, b, to_core(a), to_core(b)]
        if s == min(2, ring.half - 1):
            [a, *normed_parts[2:]] = sends.pop(0)
            back_parts = [a, to_far(a)]
        if s == ring.half - 1:
            out.step(*sends.pop(0))
            [a, b] = sends.pop(0)
            back_parts = [a, b, to_core(a), to_core(b)]
    xs, os = together([x for x, _ in first.pieces] + normed_parts, out.ready())
    out.step(*os)
    n = len(first.pieces)
    first_w, normed, normed_t, raw, gate_raw = project(
        [(x, c0) for x, (_, c0) in zip(xs[:n], first.pieces)], offsets, xs[n:], D
    )
    chunks = TOK_DEV // Q
    n = chunks // FWD_PARTS
    carry = ()
    for i in range(FWD_PARTS):
        if out.s < ring.half:
            gated_by = [carry[3]] if carry else [raw]
            gated_by, os = together(gated_by, out.ready())
            out.step(*os)
            if carry:
                carry = carry[:3] + (gated_by[0],) + carry[4:]
            else:
                raw = gated_by[0]
        carry = tuple(ssd_fwd(i * n, n, chunks, seq_first, raw, params, carry))
    while out.s < ring.half:
        out.step(*out.ready())
    ssd, pre, states = carry[:3]

    out_w, back_mix, back_y, sums, gated = cotangent(out.pieces, offsets, back_parts, ssd, gate_raw, gain, D)
    total = Spread(sums, "tensor", n_tensor)
    while total.groups:
        total.step(total.x)
    sums = total.x
    mixer = mixer_blocks(order, quarter, gated, out_w)
    sums, mixer = lax.optimization_barrier((sums, mixer))
    normed_y, back_gate, back_ssd, gain_grad = gate_back(sums, back_y, gate_raw, ssd, gain)
    gate_sum = Scatter(ring, weight_grad(ring_at, normed_t, back_gate, n_dp))

    half_rows = quarter // 2
    gs, ms = together(gate_sum.ready(), [mixer[:2]])
    gate_sum.step(*gs)
    got = to_core(ms[0])
    out_grad = contract(back_mix, normed_y, 0, 0, bf16)
    out_out = lax.psum_scatter(out_grad, "dp", scatter_dimension=0, tiled=True).astype(f32)
    n = chunks // BACK_PARTS
    away = (mixer[2].astype(f32) + got[0].astype(f32)).astype(bf16)
    away = [away[:half_rows], away[half_rows:]]
    carry, mixer_parts = (), []
    for k, i in enumerate(reversed(range(BACK_PARTS))):
        held = [carry[2]] if carry else [back_ssd]
        held, gs, ms, mixer_parts = together(held, gate_sum.ready(), [away[k]], mixer_parts)
        if carry:
            carry = carry[:2] + (held[0],) + carry[3:]
        else:
            back_ssd = held[0]
        gate_sum.step(*gs)
        mixer_parts.append(to_far(ms[0]))
        carry = tuple(ssd_bwd(i * n, n, chunks, seq_first, raw, pre, ssd, back_ssd, states, params, carry))
    back_first, back_vs, _, _, _, acc, acs = carry
    square = pick(sums, me)[0]
    local_inv = lax.rsqrt(square / E + EPSILON)

    value_sum = Scatter(ring, weight_grad(ring_at, normed_t, back_vs, n_dp))
    gs, vs, mixer_parts, [back_first] = together(gate_sum.ready(), value_sum.ready(), mixer_parts, [back_first])
    value_sum.step(*vs)
    gate_sum.step(*gs)
    state_sum = Share(
        state_weight_grad(state_at, normed_t, back_first, n_dp, n_tensor).reshape(n_tensor, n_dp, rows // n_tensor, 2 * NS),
        "tensor",
        n_tensor,
    )
    away, ng = back_normed_rows(order[:2], quarter, back_first, back_gate, first_w, normed, zeros(8, D))
    vs, gs, cs, ss, [back_first] = together(
        value_sum.ready(), [gate_sum.f, gate_sum.b], [away], state_sum.ready(), [back_first]
    )
    value_sum.step(*vs)
    gate_sum.f, gate_sum.b = gs
    near = to_core(cs[0])
    state_sum.step(ss)
    keep, ng = back_normed_rows(order[2:], quarter, back_first, back_gate, first_w, normed, ng)
    while gate_sum.s:
        gate_sum.step(*gate_sum.ready())
    gate_out = gate_sum.total()
    output = hidden_in + (local_mask * local_inv)[:, None] * (
        mixer[3].astype(f32) + got[1].astype(f32) + jnp.concatenate(mixer_parts, axis=0).astype(f32)
    )
    away = (keep[0].astype(f32) + near[0].astype(f32)).astype(bf16)
    state_sum = Share(state_sum.x[0], "dp", n_dp)
    shared = jnp.concatenate([acc[:5, VW:], (ng[0] / norm_gain).reshape(6, 256), zeros(5, 256)], axis=0)
    shared = Spread(shared, "tensor", n_tensor)
    vs, cs, ss, ps = together(value_sum.ready(), [away[:half_rows], away[half_rows:]], state_sum.ready(), [shared.x])
    value_sum.step(*vs)
    got = [to_far(cs[0])]
    state_sum.step(ss)
    shared.step(ps[0])
    own = jnp.concatenate(
        [acc[:6], jnp.concatenate([gain_grad[0], acs[0], acs[1]])[None], zeros(1, CW)], axis=0
    )
    while shared.groups:
        shared.step(shared.x)
    small = Spread(jnp.concatenate([own, shared.x.reshape(4, CW)], axis=0), "dp", n_dp)
    vs, cs, ss, ps = together(value_sum.ready(), [got[0], cs[1]], state_sum.ready(), [small.x])
    value_sum.step(*vs)
    got = [cs[0], to_far(cs[1])]
    state_sum.step(ss)
    small.step(ps[0])
    if value_sum.s:
        while value_sum.s:
            value_sum.step(*value_sum.ready())
        while state_sum.groups:
            state_sum.step(state_sum.ready())
    vs, cs, ss, ps = together([value_sum.f, value_sum.b], got, [state_sum.x], [small.x])
    value_sum.f, value_sum.b = vs
    small.x = ps[0]
    while small.groups:
        small.step(small.x)
    small, state_out = small.x, ss[0][0]
    value_out = value_sum.total()
    back_rows = keep[1].astype(f32) + near[1].astype(f32) + jnp.concatenate(cs, axis=0).astype(f32)
    back_scaled = back_rows * norm_gain[None, :]
    hidden_gradient = out_cotangent + inv_rms[:, None] * (
        back_scaled - scaled * jnp.mean(back_scaled * scaled, axis=-1)[:, None]
    )
    shared = small[8:].reshape(16, 256)
    index = dp * n_tensor + me
    all_count = n_dp * n_tensor
    kern_share = 2 * NS // all_count
    state_kernel_out = lax.dynamic_slice(shared, (0, index * kern_share), (5, kern_share))
    norm_out = lax.dynamic_slice(shared[5:11].reshape(D), (index * (D // all_count),), (D // all_count,))
    return (
        output,
        hidden_gradient,
        norm_out,
        jnp.stack([gate_out, value_out[:, :VW]], axis=1),
        state_out,
        value_out[:, VW : VW + heads],
        small[:4, :VW].T,
        small[4, :VW],
        state_kernel_out[:4].T,
        state_kernel_out[4],
        small[6, VW + 128 : VW + 128 + heads],
        small[6, VW : VW + heads],
        jnp.sum(small[5, :VW].reshape(heads, HW), axis=1),
        small[6, :VW],
        out_out,
    )


def solution(mesh):
    in_specs = (
        P(("dp", "tensor"), None),
        P(),
        P("dp", None, "tensor"),
        P("dp", None),
        P("dp", "tensor"),
        P("tensor", None),
        P("tensor"),
        P(),
        P(),
        P("tensor"),
        P("tensor"),
        P("tensor"),
        P("tensor"),
        P("dp", "tensor"),
        P(("dp", "tensor"), None),
        P(),
        P(),
        P(),
    )
    out_specs = (
        P(("dp", "tensor"), None),
        P(("dp", "tensor"), None),
        P(("dp", "tensor")),
        P("dp", None, "tensor"),
        P(("dp", "tensor"), None),
        P("dp", "tensor"),
        P("tensor", None),
        P("tensor"),
        P(("dp", "tensor"), None),
        P(("dp", "tensor")),
        P("tensor"),
        P("tensor"),
        P("tensor"),
        P("tensor"),
        P("dp", "tensor"),
    )
    return jax.shard_map(
        partial(body, mesh.shape["dp"], mesh.shape["tensor"]),
        mesh=mesh,
        in_specs=in_specs,
        out_specs=out_specs,
        check_vma=False,
    )
```

time: 848 us -> 333 us (0.39)
  Pallas kernels: 486 us -> 84.6 us
  matrix products: 53.3 us -> 6.49 us
  waiting for transfers between devices: 124 us -> 97.8 us
  starting transfers between devices: 78.8 us -> 55.9 us
  local copies, waits for them, and re-layouts: 49.8 us -> 35.6 us
    pallas_call x9 -> x13, Pallas kernels: 486 us -> 84.6 us  [the longest x2 29.8 us: ssd_bwd(): pl.pallas_call(partial(bwd_kernel, c0, nc, nall), out_shape=(sd((nall * Q...]
    dot_general x11 -> x1, matrix products: 53.3 us -> 6.49 us  [contract(): lax.dot_general(left, right, (((left_dim,), (right_dim,)), ((), ())), pre...]
    ppermute x77 -> x61, waiting for transfers between devices: 124 us -> 97.8 us  [the longest x32 81.5 us: hop(): return (lax.ppermute(f, 'dp', self.ahead), lax.ppermute(b, 'dp', self.back))]
    ppermute x77 -> x61, starting transfers between devices: 78.8 us -> 55.9 us  [the longest x32 33.2 us: hop(): return (lax.ppermute(f, 'dp', self.ahead), lax.ppermute(b, 'dp', self.back))]
    unnamed x147 -> x117, local copies, waits for them, and re-layouts: 12.2 us -> 24.2 us
  transfers between devices with their start and end apart: 77 -> 62, of which waited for: 32 -> 21; matrix products, arithmetic and copies ran while one was open for 14% -> 12% of each run, Pallas kernels for 58% -> 22%
where the time goes in v2:
time: 333 us; the launch traced here: 326 us
  waiting for transfers between devices  97.8 us (29%)
  Pallas kernels  84.6 us (25%)
  starting transfers between devices  55.9 us (17%)
  local copies, waits for them, and re-layouts  35.6 us (11%)
  other arithmetic  30.6 us (9%)
  between operations  15.4 us (5%)
  matrix products  6.49 us (2%)
    ppermute x32, waiting for transfers between devices, hop(): return (lax.ppermute(f, 'dp', self.ahead), lax.ppermute(b, 'dp', self.back))  81.5 us
    ppermute x32, starting transfers between devices, hop(): return (lax.ppermute(f, 'dp', self.ahead), lax.ppermute(b, 'dp', self.back))  33.2 us
    pallas_call x2, Pallas kernels, ssd_bwd(): pl.pallas_call(partial(bwd_kernel, c0, nc, nall), out_shape=(sd((nall * Q...  29.8 us
    unnamed x117, local copies, waits for them, and re-layouts  24.2 us
    ppermute x29, starting transfers between devices, swap(): return lax.ppermute(x, axis, [(i, i ^ bits) for i in range(count)])  22.7 us
    ppermute x29, waiting for transfers between devices, swap(): return lax.ppermute(x, axis, [(i, i ^ bits) for i in range(count)])  16.4 us
    pallas_call x1, Pallas kernels, project(): pl.pallas_call(partial(project_kernel, cols, rows, nx), out_shape=(sd((to...  12.3 us
    pallas_call x2, Pallas kernels, ssd_fwd(): pl.pallas_call(partial(fwd_kernel, c0, nc), out_shape=(sd((nall * Q, VW))...  10.7 us
  transfers between devices with their start and end apart: 62, of which 21 were waited for; matrix products, arithmetic and copies ran while one was open for 12% of the time, Pallas kernels for 22%

profile of v2, /device:TPU:0, one launch (start us, length us, event | category | flops | bytes accessed | tf_op | source)
XLA Modules:
  0.0 326.5 jit_solution(13119087187360724356)
XLA Ops:
  7.2 1.7 multiply_reduce_fusion.1
  10.1 3.0 collective-permute-start.2
  16.5 1.6 collective-permute-start.1
  18.7 15.8 %collective-permute-done.1.refs_2_ = bf16[192,1920]{1,0:T(8,128)(2,1)S(1)} collective-permute-done((bf16[192,1920]{1,0:T(8,128)(2,1)S(1)}, bf16[192,1920]{1,0:T(8,128)(2,1)S(1)}, u32[]{:S(2)}, u32[]{:S(2)}) %collective-permute-start.1) | collective-permute-done | bytes 737312 | tf_op jit(solution)/shard_map/ppermute | solution.py:553
  36.9 1.5 collective-permute-start.4
  38.5 1.6 multiply_convert_fusion.refs_9_
  40.1 15.0 %collective-permute-done.3.refs_3_ = bf16[192,1920]{1,0:T(8,128)(2,1)S(1)} collective-permute-done((bf16[192,1920]{1,0:T(8,128)(2,1)}, bf16[192,1920]{1,0:T(8,128)(2,1)S(1)}, u32[]{:S(2)}, u32[]{:S(2)}) %collective-permute-start.3) | collective-permute-done | bytes 737312 | tf_op jit(solution)/shard_map/ppermute | solution.py:553
  55.7 1.6 collective-permute-start.7
  57.8 15.3 %collective-permute-done.7.refs_5_ = bf16[192,1920]{1,0:T(8,128)(2,1)S(1)} collective-permute-done((bf16[192,1920]{1,0:T(8,128)(2,1)S(1)}, bf16[192,1920]{1,0:T(8,128)(2,1)S(1)}, u32[]{:S(2)}, u32[]{:S(2)}) %collective-permute-start.7) | collective-permute-done | bytes 737312 | tf_op jit(solution)/shard_map/ppermute | solution.py:553
  76.2 1.6 collective-permute-start.10
  78.2 11.5 %collective-permute-done.10.refs_1_ = bf16[192,768]{1,0:T(8,128)(2,1)S(1)} collective-permute-done((bf16[192,768]{1,0:T(8,128)(2,1)S(1)}, bf16[192,768]{1,0:T(8,128)(2,1)S(1)}, u32[]{:S(2)}, u32[]{:S(2)}) %collective-permute-start.10) | collective-permute-done | bytes 294944 | tf_op jit(solution)/shard_map/ppermute | solution.py:553
  94.1 12.3 %project.1 = (bf16[1536,1920]{1,0:T(8,128)(2,1)}, bf16[1024,1536]{1,0:T(8,128)(2,1)S(1)}, bf16[1536,1024]{1,0:T(8,128)(2,1)S(1)}, f32[1024,1152]{1,0:T(8,128)S(1)}, f32[1024,768]{1,0:T(8,128)S(1)}) custom-call(s32[13]{0:T(128)S(1)} %pad_add_fusion.off_ref, bf16[192,1920]{1,0:T(8,128)(2,1)S(1)} %fusion.6.refs_0_, ...), custom_call_target="tpu_custom_call" | custom-call | flops 6039797760 | bytes 30000000 | tf_op jit(solution)/shard_map/project/pallas_call | solution.py:328
  106.4 1.7 copy-done.6
  110.2 5.0 %ssd_forward_0.1 = (f32[1024,768]{1,0:T(8,128)S(1)}, f32[1024,1024]{1,0:T(8,128)S(1)}, f32[8,128,768]{2,1,0:T(8,128)S(1)}, f32[128,768]{1,0:T(8,128)S(1)}, f32[8,1024]{1,0:T(8,128)S(1)}) custom-call(s32[4]{0:T(128)S(1)} %convert_element_type.326.first_ref, f32[1024,1152]{1,0:T(8,128)S(1)} %get-tuple-element.179.raw_ref, f32[8,1024]{1,0:T(8,128)S(1)} %concatenate.34.par_ref), custom_call_target="tpu_custom_call" | custom-call | flops 750000000 | bytes 15000000 | tf_op jit(solution)/shard_map/ssd_forward_0/pallas_call | solution.py:225
  115.2 1.8 collective-permute-done.16.refs_5_
  119.4 5.7 %ssd_forward_4.1 = (f32[1024,768]{1,0:T(8,128)S(1)}, f32[1024,1024]{1,0:T(8,128)S(1)}, f32[8,128,768]{2,1,0:T(8,128)S(1)}, f32[128,768]{1,0:T(8,128)}, f32[8,1024]{1,0:T(8,128)}) custom-call(s32[4]{0:T(128)S(1)} %convert_element_type.326.first_ref, ...), custom_call_target="tpu_custom_call", output_to_operand_aliasing={{0}: (5, {}), {1}: (6, {}), {2}: (7, {})} | custom-call | flops 750000000 | bytes 15000000 | tf_op jit(solution)/shard_map/ssd_forward_4/pallas_call | solution.py:225
  125.2 2.0 copy-done.2
  127.1 1.6 copy-done.4
  128.8 6.1 %cotangent.1 = (bf16[1536,768]{1,0:T(8,128)(2,1)S(1)}, bf16[1024,1536]{1,0:T(8,128)(2,1)S(1)}, f32[1024,768]{1,0:T(8,128)S(1)}, f32[4,8,256]{2,1,0:T(8,128)S(1)}, bf16[1024,768]{1,0:T(8,128)(2,1)S(1)}) custom-call(s32[13]{0:T(128)S(1)} %pad_add_fusion.off_ref, bf16[192,768]{1,0:T(8,128)(2,1)S(1)} %copy-done.18, ...), custom_call_target="tpu_custom_call" | custom-call | flops 2415919104 | bytes 24000000 | tf_op jit(solution)/shard_map/cotangent/pallas_call | solution.py:377
  134.9 1.7 copy-done.19
  138.4 3.8 %mixer_rows.1 = bf16[4,256,1536]{2,1,0:T(8,128)(2,1)S(1)} custom-call(s32[4]{0:T(128)S(1)} %get-tuple-element.194.at_ref, bf16[1024,768]{1,0:T(8,128)(2,1)S(1)} %get-tuple-element.195.x_ref, bf16[1536,768]{1,0:T(8,128)(2,1)S(1)} %get-tuple-element.196.w_ref), custom_call_target="tpu_custom_call" | custom-call | flops 2415919104 | bytes 7000000 | tf_op jit(solution)/shard_map/mixer_rows/pallas_call | solution.py:469
  144.5 3.3 %gate_back.1 = (bf16[1024,768]{1,0:T(8,128)(2,1)S(1)}, bf16[1024,768]{1,0:T(8,128)(2,1)S(1)}, f32[1024,768]{1,0:T(8,128)S(1)}, f32[8,768]{1,0:T(8,128)S(1)}) custom-call(f32[4,8,256]{2,1,0:T(8,128)S(1)} %add_add_fusion.1.sum_ref, f32[1024,768]{1,0:T(8,128)S(1)} %get-tuple-element.201.by_ref, f32[1024,768]{1,0:T(8,128)S(1)} %get-tuple-element.192.refs_14_.gr_ref, ...), custom_call_target="tpu_custom_call" | custom-call | flops 20000000 | bytes 15000000 | tf_op jit(solution)/shard_map/gate_back/pallas_call | solution.py:422
  147.8 3.3 %weight_grad.2 = bf16[8,192,768]{2,1,0:T(8,128)(2,1)S(1)} custom-call(s32[8]{0:T(128)S(1)} %fusion.42.at_ref, bf16[1536,1024]{1,0:T(8,128)(2,1)S(1)} %get-tuple-element.200.xt_ref, bf16[1024,768]{1,0:T(8,128)(2,1)S(1)} %get-tuple-element.202.back_ref.gate_ref), custom_call_target="tpu_custom_call" | custom-call | flops 2415919104 | bytes 8000000 | tf_op jit(solution)/shard_map/weight_grad/pallas_call | solution.py:495
  155.0 6.5 %convolution_convert_fusion = bf16[1536,768]{1,0:T(8,128)(2,1)} fusion(bf16[1024,1536]{1,0:T(8,128)(2,1)} %copy-done.19, bf16[1024,768]{1,0:T(8,128)(2,1)} %copy-done.20), kind=kOutput, calls=%fused_computation | convolution fusion | flops 2417098752 | bytes 7077888 | tf_op jit(solution)/shard_map/dot_general | solution.py:264
  161.4 2.0 fusion.19
  163.4 1.6 add_convert_fusion.1
  169.2 2.3 copy-done.1
  171.5 2.2 copy-done.3
  173.7 1.9 copy-done.5
  175.6 1.9 copy-done.9
  177.5 14.5 %ssd_backward_4.1 = (bf16[1024,1152]{1,0:T(8,128)(2,1)S(1)}, bf16[1024,896]{1,0:T(8,128)(2,1)S(1)}, f32[128,768]{1,0:T(8,128)S(1)}, f32[128,768]{1,0:T(8,128)S(1...) custom-call(s32[4]{0:T(128)S(1)} %convert_element_type.326.first_ref, ...), custom_call_target="tpu_custom_call" | custom-call | flops 1500000000 | bytes 30000000 | tf_op jit(solution)/shard_map/ssd_backward_4/pallas_call | solution.py:240
  194.2 15.2 %ssd_backward_0.1 = (bf16[1024,1152]{1,0:T(8,128)(2,1)S(1)}, bf16[1024,896]{1,0:T(8,128)(2,1)S(1)}, f32[128,768]{1,0:T(8,128)}, f32[128,768]{1,0:T(8,128)}, f32[...) custom-call(s32[4]{0:T(128)S(1)} %convert_element_type.326.first_ref, ...), custom_call_target="tpu_custom_call", output_to_operand_aliasing={{0}: (12, {}), {1}: (13, {})} | custom-call | flops 1500000000 | bytes 30000000 | tf_op jit(solution)/shard_map/ssd_backward_0/pallas_call | solution.py:240
  209.4 1.6 collective-permute-start.31
  212.8 4.2 %weight_grad.3 = bf16[8,192,896]{2,1,0:T(8,128)(2,1)S(1)} custom-call(s32[8]{0:T(128)S(1)} %fusion.42.at_ref, bf16[1536,1024]{1,0:T(8,128)(2,1)S(1)} %copy-done.13, bf16[1024,896]{1,0:T(8,128)(2,1)S(1)} %get-tuple-element.223.back_ref), custom_call_target="tpu_custom_call" | custom-call | flops 2818572288 | bytes 8000000 | tf_op jit(solution)/shard_map/weight_grad/pallas_call | solution.py:495
  217.0 1.8 collective-permute-done.31
  219.1 2.1 collective-permute-done.33
  221.2 1.6 collective-permute-start.34
  223.3 1.6 collective-permute-start.36
  225.5 1.8 state_weight_grad.1
  227.4 5.1 %back_normed.2 = (bf16[2,256,1536]{2,1,0:T(8,128)(2,1)}, f32[8,1536]{1,0:T(8,128)S(1)}) custom-call(s32[2]{0:T(128)S(1)} %get-tuple-element.360.at_ref, bf16[1024,1152]{1,0:T(8,128)(2,1)S(1)} %get-tuple-element.238.first_ref.back_ref, bf16[1024,768]{1,0:T(8,128)(2,1)S(1)} %copy-done.11, bf16[1536,1920]{1,0:T(8,128)(2,1)S(1)} %bitcast.179, ...), custom_call_target="tpu_custom_call" | custom-call | flops 3019898880 | bytes 16000000 | tf_op jit(solution)/shard_map/back_normed/pallas_call | solution.py:448
  233.3 2.4 collective-permute-done.35
  236.5 3.1 collective-permute-done.36
  239.6 3.3 collective-permute-done.37
  243.6 4.3 %back_normed.3 = (bf16[2,256,1536]{2,1,0:T(8,128)(2,1)S(1)}, f32[8,1536]{1,0:T(8,128)S(1)}) custom-call(s32[2]{0:T(128)S(1)} %get-tuple-element.359.at_ref, bf16[1024,1152]{1,0:T(8,128)(2,1)S(1)} %get-tuple-element.238.first_ref.back_ref, bf16[1024,768]{1,0:T(8,128)(2,1)S(1)} %copy-done.11, bf16[1536,1920]{1,0:T(8,128)(2,1)S(1)} %bitcast.179, ...), custom_call_target="tpu_custom_call" | custom-call | flops 3019898880 | bytes 16000000 | tf_op jit(solution)/shard_map/back_normed/pallas_call | solution.py:448
  248.1 1.8 collective-permute-start.43
  249.9 1.6 collective-permute-start.39
  252.0 3.8 %collective-permute-done.42 = bf16[1,8,48,256]{3,2,1,0:T(8,128)(2,1)S(1)} collective-permute-done((bf16[1,8,48,256]{3,2,1,0:T(8,128)(2,1)S(1)}, bf16[1,8,48,256]{3,2,1,0:T(8,128)(2,1)S(1)}, u32[]{:S(2)}, u32[]{:S(2)}) %collective-permute-start.42) | collective-permute-done | bytes 196640 | tf_op jit(solution)/shard_map/ppermute | solution.py:604
  255.8 3.3 %collective-permute-done.43 = bf16[1,8,48,256]{3,2,1,0:T(8,128)(2,1)S(1)} collective-permute-done((bf16[1,8,48,256]{3,2,1,0:T(8,128)(2,1)S(1)}, bf16[1,8,48,256]{3,2,1,0:T(8,128)(2,1)S(1)}, u32[]{:S(2)}, u32[]{:S(2)}) %collective-permute-start.43) | collective-permute-done | bytes 196640 | tf_op jit(solution)/shard_map/ppermute | solution.py:604
  261.6 2.0 fusion.9
  270.5 2.8 collective-permute-done.47
  273.4 6.4 %collective-permute-done.44 = bf16[192,896]{1,0:T(8,128)(2,1)S(1)} collective-permute-done((bf16[192,896]{1,0:T(8,128)(2,1)}, bf16[192,896]{1,0:T(8,128)(2,1)S(1)}, u32[]{:S(2)}, u32[]{:S(2)}) %collective-permute-start.44) | collective-permute-done | bytes 344096 | tf_op jit(solution)/shard_map/ppermute | solution.py:553
  279.8 2.1 fusion.8
  282.2 2.5 collective-permute-start.55
  284.7 1.7 collective-permute-start.56
  286.3 2.0 collective-permute-start.52
  289.0 2.1 fusion.15
  292.1 4.3 %collective-permute-done.57 = f32[12,1024]{1,0:T(8,128)S(1)} collective-permute-done((f32[12,1024]{1,0:T(8,128)S(1)}, f32[12,1024]{1,0:T(8,128)S(1)}, u32[]{:S(2)}, u32[]{:S(2)}) %collective-permute-start.57) | collective-permute-done | bytes 49184 | tf_op jit(solution)/shard_map/ppermute | solution.py:604
  297.0 1.8 convert_element_type.412
  298.9 2.7 collective-permute-start.60
  301.6 1.8 collective-permute-start.58
  303.3 1.8 multiply_reduce_fusion
  305.1 1.5 fusion.7
  307.0 4.3 %multiply_add_fusion = (f32[256,1536]{1,0:T(8,128)}, f32[256,1536]{1,0:T(8,128)}) fusion(f32[256,1536]{1,0:T(8,128)S(1)} %copy-done.27, f32[256,1536]{1,0:T(8,128)S(1)} %copy-done.26, f32[256]{0:T(256)S(1)} %broadcast_multiply_fusion, f32[1536]{0:T(1024)S(1)} %copy-done.39, f32[256]{0:T(256)S(1)} %add_rsqrt_fusion, ...), kind=kLoop, calls=%fused_computation.8 | loop fusion | flops 9437184 | bytes 11019264 | tf_op jit(solution)/shard_map/add | solution.py:876
  312.1 1.9 copy.57
  (288 shorter events, 59.7 us)
Async XLA Ops:
  7.2 289.9 %reduce-scatter.2.cloned.1.call-start = ((), (), s32[]{:S(2)}) async-start(), calls=%async_computation.1 | async-start | bytes 2654208 | tf_op jit(solution)/shard_map/reduce_scatter | solution.py:799
  10.1 25.7 %collective-permute-start.2 = (bf16[256,1536]{1,0:T(8,128)(2,1)S(1)}, bf16[256,1536]{1,0:T(8,128)(2,1)S(1)}, u32[]{:S(2)}, u32[]{:S(2)}) collective-permute-start(bf16[256,1536]{1,0:T(8,128)(2,1)S(1)} %multiply_convert_fusion.1.refs_9_), channel_id=1, source_target_pairs={{0,2},{1,3},{2,0},{3,1},{4,6},{5,7},{6,4},{7,5},{8,10},{9,11},{10,... | collective-permute-start | bytes 2359304 | tf_op jit(solution)/shard_map/ppermute | solution.py:604
  16.5 18.0 %collective-permute-start.1 = (bf16[192,1920]{1,0:T(8,128)(2,1)S(1)}, bf16[192,1920]{1,0:T(8,128)(2,1)S(1)}, u32[]{:S(2)}, u32[]{:S(2)}) collective-permute-start(bf16[192,1920]{1,0:T(8,128)(2,1)S(1)} %fusion.6.refs_0_), channel_id=1, source_target_pairs={{8,0},{16,8},{24,16},{28,24},{20,28},{12,20},{4,12},{0,4},{9,1},{1... | collective-permute-start | bytes 2211848 | tf_op jit(solution)/shard_map/ppermute | solution.py:553
  18.1 17.8 %collective-permute-start = (bf16[192,1920]{1,0:T(8,128)(2,1)S(1)}, bf16[192,1920]{1,0:T(8,128)(2,1)}, u32[]{:S(2)}, u32[]{:S(2)}) collective-permute-start(bf16[192,1920]{1,0:T(8,128)(2,1)S(1)} %fusion.6.refs_0_), channel_id=1, source_target_pairs={{0,8},{8,16},{16,24},{24,28},{28,20},{20,12},{12,4},{4,0},{1,9},{9... | collective-permute-start | bytes 2211848 | tf_op jit(solution)/shard_map/ppermute | solution.py:553
  35.8 19.3 %collective-permute-start.5 = (bf16[256,1536]{1,0:T(8,128)(2,1)S(1)}, bf16[256,1536]{1,0:T(8,128)(2,1)S(1)}, u32[]{:S(2)}, u32[]{:S(2)}) collective-permute-start(bf16[256,1536]{1,0:T(8,128)(2,1)S(1)} %multiply_convert_fusion.1.refs_9_), channel_id=1, source_target_pairs={{0,1},{1,0},{2,3},{3,2},{4,5},{5,4},{6,7},{7,6},{8,9},{9,8},{10,11... | collective-permute-start | bytes 2359304 | tf_op jit(solution)/shard_map/ppermute | solution.py:604
  35.8 19.3 %collective-permute-start.6 = (bf16[256,1536]{1,0:T(8,128)(2,1)S(1)}, bf16[256,1536]{1,0:T(8,128)(2,1)S(1)}, u32[]{:S(2)}, u32[]{:S(2)}) collective-permute-start(bf16[256,1536]{1,0:T(8,128)(2,1)S(1)} %collective-permute-done.2.refs_10_), channel_id=1, source_target_pairs={{0,1},{1,0},{2,3},{3,2},{4,5},{5,4},{6,7},{7,6},{8,9},{9,8},{10,11... | collective-permute-start | bytes 2359304 | tf_op jit(solution)/shard_map/ppermute | solution.py:604
  36.4 18.7 %collective-permute-start.3 = (bf16[192,1920]{1,0:T(8,128)(2,1)}, bf16[192,1920]{1,0:T(8,128)(2,1)S(1)}, u32[]{:S(2)}, u32[]{:S(2)}) collective-permute-start(bf16[192,1920]{1,0:T(8,128)(2,1)} %collective-permute-done.refs_1_), channel_id=1, source_target_pairs={{0,8},{8,16},{16,24},{24,28},{28,20},{20,12},{12,4},{4,0},{1,9},{9... | collective-permute-start | bytes 2211848 | tf_op jit(solution)/shard_map/ppermute | solution.py:553
  36.9 18.2 %collective-permute-start.4 = (bf16[192,1920]{1,0:T(8,128)(2,1)S(1)}, bf16[192,1920]{1,0:T(8,128)(2,1)S(1)}, u32[]{:S(2)}, u32[]{:S(2)}) collective-permute-start(bf16[192,1920]{1,0:T(8,128)(2,1)S(1)} %collective-permute-done.1.refs_2_), channel_id=1, source_target_pairs={{8,0},{16,8},{24,16},{28,24},{20,28},{12,20},{4,12},{0,4},{9,1},{1... | collective-permute-start | bytes 2211848 | tf_op jit(solution)/shard_map/ppermute | solution.py:553
  38.5 37.7 %copy-start.18 = (bf16[192,768]{1,0:T(8,128)(2,1)S(1)}, bf16[192,768]{1,0:T(8,128)(2,1)}, u32[]{:S(2)}) copy-start(bf16[192,768]{1,0:T(8,128)(2,1)} %refs_0_.1) | copy-start | bytes 884740
  55.1 19.0 %collective-permute-start.9 = (bf16[256,1536]{1,0:T(8,128)(2,1)S(1)}, bf16[256,1536]{1,0:T(8,128)(2,1)S(1)}, u32[]{:S(2)}, u32[]{:S(2)}) collective-permute-start(bf16[256,1536]{1,0:T(8,128)(2,1)S(1)} %multiply_convert_fusion.refs_9_), channel_id=1, source_target_pairs={{0,2},{1,3},{2,0},{3,1},{4,6},{5,7},{6,4},{7,5},{8,10},{9,11},{10,... | collective-permute-start | bytes 2359304 | tf_op jit(solution)/shard_map/ppermute | solution.py:604
  55.7 17.3 %collective-permute-start.7 = (bf16[192,1920]{1,0:T(8,128)(2,1)S(1)}, bf16[192,1920]{1,0:T(8,128)(2,1)S(1)}, u32[]{:S(2)}, u32[]{:S(2)}) collective-permute-start(bf16[192,1920]{1,0:T(8,128)(2,1)S(1)} %collective-permute-done.3.refs_3_), channel_id=1, source_target_pairs={{0,8},{8,16},{16,24},{24,28},{28,20},{20,12},{12,4},{4,0},{1,9},{9... | collective-permute-start | bytes 2211848 | tf_op jit(solution)/shard_map/ppermute | solution.py:553
  57.3 16.7 %collective-permute-start.8 = (bf16[192,1920]{1,0:T(8,128)(2,1)S(1)}, bf16[192,1920]{1,0:T(8,128)(2,1)S(1)}, u32[]{:S(2)}, u32[]{:S(2)}) collective-permute-start(bf16[192,1920]{1,0:T(8,128)(2,1)S(1)} %collective-permute-done.4.refs_4_), channel_id=1, source_target_pairs={{8,0},{16,8},{24,16},{28,24},{20,28},{12,20},{4,12},{0,4},{9,1},{1... | collective-permute-start | bytes 2211848 | tf_op jit(solution)/shard_map/ppermute | solution.py:553
  74.1 15.7 %collective-permute-start.13 = (bf16[192,1024]{1,0:T(8,128)(2,1)S(1)}, bf16[192,1024]{1,0:T(8,128)(2,1)S(1)}, u32[]{:S(2)}, u32[]{:S(2)}) collective-permute-start(bf16[192,1024]{1,0:T(8,128)(2,1)S(1)} %slice.294), channel_id=1, source_target_pairs={{8,0},{16,8},{24,16},{28,24},{20,28},{12,20},{4,12},{0,4},{9,1},{1... | collective-permute-start | bytes 1179656 | tf_op jit(solution)/shard_map/ppermute | solution.py:553
  75.4 14.3 %collective-permute-start.12 = (bf16[192,896]{1,0:T(8,128)(2,1)S(1)}, bf16[192,896]{1,0:T(8,128)(2,1)S(1)}, u32[]{:S(2)}, u32[]{:S(2)}) collective-permute-start(bf16[192,896]{1,0:T(8,128)(2,1)S(1)} %slice.293), channel_id=1, source_target_pairs={{0,8},{8,16},{16,24},{24,28},{28,20},{20,12},{12,4},{4,0},{1,9},{9... | collective-permute-start | bytes 1032200 | tf_op jit(solution)/shard_map/ppermute | solution.py:553
  76.2 13.6 %collective-permute-start.10 = (bf16[192,768]{1,0:T(8,128)(2,1)S(1)}, bf16[192,768]{1,0:T(8,128)(2,1)S(1)}, u32[]{:S(2)}, u32[]{:S(2)}) collective-permute-start(bf16[192,768]{1,0:T(8,128)(2,1)S(1)} %copy-done.18), channel_id=1, source_target_pairs={{0,8},{8,16},{16,24},{24,28},{28,20},{20,12},{12,4},{4,0},{1,9},{9... | collective-permute-start | bytes 884744 | tf_op jit(solution)/shard_map/ppermute | solution.py:553
  77.8 12.0 %collective-permute-start.11 = (bf16[192,768]{1,0:T(8,128)(2,1)S(1)}, bf16[192,768]{1,0:T(8,128)(2,1)S(1)}, u32[]{:S(2)}, u32[]{:S(2)}) collective-permute-start(bf16[192,768]{1,0:T(8,128)(2,1)S(1)} %copy-done.18), channel_id=1, source_target_pairs={{8,0},{16,8},{24,16},{28,24},{20,28},{12,20},{4,12},{0,4},{9,1},{1... | collective-permute-start | bytes 884744 | tf_op jit(solution)/shard_map/ppermute | solution.py:553
  78.2 50.5 %collective-permute-start.20 = (bf16[256,1536]{1,0:T(8,128)(2,1)S(1)}, bf16[256,1536]{1,0:T(8,128)(2,1)S(1)}, u32[]{:S(2)}, u32[]{:S(2)}) collective-permute-start(bf16[256,1536]{1,0:T(8,128)(2,1)S(1)} %multiply_convert_fusion.refs_9_), channel_id=1, source_target_pairs={{0,1},{1,0},{2,3},{3,2},{4,5},{5,4},{6,7},{7,6},{8,9},{9,8},{10,11... | collective-permute-start | bytes 2359304 | tf_op jit(solution)/shard_map/ppermute | solution.py:604
  89.8 39.0 %collective-permute-start.21 = (bf16[256,1536]{1,0:T(8,128)(2,1)S(1)}, bf16[256,1536]{1,0:T(8,128)(2,1)S(1)}, u32[]{:S(2)}, u32[]{:S(2)}) collective-permute-start(bf16[256,1536]{1,0:T(8,128)(2,1)S(1)} %collective-permute-done.9.refs_10_), channel_id=1, source_target_pairs={{0,1},{1,0},{2,3},{3,2},{4,5},{5,4},{6,7},{7,6},{8,9},{9,8},{10,11... | collective-permute-start | bytes 2359304 | tf_op jit(solution)/shard_map/ppermute | solution.py:604
  89.8 18.3 %collective-permute-start.14 = (bf16[192,768]{1,0:T(8,128)(2,1)S(1)}, bf16[192,768]{1,0:T(8,128)(2,1)S(1)}, u32[]{:S(2)}, u32[]{:S(2)}) collective-permute-start(bf16[192,768]{1,0:T(8,128)(2,1)S(1)} %collective-permute-done.10.refs_1_), channel_id=1, source_target_pairs={{0,8},{8,16},{16,24},{24,28},{28,20},{20,12},{12,4},{4,0},{1,9},{9... | collective-permute-start | bytes 884744 | tf_op jit(solution)/shard_map/ppermute | solution.py:553
  90.5 17.6 %collective-permute-start.15 = (bf16[192,768]{1,0:T(8,128)(2,1)S(1)}, bf16[192,768]{1,0:T(8,128)(2,1)S(1)}, u32[]{:S(2)}, u32[]{:S(2)}) collective-permute-start(bf16[192,768]{1,0:T(8,128)(2,1)S(1)} %collective-permute-done.11.refs_2_), channel_id=1, source_target_pairs={{8,0},{16,8},{24,16},{28,24},{20,28},{12,20},{4,12},{0,4},{9,1},{1... | collective-permute-start | bytes 884744 | tf_op jit(solution)/shard_map/ppermute | solution.py:553
  108.1 39.7 %copy-start.12 = (bf16[1536,1024]{1,0:T(8,128)(2,1)}, bf16[1536,1024]{1,0:T(8,128)(2,1)S(1)}, u32[]{:S(2)}) copy-start(bf16[1536,1024]{1,0:T(8,128)(2,1)S(1)} %get-tuple-element.200.xt_ref) | copy-start | bytes 9437188
  108.1 8.9 %collective-permute-start.16 = (bf16[192,768]{1,0:T(8,128)(2,1)S(1)}, bf16[192,768]{1,0:T(8,128)(2,1)S(1)}, u32[]{:S(2)}, u32[]{:S(2)}) collective-permute-start(bf16[192,768]{1,0:T(8,128)(2,1)S(1)} %collective-permute-done.14.refs_3_), channel_id=1, source_target_pairs={{0,8},{8,16},{16,24},{24,28},{28,20},{20,12},{12,4},{4,0},{1,9},{9... | collective-permute-start | bytes 884744 | tf_op jit(solution)/shard_map/ppermute | solution.py:553
  108.8 8.3 %collective-permute-start.17 = (bf16[192,768]{1,0:T(8,128)(2,1)S(1)}, bf16[192,768]{1,0:T(8,128)(2,1)S(1)}, u32[]{:S(2)}, u32[]{:S(2)}) collective-permute-start(bf16[192,768]{1,0:T(8,128)(2,1)S(1)} %collective-permute-done.15.refs_4_), channel_id=1, source_target_pairs={{8,0},{16,8},{24,16},{28,24},{20,28},{12,20},{4,12},{0,4},{9,1},{1... | collective-permute-start | bytes 884744 | tf_op jit(solution)/shard_map/ppermute | solution.py:553
  117.2 11.6 %collective-permute-start.18 = (bf16[192,384]{1,0:T(8,128)(2,1)S(1)}, bf16[192,384]{1,0:T(8,128)(2,1)S(1)}, u32[]{:S(2)}, u32[]{:S(2)}) collective-permute-start(bf16[192,384]{1,0:T(8,128)(2,1)S(1)} %slice.295), channel_id=1, source_target_pairs={{0,8},{8,16},{16,24},{24,28},{28,20},{20,12},{12,4},{4,0},{1,9},{9... | collective-permute-start | bytes 442376 | tf_op jit(solution)/shard_map/ppermute | solution.py:553
  118.3 10.5 %collective-permute-start.19 = (bf16[192,384]{1,0:T(8,128)(2,1)S(1)}, bf16[192,384]{1,0:T(8,128)(2,1)S(1)}, u32[]{:S(2)}, u32[]{:S(2)}) collective-permute-start(bf16[192,384]{1,0:T(8,128)(2,1)S(1)} %slice.296), channel_id=1, source_target_pairs={{8,0},{16,8},{24,16},{28,24},{20,28},{12,20},{4,12},{0,4},{9,1},{1... | collective-permute-start | bytes 442376 | tf_op jit(solution)/shard_map/ppermute | solution.py:553
  136.6 5.7 %collective-permute-start.24 = (f32[4,8,256]{2,1,0:T(8,128)S(1)}, f32[4,8,256]{2,1,0:T(8,128)S(1)}, u32[]{:S(2)}, u32[]{:S(2)}) collective-permute-start(f32[4,8,256]{2,1,0:T(8,128)S(1)} %get-tuple-element.193), channel_id=1, source_target_pairs={{0,3},{1,2},{2,1},{3,0},{4,7},{5,6},{6,5},{7,4},{8,11},{9,10},{10,... | collective-permute-start | bytes 98312 | tf_op jit(solution)/shard_map/ppermute | solution.py:604
  136.6 5.7 %collective-permute-start.23 = (f32[4,8,256]{2,1,0:T(8,128)S(1)}, f32[4,8,256]{2,1,0:T(8,128)S(1)}, u32[]{:S(2)}, u32[]{:S(2)}) collective-permute-start(f32[4,8,256]{2,1,0:T(8,128)S(1)} %get-tuple-element.193), channel_id=1, source_target_pairs={{0,2},{1,3},{2,0},{3,1},{4,6},{5,7},{6,4},{7,5},{8,10},{9,11},{10,... | collective-permute-start | bytes 98312 | tf_op jit(solution)/shard_map/ppermute | solution.py:604
  137.5 4.8 %collective-permute-start.22 = (f32[4,8,256]{2,1,0:T(8,128)S(1)}, f32[4,8,256]{2,1,0:T(8,128)S(1)}, u32[]{:S(2)}, u32[]{:S(2)}) collective-permute-start(f32[4,8,256]{2,1,0:T(8,128)S(1)} %get-tuple-element.193), channel_id=1, source_target_pairs={{0,1},{1,0},{2,3},{3,2},{4,5},{5,4},{6,7},{7,6},{8,9},{9,8},{10,11... | collective-permute-start | bytes 98312 | tf_op jit(solution)/shard_map/ppermute | solution.py:604
  152.7 10.7 %collective-permute-start.25 = (bf16[2,256,1536]{2,1,0:T(8,128)(2,1)}, bf16[2,256,1536]{2,1,0:T(8,128)(2,1)}, u32[]{:S(2)}, u32[]{:S(2)}) collective-permute-start(bf16[2,256,1536]{2,1,0:T(8,128)(2,1)} %slice.231), channel_id=1, source_target_pairs={{0,1},{1,0},{2,3},{3,2},{4,5},{5,4},{6,7},{7,6},{8,9},{9,8},{10,11... | collective-permute-start | bytes 4718600 | tf_op jit(solution)/shard_map/ppermute | solution.py:604
  152.9 8.5 %collective-permute-start.26 = (bf16[192,384]{1,0:T(8,128)(2,1)}, bf16[192,384]{1,0:T(8,128)(2,1)S(1)}, u32[]{:S(2)}, u32[]{:S(2)}) collective-permute-start(bf16[192,384]{1,0:T(8,128)(2,1)} %get-tuple-element.206), channel_id=1, source_target_pairs={{0,8},{8,16},{16,24},{24,28},{28,20},{20,12},{12,4},{4,0},{1,9},{9... | collective-permute-start | bytes 442376 | tf_op jit(solution)/shard_map/ppermute | solution.py:553
  154.1 7.3 %collective-permute-start.27 = (bf16[192,384]{1,0:T(8,128)(2,1)}, bf16[192,384]{1,0:T(8,128)(2,1)}, u32[]{:S(2)}, u32[]{:S(2)}) collective-permute-start(bf16[192,384]{1,0:T(8,128)(2,1)} %get-tuple-element.207), channel_id=1, source_target_pairs={{8,0},{16,8},{24,16},{28,24},{20,28},{12,20},{4,12},{0,4},{9,1},{1... | collective-permute-start | bytes 442376 | tf_op jit(solution)/shard_map/ppermute | solution.py:553
  165.9 26.1 %collective-permute-start.28 = (bf16[192,768]{1,0:T(8,128)(2,1)}, bf16[192,768]{1,0:T(8,128)(2,1)}, u32[]{:S(2)}, u32[]{:S(2)}) collective-permute-start(bf16[192,768]{1,0:T(8,128)(2,1)} %get-tuple-element.211), channel_id=1, source_target_pairs={{0,8},{8,16},{16,24},{24,28},{28,20},{20,12},{12,4},{4,0},{1,9},{9... | collective-permute-start | bytes 884744 | tf_op jit(solution)/shard_map/ppermute | solution.py:553
  167.1 25.0 %collective-permute-start.29 = (bf16[192,768]{1,0:T(8,128)(2,1)}, bf16[192,768]{1,0:T(8,128)(2,1)}, u32[]{:S(2)}, u32[]{:S(2)}) collective-permute-start(bf16[192,768]{1,0:T(8,128)(2,1)} %get-tuple-element.212), channel_id=1, source_target_pairs={{8,0},{16,8},{24,16},{28,24},{20,28},{12,20},{4,12},{0,4},{9,1},{1... | collective-permute-start | bytes 884744 | tf_op jit(solution)/shard_map/ppermute | solution.py:553
  168.2 25.2 %collective-permute-start.30 = (bf16[128,1536]{1,0:T(8,128)(2,1)}, bf16[128,1536]{1,0:T(8,128)(2,1)S(1)}, u32[]{:S(2)}, u32[]{:S(2)}) collective-permute-start(bf16[128,1536]{1,0:T(8,128)(2,1)} %get-tuple-element.213), channel_id=1, source_target_pairs={{0,2},{1,3},{2,0},{3,1},{4,6},{5,7},{6,4},{7,5},{8,10},{9,11},{10,... | collective-permute-start | bytes 1179656 | tf_op jit(solution)/shard_map/ppermute | solution.py:604
  209.4 9.3 %collective-permute-start.31 = (bf16[192,768]{1,0:T(8,128)(2,1)S(1)}, bf16[192,768]{1,0:T(8,128)(2,1)S(1)}, u32[]{:S(2)}, u32[]{:S(2)}) collective-permute-start(bf16[192,768]{1,0:T(8,128)(2,1)S(1)} %get-tuple-element.214), channel_id=1, source_target_pairs={{0,8},{8,16},{16,24},{24,28},{28,20},{20,12},{12,4},{4,0},{1,9},{9... | collective-permute-start | bytes 884744 | tf_op jit(solution)/shard_map/ppermute | solution.py:553
  211.1 7.9 %collective-permute-start.32 = (bf16[192,768]{1,0:T(8,128)(2,1)S(1)}, bf16[192,768]{1,0:T(8,128)(2,1)S(1)}, u32[]{:S(2)}, u32[]{:S(2)}) collective-permute-start(bf16[192,768]{1,0:T(8,128)(2,1)S(1)} %get-tuple-element.215), channel_id=1, source_target_pairs={{8,0},{16,8},{24,16},{28,24},{20,28},{12,20},{4,12},{0,4},{9,1},{1... | collective-permute-start | bytes 884744 | tf_op jit(solution)/shard_map/ppermute | solution.py:553
  211.5 9.7 %collective-permute-start.33 = (bf16[128,1536]{1,0:T(8,128)(2,1)S(1)}, bf16[128,1536]{1,0:T(8,128)(2,1)S(1)}, u32[]{:S(2)}, u32[]{:S(2)}) collective-permute-start(bf16[128,1536]{1,0:T(8,128)(2,1)S(1)} %copy-done.34), channel_id=1, source_target_pairs={{0,2},{1,3},{2,0},{3,1},{4,6},{5,7},{6,4},{7,5},{8,10},{9,11},{10,... | collective-permute-start | bytes 1179656 | tf_op jit(solution)/shard_map/ppermute | solution.py:604
  221.2 12.1 %collective-permute-start.34 = (bf16[192,384]{1,0:T(8,128)(2,1)S(1)}, bf16[192,384]{1,0:T(8,128)(2,1)S(1)}, u32[]{:S(2)}, u32[]{:S(2)}) collective-permute-start(bf16[192,384]{1,0:T(8,128)(2,1)S(1)} %slice_bitcast_fusion.25), channel_id=1, source_target_pairs={{0,8},{8,16},{16,24},{24,28},{28,20},{20,12},{12,4},{4,0},{1,9},{9... | collective-permute-start | bytes 442376 | tf_op jit(solution)/shard_map/ppermute | solution.py:553
  222.8 12.9 %collective-permute-start.35 = (bf16[192,512]{1,0:T(8,128)(2,1)S(1)}, bf16[192,512]{1,0:T(8,128)(2,1)S(1)}, u32[]{:S(2)}, u32[]{:S(2)}) collective-permute-start(bf16[192,512]{1,0:T(8,128)(2,1)S(1)} %slice_bitcast_fusion.24), channel_id=1, source_target_pairs={{8,0},{16,8},{24,16},{28,24},{20,28},{12,20},{4,12},{0,4},{9,1},{1... | collective-permute-start | bytes 589832 | tf_op jit(solution)/shard_map/ppermute | solution.py:553
  223.3 16.4 %collective-permute-start.36 = (bf16[192,768]{1,0:T(8,128)(2,1)S(1)}, bf16[192,768]{1,0:T(8,128)(2,1)S(1)}, u32[]{:S(2)}, u32[]{:S(2)}) collective-permute-start(bf16[192,768]{1,0:T(8,128)(2,1)S(1)} %get-tuple-element.231), channel_id=1, source_target_pairs={{0,8},{8,16},{16,24},{24,28},{28,20},{20,12},{12,4},{4,0},{1,9},{9... | collective-permute-start | bytes 884744 | tf_op jit(solution)/shard_map/ppermute | solution.py:553
  224.8 18.1 %collective-permute-start.37 = (bf16[192,768]{1,0:T(8,128)(2,1)S(1)}, bf16[192,768]{1,0:T(8,128)(2,1)S(1)}, u32[]{:S(2)}, u32[]{:S(2)}) collective-permute-start(bf16[192,768]{1,0:T(8,128)(2,1)S(1)} %get-tuple-element.232), channel_id=1, source_target_pairs={{8,0},{16,8},{24,16},{28,24},{20,28},{12,20},{4,12},{0,4},{9,1},{1... | collective-permute-start | bytes 884744 | tf_op jit(solution)/shard_map/ppermute | solution.py:553
  242.9 20.7 %collective-permute-start.38 = (bf16[2,256,1536]{2,1,0:T(8,128)(2,1)}, bf16[2,256,1536]{2,1,0:T(8,128)(2,1)}, u32[]{:S(2)}, u32[]{:S(2)}) collective-permute-start(bf16[2,256,1536]{2,1,0:T(8,128)(2,1)} %get-tuple-element.241), channel_id=1, source_target_pairs={{0,1},{1,0},{2,3},{3,2},{4,5},{5,4},{6,7},{7,6},{8,9},{9,8},{10,11... | collective-permute-start | bytes 4718600 | tf_op jit(solution)/shard_map/ppermute | solution.py:604
  247.9 3.6 %collective-permute-start.41 = (bf16[1,8,48,256]{3,2,1,0:T(8,128)(2,1)}, bf16[1,8,48,256]{3,2,1,0:T(8,128)(2,1)S(1)}, u32[]{:S(2)}, u32[]{:S(2)}) collective-permute-start(bf16[1,8,48,256]{3,2,1,0:T(8,128)(2,1)} %get-tuple-element.244), channel_id=1, source_target_pairs={{0,1},{1,0},{2,3},{3,2},{4,5},{5,4},{6,7},{7,6},{8,9},{9,8},{10,11... | collective-permute-start | bytes 589832 | tf_op jit(solution)/shard_map/ppermute | solution.py:604
  248.0 7.8 %collective-permute-start.42 = (bf16[1,8,48,256]{3,2,1,0:T(8,128)(2,1)S(1)}, bf16[1,8,48,256]{3,2,1,0:T(8,128)(2,1)S(1)}, u32[]{:S(2)}, u32[]{:S(2)}) collective-permute-start(bf16[1,8,48,256]{3,2,1,0:T(8,128)(2,1)S(1)} %copy-done.38), channel_id=1, source_target_pairs={{0,2},{1,3},{2,0},{3,1},{4,6},{5,7},{6,4},{7,5},{8,10},{9,11},{10,... | collective-permute-start | bytes 589832 | tf_op jit(solution)/shard_map/ppermute | solution.py:604
  248.1 11.0 %collective-permute-start.43 = (bf16[1,8,48,256]{3,2,1,0:T(8,128)(2,1)S(1)}, bf16[1,8,48,256]{3,2,1,0:T(8,128)(2,1)S(1)}, u32[]{:S(2)}, u32[]{:S(2)}) collective-permute-start(bf16[1,8,48,256]{3,2,1,0:T(8,128)(2,1)S(1)} %get-tuple-element.246), channel_id=1, source_target_pairs={{0,3},{1,2},{2,1},{3,0},{4,7},{5,6},{6,5},{7,4},{8,11},{9,10},{10,... | collective-permute-start | bytes 589832 | tf_op jit(solution)/shard_map/ppermute | solution.py:604
  249.9 10.5 %collective-permute-start.39 = (bf16[192,896]{1,0:T(8,128)(2,1)}, bf16[192,896]{1,0:T(8,128)(2,1)S(1)}, u32[]{:S(2)}, u32[]{:S(2)}) collective-permute-start(bf16[192,896]{1,0:T(8,128)(2,1)} %get-tuple-element.242), channel_id=1, source_target_pairs={{0,8},{8,16},{16,24},{24,28},{28,20},{20,12},{12,4},{4,0},{1,9},{9... | collective-permute-start | bytes 1032200 | tf_op jit(solution)/shard_map/ppermute | solution.py:553
  251.5 10.0 %collective-permute-start.40 = (bf16[192,896]{1,0:T(8,128)(2,1)S(1)}, bf16[192,896]{1,0:T(8,128)(2,1)S(1)}, u32[]{:S(2)}, u32[]{:S(2)}) collective-permute-start(bf16[192,896]{1,0:T(8,128)(2,1)S(1)} %get-tuple-element.243), channel_id=1, source_target_pairs={{8,0},{16,8},{24,16},{28,24},{20,28},{12,20},{4,12},{0,4},{9,1},{1... | collective-permute-start | bytes 1032200 | tf_op jit(solution)/shard_map/ppermute | solution.py:553
  265.8 3.5 %collective-permute-start.50 = (f32[16,256]{1,0:T(8,128)S(1)}, f32[16,256]{1,0:T(8,128)S(1)}, u32[]{:S(2)}, u32[]{:S(2)}) collective-permute-start(f32[16,256]{1,0:T(8,128)S(1)} %maximum_maximum_fusion), channel_id=1, source_target_pairs={{0,3},{1,2},{2,1},{3,0},{4,7},{5,6},{6,5},{7,4},{8,11},{9,10},{10,... | collective-permute-start | bytes 49160 | tf_op jit(solution)/shard_map/ppermute | solution.py:604
  265.8 4.3 %collective-permute-start.49 = (f32[16,256]{1,0:T(8,128)S(1)}, f32[16,256]{1,0:T(8,128)S(1)}, u32[]{:S(2)}, u32[]{:S(2)}) collective-permute-start(f32[16,256]{1,0:T(8,128)S(1)} %maximum_maximum_fusion), channel_id=1, source_target_pairs={{0,2},{1,3},{2,0},{3,1},{4,6},{5,7},{6,4},{7,5},{8,10},{9,11},{10,... | collective-permute-start | bytes 49160 | tf_op jit(solution)/shard_map/ppermute | solution.py:604
  266.7 3.8 %collective-permute-start.48 = (f32[16,256]{1,0:T(8,128)S(1)}, f32[16,256]{1,0:T(8,128)S(1)}, u32[]{:S(2)}, u32[]{:S(2)}) collective-permute-start(f32[16,256]{1,0:T(8,128)S(1)} %maximum_maximum_fusion), channel_id=1, source_target_pairs={{0,1},{1,0},{2,3},{3,2},{4,5},{5,4},{6,7},{7,6},{8,9},{9,8},{10,11... | collective-permute-start | bytes 49160 | tf_op jit(solution)/shard_map/ppermute | solution.py:604
  267.7 5.7 %collective-permute-start.47 = (bf16[4,48,256]{2,1,0:T(8,128)(2,1)S(1)}, bf16[4,48,256]{2,1,0:T(8,128)(2,1)S(1)}, u32[]{:S(2)}, u32[]{:S(2)}) collective-permute-start(bf16[4,48,256]{2,1,0:T(8,128)(2,1)S(1)} %fusion.26), channel_id=1, source_target_pairs={{0,4},{4,0},{8,12},{12,8},{16,20},{20,16},{24,28},{28,24},{1,5},{5... | collective-permute-start | bytes 294920 | tf_op jit(solution)/shard_map/ppermute | solution.py:604
  268.1 11.7 %collective-permute-start.44 = (bf16[192,896]{1,0:T(8,128)(2,1)}, bf16[192,896]{1,0:T(8,128)(2,1)S(1)}, u32[]{:S(2)}, u32[]{:S(2)}) collective-permute-start(bf16[192,896]{1,0:T(8,128)(2,1)} %get-tuple-element.249), channel_id=1, source_target_pairs={{0,8},{8,16},{16,24},{24,28},{28,20},{20,12},{12,4},{4,0},{1,9},{9... | collective-permute-start | bytes 1032200 | tf_op jit(solution)/shard_map/ppermute | solution.py:553
  269.3 10.5 %collective-permute-start.45 = (bf16[192,896]{1,0:T(8,128)(2,1)S(1)}, bf16[192,896]{1,0:T(8,128)(2,1)S(1)}, u32[]{:S(2)}, u32[]{:S(2)}) collective-permute-start(bf16[192,896]{1,0:T(8,128)(2,1)S(1)} %get-tuple-element.250), channel_id=1, source_target_pairs={{8,0},{16,8},{24,16},{28,24},{20,28},{12,20},{4,12},{0,4},{9,1},{1... | collective-permute-start | bytes 1032200 | tf_op jit(solution)/shard_map/ppermute | solution.py:553
  270.1 11.8 %collective-permute-start.46 = (bf16[128,1536]{1,0:T(8,128)(2,1)}, bf16[128,1536]{1,0:T(8,128)(2,1)}, u32[]{:S(2)}, u32[]{:S(2)}) collective-permute-start(bf16[128,1536]{1,0:T(8,128)(2,1)} %get-tuple-element.251), channel_id=1, source_target_pairs={{0,2},{1,3},{2,0},{3,1},{4,6},{5,7},{6,4},{7,5},{8,10},{9,11},{10,... | collective-permute-start | bytes 1179656 | tf_op jit(solution)/shard_map/ppermute | solution.py:604
  281.9 6.4 %collective-permute-start.54 = (bf16[1,48,256]{2,1,0:T(8,128)(2,1)S(1)}, bf16[1,48,256]{2,1,0:T(8,128)(2,1)S(1)}, u32[]{:S(2)}, u32[]{:S(2)}) collective-permute-start(bf16[1,48,256]{2,1,0:T(8,128)(2,1)S(1)} %get-tuple-element.261), channel_id=1, source_target_pairs={{0,8},{4,12},{8,0},{12,4},{16,24},{20,28},{24,16},{28,20},{1,9},{5... | collective-permute-start | bytes 73736 | tf_op jit(solution)/shard_map/ppermute | solution.py:604
  282.2 8.9 %collective-permute-start.55 = (bf16[1,48,256]{2,1,0:T(8,128)(2,1)S(1)}, bf16[1,48,256]{2,1,0:T(8,128)(2,1)S(1)}, u32[]{:S(2)}, u32[]{:S(2)}) collective-permute-start(bf16[1,48,256]{2,1,0:T(8,128)(2,1)S(1)} %get-tuple-element.262), channel_id=1, source_target_pairs={{0,16},{4,20},{8,24},{12,28},{16,0},{20,4},{24,8},{28,12},{1,17},{... | collective-permute-start | bytes 73736 | tf_op jit(solution)/shard_map/ppermute | solution.py:604
  284.7 6.8 %collective-permute-start.56 = (bf16[1,48,256]{2,1,0:T(8,128)(2,1)S(1)}, bf16[1,48,256]{2,1,0:T(8,128)(2,1)S(1)}, u32[]{:S(2)}, u32[]{:S(2)}) collective-permute-start(bf16[1,48,256]{2,1,0:T(8,128)(2,1)S(1)} %get-tuple-element.263), channel_id=1, source_target_pairs={{0,24},{4,28},{8,16},{12,20},{16,8},{20,12},{24,0},{28,4},{1,25},{... | collective-permute-start | bytes 73736 | tf_op jit(solution)/shard_map/ppermute | solution.py:604
  286.3 12.5 %collective-permute-start.51 = (bf16[192,896]{1,0:T(8,128)(2,1)}, bf16[192,896]{1,0:T(8,128)(2,1)}, u32[]{:S(2)}, u32[]{:S(2)}) collective-permute-start(bf16[192,896]{1,0:T(8,128)(2,1)} %get-tuple-element.257), channel_id=1, source_target_pairs={{0,8},{8,16},{16,24},{24,28},{28,20},{20,12},{12,4},{4,0},{1,9},{9... | collective-permute-start | bytes 1032200 | tf_op jit(solution)/shard_map/ppermute | solution.py:553
  286.3 12.5 %collective-permute-start.52 = (bf16[192,896]{1,0:T(8,128)(2,1)}, bf16[192,896]{1,0:T(8,128)(2,1)}, u32[]{:S(2)}, u32[]{:S(2)}) collective-permute-start(bf16[192,896]{1,0:T(8,128)(2,1)} %get-tuple-element.258), channel_id=1, source_target_pairs={{8,0},{16,8},{24,16},{28,24},{20,28},{12,20},{4,12},{0,4},{9,1},{1... | collective-permute-start | bytes 1032200 | tf_op jit(solution)/shard_map/ppermute | solution.py:553
  288.4 10.5 %collective-permute-start.53 = (bf16[128,1536]{1,0:T(8,128)(2,1)}, bf16[128,1536]{1,0:T(8,128)(2,1)S(1)}, u32[]{:S(2)}, u32[]{:S(2)}) collective-permute-start(bf16[128,1536]{1,0:T(8,128)(2,1)} %get-tuple-element.260), channel_id=1, source_target_pairs={{0,2},{1,3},{2,0},{3,1},{4,6},{5,7},{6,4},{7,5},{8,10},{9,11},{10,... | collective-permute-start | bytes 1179656 | tf_op jit(solution)/shard_map/ppermute | solution.py:604
  291.1 5.3 %collective-permute-start.57 = (f32[12,1024]{1,0:T(8,128)S(1)}, f32[12,1024]{1,0:T(8,128)S(1)}, u32[]{:S(2)}, u32[]{:S(2)}) collective-permute-start(f32[12,1024]{1,0:T(8,128)S(1)} %pad_maximum_fusion.2), channel_id=1, source_target_pairs={{0,4},{4,0},{8,12},{12,8},{16,20},{20,16},{24,28},{28,24},{1,5},{5... | collective-permute-start | bytes 147464 | tf_op jit(solution)/shard_map/ppermute | solution.py:604
  298.9 15.1 %collective-permute-start.60 = (f32[12,1024]{1,0:T(8,128)}, f32[12,1024]{1,0:T(8,128)}, u32[]{:S(2)}, u32[]{:S(2)}) collective-permute-start(f32[12,1024]{1,0:T(8,128)} %add.273), channel_id=1, source_target_pairs={{0,24},{4,28},{8,16},{12,20},{16,8},{20,12},{24,0},{28,4},{1,25},{... | collective-permute-start | bytes 147464 | tf_op jit(solution)/shard_map/ppermute | solution.py:604
  301.6 12.5 %collective-permute-start.59 = (f32[12,1024]{1,0:T(8,128)}, f32[12,1024]{1,0:T(8,128)}, u32[]{:S(2)}, u32[]{:S(2)}) collective-permute-start(f32[12,1024]{1,0:T(8,128)} %add.273), channel_id=1, source_target_pairs={{0,16},{4,20},{8,24},{12,28},{16,0},{20,4},{24,8},{28,12},{1,17},{... | collective-permute-start | bytes 147464 | tf_op jit(solution)/shard_map/ppermute | solution.py:604
  301.6 12.5 %collective-permute-start.58 = (f32[12,1024]{1,0:T(8,128)}, f32[12,1024]{1,0:T(8,128)}, u32[]{:S(2)}, u32[]{:S(2)}) collective-permute-start(f32[12,1024]{1,0:T(8,128)} %add.273), channel_id=1, source_target_pairs={{0,8},{4,12},{8,0},{12,4},{16,24},{20,28},{24,16},{28,20},{1,9},{5... | collective-permute-start | bytes 147464 | tf_op jit(solution)/shard_map/ppermute | solution.py:604
  (55 other events, 352.3 us)
Sparse Core Ops, SparseCore 0:
  168.3 75.1 reduce-scatter.1
